TPU v7x, 32 devices: a whole 2x2x4 slice. The times are simulated.
32 devices in a mesh: op: 8 (over y, x, core), sec: 4 (over z).
Axes of the slice: x: 2, y: 2, z: 4, core: 2. Of those that a mesh axis runs over, the one named last changes fastest.
Arguments:
- wavefunction: bfloat16 [16, 256, 256], P('sec'), may hold values from -6 to 6
- left_operators: bfloat16 [32, 16, 256, 256], P('op', 'sec'), may hold values from -0.375 to 0.375
- right_operators: bfloat16 [32, 16, 256, 256], P('op', 'sec'), may hold values from -0.375 to 0.375
- rotations: bfloat16 [16, 256, 256], P('sec'), may hold values from -0.375 to 0.375
- charges: int32 [32], P('op'), may hold values from -1 to 1
- present_blocks: int32 [32, 16], P('op', 'sec'), may hold values 0 or 1
- directions: int32 [32, 1], P('op'), may hold values from 0 to 3, as said below
Outputs:
- sigma_vector: float32 [16, 256, 256], P('sec', 'op')
- regrouped: bfloat16 [64, 16, 256, 256], P('op', 'sec')
Inputs may be any that keep to these rules, and one draw needn't show every extreme that they name: `directions`: among the pairs of one index of op, each direction is named by at most 2 pairs, some direction is named by exactly 2, and every direction other than 0 is named at least once.
All inputs are finite; a program needn't handle non-finite values. No bound on the sum of `present_blocks` on one device may be relied on, other than what follows from the above.
Results may differ from a plain program's by a relative error of at most 0.0049.
Values may be sent and summed in bfloat16 or wider, within the bound.
No kernel may reach another device: no remote copies, remote signals or barrier semaphores. Data moves between devices by JAX's collectives and lax.ppermute only.
A program may use at most 64 MiB of HBM per device.

v0:
```python
import math

import jax
import jax.numpy as jnp
from jax import lax
from jax.sharding import PartitionSpec as P

DIRS = 4
CAPS = 2


def passed_along(value, axis, steps):
    count = lax.axis_size(axis)
    leading, last = (max(0, -steps), min(count, count - steps))
    return lax.ppermute(value, axis, [(source, source + steps) for source in range(leading, last)])


def padded(cells, sides, width):
    for axis, dim in sides:
        count = lax.axis_size(axis)
        ends = count - 1
        head = lax.slice_in_dim(cells, 0, width, axis=dim)
        tail = lax.slice_in_dim(cells, cells.shape[dim] - width, cells.shape[dim], axis=dim)
        cells = jnp.concatenate(
            [
                lax.ppermute(tail, axis, [(i, (i + 1) % count) for i in range(ends)]),
                cells,
                lax.ppermute(head, axis, [((i + 1) % count, i) for i in range(ends)]),
            ],
            axis=dim,
        )
    return cells


def shifted(value, axis, by):
    devices = lax.axis_size(axis)
    return lax.ppermute(value, axis, [(i, (i + by) % devices) for i in range(devices)])


def body(
    wavefunction, left_operators, right_operators, rotations, charges, present_blocks, directions
):
    local_sectors = wavefunction.shape[0]
    local_pairs = left_operators.shape[0]
    width = wavefunction.shape[1]
    weights = present_blocks.astype(jnp.float32)
    halfway = jnp.einsum(
        "psij,sjk->psik", left_operators, wavefunction, preferred_element_type=jnp.float32
    ).astype(jnp.bfloat16)
    charge_values = jnp.arange(3, dtype=jnp.int32) - 1
    selector = (charges[None, :] == charge_values[:, None]).astype(jnp.bfloat16)[
        :, :, None
    ] * present_blocks.astype(jnp.bfloat16)[None, :, :]
    masked = selector[:, :, :, None, None] * halfway[None]
    partials = jnp.einsum(
        "cpsik,psmk->csim", masked, right_operators, preferred_element_type=jnp.float32
    )
    padding = jnp.zeros((1, width, width), jnp.float32)
    extended = (
        jnp.concatenate([partials[0], padding, padding], axis=0)
        + jnp.concatenate([padding, partials[1], padding], axis=0)
        + jnp.concatenate([padding, padding, partials[2]], axis=0)
    )
    from_below = passed_along(extended[local_sectors + 1].astype(jnp.bfloat16), "sec", 1).astype(
        jnp.float32
    )
    from_above = passed_along(extended[0].astype(jnp.bfloat16), "sec", -1).astype(jnp.float32)
    interior = extended[1 : local_sectors + 1]
    interior = interior.at[0].add(from_below).at[local_sectors - 1].add(from_above)
    summed = lax.psum_scatter(interior, "op", scatter_dimension=1, tiled=True)
    pair_total = local_pairs * lax.axis_size("op")
    sigma_vector = summed / math.sqrt(pair_total)
    rot_padded = padded(rotations, (("sec", 0),), 1)
    rotated = jnp.einsum(
        "psij,sjk->psik", left_operators, rotations, preferred_element_type=jnp.float32
    ).astype(jnp.bfloat16)
    indices = jnp.arange(local_sectors, dtype=jnp.int32)[None, :] + 1 + charges[:, None]
    target = rot_padded[indices]
    renormed = (
        jnp.einsum("psji,psjk->psik", target, rotated, preferred_element_type=jnp.float32)
        * weights[:, :, None, None]
    ).astype(jnp.bfloat16)
    kinds = directions[:, 0]
    matching = kinds[:, None] == kinds[None, :]
    earlier = jnp.arange(local_pairs)[None, :] < jnp.arange(local_pairs)[:, None]
    position = jnp.sum(jnp.logical_and(matching, earlier), axis=1)
    chooser = jnp.logical_and(
        kinds[None, None, :] == jnp.arange(DIRS)[:, None, None],
        position[None, None, :] == jnp.arange(CAPS)[None, :, None],
    ).astype(jnp.bfloat16)
    payload = jnp.einsum(
        "dcp,psik->dcsik", chooser, renormed, preferred_element_type=jnp.float32
    ).astype(jnp.bfloat16)
    half_axis = lax.axis_size("op") // 2
    moved_one = shifted(payload[1], "op", 1)
    moved_two = shifted(payload[2], "op", -1)
    moved_three = shifted(payload[3], "op", half_axis)
    regrouped = jnp.stack([payload[0], moved_one, moved_two, moved_three], axis=0)
    regrouped = regrouped.reshape(DIRS * CAPS, local_sectors, width, width)
    return (sigma_vector, regrouped)


def solution(mesh):
    placed = (
        P("sec", None, None),
        P("op", "sec", None, None),
        P("op", "sec", None, None),
        P("sec", None, None),
        P("op"),
        P("op", "sec"),
        P("op", None),
    )
    return jax.shard_map(
        body,
        mesh=mesh,
        in_specs=placed,
        out_specs=(P("sec", "op", None), P("op", "sec", None, None)),
        check_vma=False,
    )
```

profile of v0, /device:TPU:1, one launch (start us, length us, event | category | flops | bytes accessed | tf_op | source)
XLA Modules:
  0.0 125.4 jit_solution(14503395027260705039)
XLA Ops:
  8.4 4.0 %collective-permute-start.2 = (bf16[1,256,256]{2,1,0:T(8,128)(2,1)S(1)}, bf16[1,256,256]{2,1,0:T(8,128)(2,1)S(1)}, u32[]{:S(2)}, u32[]{:S(2)}) collective-permute-start(bf16[1,256,256]{2,1,0:T(8,128)(2,1)S(1)} %get-tuple-element.37), channel_id=1, source_target_pairs={{0,1},{1,2},{2,3},{4,5},{5,6},{6,7},{8,9},{9,10},{10,11},{12,13},{... | collective-permute-start | bytes 393224 | tf_op jit(solution)/shard_map/ppermute | solution.py:26
  12.4 1.3 %collective-permute-start.3 = (bf16[1,256,256]{2,1,0:T(8,128)(2,1)S(1)}, bf16[1,256,256]{2,1,0:T(8,128)(2,1)}, u32[]{:S(2)}, u32[]{:S(2)}) collective-permute-start(bf16[1,256,256]{2,1,0:T(8,128)(2,1)S(1)} %get-tuple-element.38), channel_id=1, source_target_pairs={{1,0},{2,1},{3,2},{5,4},{6,5},{7,6},{9,8},{10,9},{11,10},{13,12},{... | collective-permute-start | bytes 393224 | tf_op jit(solution)/shard_map/ppermute | solution.py:28
  14.6 3.1 %convert_bitcast_fusion.1 = bf16[4,4,256,256]{2,3,0,1:T(8,128)(2,1)} fusion(bf16[4,4,256,256]{3,2,1,0:T(8,128)(2,1)S(1)} %copy-done, bf16[4,256,256]{2,1,0:T(8,128)(2,1)} %param.11), kind=kOutput, calls=%fused_computation.13 | convolution fusion | flops 537919488 | bytes 4718592 | tf_op jit(solution)/shard_map/psij,sjk->psik/dot_general | solution.py:47
  17.7 4.2 %copy.52 = bf16[4,4,256,256]{3,2,0,1:T(8,128)(2,1)} copy(bf16[4,4,256,256]{2,3,0,1:T(8,128)(2,1)} %convert_bitcast_fusion.1) | data formatting | bytes 4194304 | tf_op jit(solution)/shard_map/convert_element_type | solution.py:49
  22.0 4.1 %fusion.8 = f32[3,4,256,256]{3,2,0,1:T(8,128)S(1)} fusion(bf16[4,4,256,256]{3,2,0,1:T(8,128)(2,1)} %copy.52, bf16[3,4,4]{1,0,2:T(4,128)(2,1)S(1)} %broadcast_multiply_fusion.1, bf16[4,4,256,256]{3,2,1,0:T(8,128)(2,1)} %param.13), kind=kOutput, calls=%fused_computation.14 | convolution fusion | flops 1613758464 | bytes 7340128 | tf_op jit(solution)/shard_map/cpsik,psmk->csim/dot_general | solution.py:55
  26.3 1.5 %fusion.25 = (bf16[6,256,256]{2,1,0:T(8,128)(2,1)S(1)}, f32[6,256,256]{2,1,0:T(8,128)}) fusion(f32[4,256,256]{2,1,0:T(8,128)S(1)} %get-tuple-element.33, f32[1,256,256]{2,1,0:T(8,128)S(1)} %broadcast_in_dim.2, f32[4,256,256]{2,1,0:T(8,128)S(1)} %get-tuple-element.34, f32[4,256,256]{2,1,0:T(8,128)S(1)} %get-tuple-element.32), kind=kLoop, calls=%fused_computation.50 | loop fusion | flops 1966080 | bytes 5767168 | tf_op jit(solution)/shard_map/convert.3
  28.5 1.3 %collective-permute-start.1 = (bf16[256,256]{1,0:T(8,128)(2,1)}, bf16[256,256]{1,0:T(8,128)(2,1)S(1)}, u32[]{:S(2)}, u32[]{:S(2)}) collective-permute-start(bf16[256,256]{1,0:T(8,128)(2,1)} %get-tuple-element.35), channel_id=1, source_target_pairs={{1,0},{2,1},{3,2},{5,4},{6,5},{7,6},{9,8},{10,9},{11,10},{13,12},{... | collective-permute-start | bytes 393224 | tf_op jit(solution)/shard_map/ppermute | solution.py:15
  29.8 5.3 %collective-permute-start = (bf16[256,256]{1,0:T(8,128)(2,1)}, bf16[256,256]{1,0:T(8,128)(2,1)}, u32[]{:S(2)}, u32[]{:S(2)}) collective-permute-start(bf16[256,256]{1,0:T(8,128)(2,1)} %get-tuple-element.36), channel_id=1, source_target_pairs={{0,1},{1,2},{2,3},{4,5},{5,6},{6,7},{8,9},{9,10},{10,11},{12,13},{... | collective-permute-start | bytes 393224 | tf_op jit(solution)/shard_map/ppermute | solution.py:15
  35.3 2.1 %convert_bitcast_fusion = bf16[4,4,256,256]{2,3,0,1:T(8,128)(2,1)} fusion(bf16[4,4,256,256]{3,2,1,0:T(8,128)(2,1)S(1)} %copy-done, bf16[4,256,256]{2,1,0:T(8,128)(2,1)S(1)} %copy-done.4), kind=kOutput, calls=%fused_computation.12 | convolution fusion | flops 537919488 | bytes 4718592 | tf_op jit(solution)/shard_map/psij,sjk->psik/dot_general | solution.py:74
  37.5 2.3 %slice.102 = f32[4,256,256]{2,1,0:T(8,128)} slice(f32[6,256,256]{2,1,0:T(8,128)} %get-tuple-element.27), slice={[1:5], [0:256], [0:256]} | slice | bytes 2097152 | tf_op jit(solution)/shard_map/slice | solution.py:68
  41.6 2.0 %gather_fusion = bf16[16,256,256]{2,1,0:T(8,128)(2,1)} fusion(bf16[6,256,256]{2,1,0:T(8,128)(2,1)S(1)} %pad_maximum_fusion.1, s32[1024]{0:T(1024)S(1)} %pad_clamp_fusion), kind=kCustom, calls=%fused_computation | custom fusion | bytes 4194368 | tf_op jit(solution)/shard_map/gather | solution.py:78
  43.6 3.1 %multiply_convert_fusion = bf16[4,4,256,256]{3,2,1,0:T(8,128)(2,1)S(1)} fusion(bf16[4,4,256,256]{3,2,1,0:T(8,128)(2,1)} %bitcast.70, bf16[4,4,256,256]{2,3,0,1:T(8,128)(2,1)} %convert_bitcast_fusion, f32[4,4]{1,0:T(4,128)S(1)} %get-tuple-element.39), kind=kOutput, calls=%fused_computation.4 | convolution fusion | flops 538968064 | bytes 6291520 | tf_op jit(solution)/shard_map/psji,psjk->psik/dot_general | solution.py:80
  46.7 2.5 %convolution_convert_fusion = bf16[4,2,4,256,256]{4,0,3,2,1:T(4,128)(2,1)S(1)} fusion(bf16[4,4,256,256]{3,2,1,0:T(8,128)(2,1)S(1)} %multiply_convert_fusion, pred[2,4]{1,0:T(4,128)(4,1)S(1)} %iota_compare_fusion.2, pred[4,4]{1,0:T(4,128)(4,1)S(1)} %iota_compare_fusion.1), kind=kOutput, calls=%fused_computation.5 | convolution fusion | flops 18874400 | bytes 6291480 | tf_op jit(solution)/shard_map/dcp,psik->dcsik/dot_general | solution.py:91
  49.2 7.1 %fusion.27 = (bf16[1,2,4,256,256]{4,0,3,2,1:T(2,128)(2,1)}, bf16[1,2,4,256,256]{4,0,3,2,1:T(2,128)(2,1)S(1)}, bf16[1,2,4,256,256]{4,0,3,2,1:T(2,128)(2,1)S(1)}, bf16[1,2,4,256,256]{4,0,3,2,1:T(2,128)(2,1)S(1)}) fusion(bf16[4,2,4,256,256]{4,0,3,2,1:T(4,128)(2,1)S(1)} %convolution_convert_fusion), kind=kLoop, calls=%fused_computation.51 | loop fusion | bytes 8388608 | tf_op jit(solution)/shard_map/slice | solution.py:98
  59.8 2.6 %collective-permute-start.4 = (bf16[2,4,256,256]{3,2,1,0:T(8,128)(2,1)}, bf16[2,4,256,256]{3,2,1,0:T(8,128)(2,1)}, u32[]{:S(2)}, u32[]{:S(2)}) collective-permute-start(bf16[2,4,256,256]{3,2,1,0:T(8,128)(2,1)} %bitcast.68), channel_id=1, source_target_pairs={{0,4},{4,8},{8,12},{12,16},{16,20},{20,24},{24,28},{28,0},{1,5},{5... | collective-permute-start | bytes 3145736 | tf_op jit(solution)/shard_map/ppermute | solution.py:37
  62.4 1.2 collective-permute-start.6
  65.8 18.2 %collective-permute-done.4 = bf16[2,4,256,256]{3,2,1,0:T(8,128)(2,1)} collective-permute-done((bf16[2,4,256,256]{3,2,1,0:T(8,128)(2,1)}, bf16[2,4,256,256]{3,2,1,0:T(8,128)(2,1)}, u32[]{:S(2)}, u32[]{:S(2)}) %collective-permute-start.4) | collective-permute-done | bytes 1048608 | tf_op jit(solution)/shard_map/ppermute | solution.py:37
  83.9 3.0 %copy.61 = bf16[1,2,4,256,256]{4,0,3,2,1:T(2,128)(2,1)S(1)} copy(bf16[1,2,4,256,256]{4,3,2,1,0:T(8,128)(2,1)} %bitcast.21) | data formatting | bytes 2097152 | tf_op jit(solution)/shard_map/stack | solution.py:98
  87.7 3.0 %copy.62 = bf16[1,2,4,256,256]{4,0,3,2,1:T(2,128)(2,1)S(1)} copy(bf16[1,2,4,256,256]{4,3,2,1,0:T(8,128)(2,1)} %bitcast.22) | data formatting | bytes 2097152 | tf_op jit(solution)/shard_map/stack | solution.py:98
  90.7 10.8 %collective-permute-done.6 = bf16[2,4,256,256]{3,2,1,0:T(8,128)(2,1)} collective-permute-done((bf16[2,4,256,256]{3,2,1,0:T(8,128)(2,1)}, bf16[2,4,256,256]{3,2,1,0:T(8,128)(2,1)}, u32[]{:S(2)}, u32[]{:S(2)}) %collective-permute-start.6) | collective-permute-done | bytes 1048608 | tf_op jit(solution)/shard_map/ppermute | solution.py:37
  101.4 3.0 %copy.63 = bf16[1,2,4,256,256]{4,0,3,2,1:T(2,128)(2,1)S(1)} copy(bf16[1,2,4,256,256]{4,3,2,1,0:T(8,128)(2,1)} %bitcast.23) | data formatting | bytes 2097152 | tf_op jit(solution)/shard_map/stack | solution.py:98
  104.4 9.8 %pad_maximum_fusion = bf16[4,2,4,256,256]{4,0,3,2,1:T(4,128)(2,1)S(1)} fusion(bf16[1,2,4,256,256]{4,0,3,2,1:T(2,128)(2,1)S(1)} %copy.63, bf16[1,2,4,256,256]{4,0,3,2,1:T(2,128)(2,1)S(1)} %copy.62, bf16[1,2,4,256,256]{4,0,3,2,1:T(2,128)(2,1)S(1)} %copy.61, bf16[1,2,4,256,256]{4,0,3,2,1:T(2,128)(2,1)S(1)} %copy-done.1), kind=kLoop, calls=%fused_computation.3 | loop fusion | flops 16777216 | bytes 8388608 | tf_op jit(solution)/shard_map/stack | solution.py:98
  114.2 2.8 %copy.64 = bf16[4,2,4,256,256]{4,3,2,1,0:T(8,128)(2,1)} copy(bf16[4,2,4,256,256]{4,0,3,2,1:T(4,128)(2,1)S(1)} %pad_maximum_fusion) | data formatting | bytes 8388608 | tf_op jit(solution)/shard_map/stack | solution.py:98
  117.0 1.6 %broadcast_multiply_fusion = f32[4,32,256]{2,1,0:T(8,128)} fusion(f32[4,32,256]{2,1,0:T(8,128)} %reduce-scatter.2.cloned.1.call-done), kind=kLoop, calls=%fused_computation.34 | loop fusion | flops 32768 | bytes 262144 | tf_op jit(solution)/shard_map/div | solution.py:72
  (47 shorter events, 11.5 us)
Async XLA Ops:
  7.2 7.4 %copy-start = (bf16[4,4,256,256]{3,2,1,0:T(8,128)(2,1)S(1)}, bf16[4,4,256,256]{3,2,1,0:T(8,128)(2,1)}, u32[]{:S(2)}) copy-start(bf16[4,4,256,256]{3,2,1,0:T(8,128)(2,1)} %param.12) | copy-start | bytes 6291460
  7.2 109.8 %reduce-scatter.2.cloned.1.call-start = ((), (), s32[]{:S(2)}) async-start(), calls=%async_computation.1 | async-start | bytes 1179648 | tf_op jit(solution)/shard_map/reduce_scatter | solution.py:70
  8.4 31.5 %collective-permute-start.2 = (bf16[1,256,256]{2,1,0:T(8,128)(2,1)S(1)}, bf16[1,256,256]{2,1,0:T(8,128)(2,1)S(1)}, u32[]{:S(2)}, u32[]{:S(2)}) collective-permute-start(bf16[1,256,256]{2,1,0:T(8,128)(2,1)S(1)} %get-tuple-element.37), channel_id=1, source_target_pairs={{0,1},{1,2},{2,3},{4,5},{5,6},{6,7},{8,9},{9,10},{10,11},{12,13},{... | collective-permute-start | bytes 393224 | tf_op jit(solution)/shard_map/ppermute | solution.py:26
  12.4 28.1 %collective-permute-start.3 = (bf16[1,256,256]{2,1,0:T(8,128)(2,1)S(1)}, bf16[1,256,256]{2,1,0:T(8,128)(2,1)}, u32[]{:S(2)}, u32[]{:S(2)}) collective-permute-start(bf16[1,256,256]{2,1,0:T(8,128)(2,1)S(1)} %get-tuple-element.38), channel_id=1, source_target_pairs={{1,0},{2,1},{3,2},{5,4},{6,5},{7,6},{9,8},{10,9},{11,10},{13,12},{... | collective-permute-start | bytes 393224 | tf_op jit(solution)/shard_map/ppermute | solution.py:28
  17.7 4.2 %copy-start.6 = (s32[4]{0:T(128)S(1)}, s32[4]{0:T(128)}, u32[]{:S(2)}) copy-start(s32[4]{0:T(128)} %param.15) | copy-start | bytes 52
  26.3 8.8 %copy-start.7 = (s32[4,1]{0,1:T(1,128)S(1)}, s32[4,1]{0,1:T(1,128)}, u32[]{:S(2)}) copy-start(s32[4,1]{0,1:T(1,128)} %param.17) | copy-start | bytes 52
  26.3 9.0 %copy-start.4 = (bf16[4,256,256]{2,1,0:T(8,128)(2,1)S(1)}, bf16[4,256,256]{2,1,0:T(8,128)(2,1)}, u32[]{:S(2)}) copy-start(bf16[4,256,256]{2,1,0:T(8,128)(2,1)} %param.14) | copy-start | bytes 1572868
  28.5 36.2 %collective-permute-start.1 = (bf16[256,256]{1,0:T(8,128)(2,1)}, bf16[256,256]{1,0:T(8,128)(2,1)S(1)}, u32[]{:S(2)}, u32[]{:S(2)}) collective-permute-start(bf16[256,256]{1,0:T(8,128)(2,1)} %get-tuple-element.35), channel_id=1, source_target_pairs={{1,0},{2,1},{3,2},{5,4},{6,5},{7,6},{9,8},{10,9},{11,10},{13,12},{... | collective-permute-start | bytes 393224 | tf_op jit(solution)/shard_map/ppermute | solution.py:15
  29.8 33.9 %collective-permute-start = (bf16[256,256]{1,0:T(8,128)(2,1)}, bf16[256,256]{1,0:T(8,128)(2,1)}, u32[]{:S(2)}, u32[]{:S(2)}) collective-permute-start(bf16[256,256]{1,0:T(8,128)(2,1)} %get-tuple-element.36), channel_id=1, source_target_pairs={{0,1},{1,2},{2,3},{4,5},{5,6},{6,7},{8,9},{9,10},{10,11},{12,13},{... | collective-permute-start | bytes 393224 | tf_op jit(solution)/shard_map/ppermute | solution.py:15
  39.8 0.7 copy-start.5
  58.6 5.0 %copy-start.2 = (f32[4,256,256]{2,1,0:T(8,128)S(1)}, f32[4,256,256]{2,1,0:T(8,128)}, u32[]{:S(2)}) copy-start(f32[4,256,256]{2,1,0:T(8,128)} %slice.102) | copy-start | bytes 3145732
  59.8 24.1 %collective-permute-start.4 = (bf16[2,4,256,256]{3,2,1,0:T(8,128)(2,1)}, bf16[2,4,256,256]{3,2,1,0:T(8,128)(2,1)}, u32[]{:S(2)}, u32[]{:S(2)}) collective-permute-start(bf16[2,4,256,256]{3,2,1,0:T(8,128)(2,1)} %bitcast.68), channel_id=1, source_target_pairs={{0,4},{4,8},{8,12},{12,16},{16,20},{20,24},{24,28},{28,0},{1,5},{5... | collective-permute-start | bytes 3145736 | tf_op jit(solution)/shard_map/ppermute | solution.py:37
  62.4 25.2 %collective-permute-start.5 = (bf16[2,4,256,256]{3,2,1,0:T(8,128)(2,1)}, bf16[2,4,256,256]{3,2,1,0:T(8,128)(2,1)}, u32[]{:S(2)}, u32[]{:S(2)}) collective-permute-start(bf16[2,4,256,256]{3,2,1,0:T(8,128)(2,1)} %bitcast.67), channel_id=1, source_target_pairs={{0,28},{4,0},{8,4},{12,8},{16,12},{20,16},{24,20},{28,24},{1,29},{... | collective-permute-start | bytes 3145736 | tf_op jit(solution)/shard_map/ppermute | solution.py:37
  62.4 39.0 %collective-permute-start.6 = (bf16[2,4,256,256]{3,2,1,0:T(8,128)(2,1)}, bf16[2,4,256,256]{3,2,1,0:T(8,128)(2,1)}, u32[]{:S(2)}, u32[]{:S(2)}) collective-permute-start(bf16[2,4,256,256]{3,2,1,0:T(8,128)(2,1)} %bitcast.66), channel_id=1, source_target_pairs={{0,16},{4,20},{8,24},{12,28},{16,0},{20,4},{24,8},{28,12},{1,17},{... | collective-permute-start | bytes 3145736 | tf_op jit(solution)/shard_map/ppermute | solution.py:37
  64.8 1.0 copy-start.3
  90.6 13.8 %copy-start.1 = (bf16[1,2,4,256,256]{4,0,3,2,1:T(2,128)(2,1)S(1)}, bf16[1,2,4,256,256]{4,0,3,2,1:T(2,128)(2,1)}, u32[]{:S(2)}) copy-start(bf16[1,2,4,256,256]{4,0,3,2,1:T(2,128)(2,1)} %get-tuple-element.28) | copy-start | bytes 3145732
Sparse Core Ops, SparseCore 0:
  65.9 38.1 reduce-scatter.1
where the time goes:
time: 127 us; the launch traced here: 125 us
  local copies, waits for them, and re-layouts  34.7 us (27%)
  waiting for transfers between devices  29.7 us (23%)
  other arithmetic  16.1 us (13%)
  starting transfers between devices  15.8 us (12%)
  matrix products  14.9 us (12%)
  between operations  14.2 us (11%)
    ppermute x3, waiting for transfers between devices, shifted(): lax.ppermute(value, axis, [(i, (i + by) % devices) for i in range(devices)])  29.7 us
    another operation x4, local copies, waits for them, and re-layouts, body(): jnp.stack([payload[0], moved_one, moved_two, moved_three], axis=0)  11.7 us
    another operation x1, other arithmetic, body(): jnp.stack([payload[0], moved_one, moved_two, moved_three], axis=0)  9.81 us
    slice x1, local copies, waits for them, and re-layouts, body(): payload[0]  7.09 us
    ppermute x2, starting transfers between devices, passed_along(): lax.ppermute(value, axis, [(source, source + steps) for source in range(l...  6.56 us
    unnamed x19, local copies, waits for them, and re-layouts  5.19 us
    convert_element_type x1, local copies, waits for them, and re-layouts, body(): halfway = jnp.einsum('psij,sjk->psik', left_operators, wavefunction, pref...  4.17 us
    dot_general x1, matrix products, body(): jnp.einsum('cpsik,psmk->csim', masked, right_operators, preferred_element...  4.06 us
  transfers between devices with their start and end apart: 8, of which 3 were waited for; matrix products, arithmetic and copies ran while one was open for 49% of the time, Pallas kernels for 0%

commit v1 on v0

v1 whole, which is shorter than its diff:
```python
import functools
import math

import jax
import jax.numpy as jnp
from jax import lax
from jax.experimental import pallas as pl
from jax.experimental.pallas import tpu as pltpu
from jax.sharding import PartitionSpec as P

DIRS = 4
CAPS = 2
META = 16
VMEM_LIMIT = 28 * 1024 * 1024

BF16 = jnp.bfloat16
F32 = jnp.float32
ANY = pl.BlockSpec(memory_space=pl.ANY)
SMEM = pl.BlockSpec(memory_space=pltpu.SMEM)
VMEM = pl.BlockSpec(memory_space=pltpu.VMEM)


def params():
    return pltpu.CompilerParams(vmem_limit_bytes=VMEM_LIMIT)


def cost(flops, moved):
    return pl.CostEstimate(flops=flops, bytes_accessed=moved, transcendentals=0)


def ranks(directions_ref, count):
    kinds = [directions_ref[p, 0] for p in range(count)]
    places = []
    for p in range(count):
        place = jnp.int32(0)
        for q in range(p):
            place = place + jnp.where(kinds[q] == kinds[p], 1, 0)
        places.append(place)
    return kinds, places


def pick(kinds, places, kind, place):
    index = jnp.int32(0)
    for p, (own, at) in enumerate(zip(kinds, places)):
        match = at == place if kind is None else jnp.logical_and(at == place, own == kind)
        index = index + jnp.where(match, p, 0)
    return index


def gather_kernel(roles, directions_ref, charges_ref, present_ref, left_ref, *refs):
    outs, (meta, sem) = refs[: len(roles)], refs[len(roles) :]
    count, sectors, width, _ = left_ref.shape
    kinds, places = ranks(directions_ref, count)
    odd = lax.rem(lax.axis_index("op"), 2)
    copies = []
    slot = 0
    chosen = []
    for out, wanted in zip(outs, roles):
        base = 0
        for role in wanted:
            if role == "extra":
                index = pick(kinds, places, None, 1)
            elif role == "half":
                index = pick(kinds, places, 3, 0)
            elif role == "core":
                index = pick(kinds, places, 1 + odd, 0)
            else:
                index = pick(kinds, places, 2 - odd, 0)
            for s in range(sectors):
                copy = pltpu.make_async_copy(
                    left_ref.at[index, s], out.at[pl.ds(base + s * width, width)], sem
                )
                copy.start()
                copies.append(copy)
            chosen.append((index, out, base + sectors * width, slot))
            slot += 1
            base += sectors * width + META
    for index, out, base, slot in chosen:
        row = lax.broadcasted_iota(jnp.int32, (META, width), 0)
        kind = jnp.int32(0)
        for p in range(count):
            kind = kind + jnp.where(index == p, kinds[p], 0)
        values = jnp.where(row == 0, charges_ref[index], jnp.where(row == 1, kind, 0))
        for s in range(sectors):
            values = jnp.where(row == 2 + s, present_ref[index, s], values)
        meta[slot] = values.astype(F32).astype(BF16)
        copy = pltpu.make_async_copy(meta.at[slot], out.at[pl.ds(base, META)], sem)
        copy.start()
        copies.append(copy)
    for copy in copies:
        copy.wait()


def gathered(roles, directions, charges, present, left):
    _, sectors, width, _ = left.shape
    rows = sectors * width + META
    pieces = sum(len(wanted) for wanted in roles)
    return pl.pallas_call(
        functools.partial(gather_kernel, roles),
        out_shape=[jax.ShapeDtypeStruct((rows * len(wanted), width), BF16) for wanted in roles],
        in_specs=[SMEM, SMEM, SMEM, ANY],
        out_specs=[ANY] * len(roles),
        scratch_shapes=[pltpu.VMEM((pieces, META, width), BF16), pltpu.SemaphoreType.DMA],
        compiler_params=params(),
        cost_estimate=cost(0, 4 * rows * width * pieces),
        name="gather_" + "_".join(wanted[0] for wanted in roles),
    )(directions, charges, present, left)


def sigma_kernel(split, chunk, charges_ref, present_ref, left, right, wave, rotations, *refs):
    outs, acc = refs[:-1], refs[-1]
    pair = pl.program_id(0)
    sectors, width = wave.shape[0], wave.shape[1]

    @pl.when(pair == 0)
    def _():
        acc[...] = jnp.zeros_like(acc)
        for s in range(sectors):
            outs[-1][s] = rotations[s].T

    charge = charges_ref[pair]
    for s in range(sectors):
        halfway = jnp.dot(left[0, s], wave[s], preferred_element_type=F32)
        halfway = (halfway * present_ref[pair, s].astype(F32)).astype(BF16)
        term = lax.dot_general(
            halfway, right[0, s], (((1,), (1,)), ((), ())), preferred_element_type=F32
        )
        at = jnp.clip(s + 1 + charge, 0, sectors + 1)
        acc[at] += term

    @pl.when(pair == pl.num_programs(0) - 1)
    def _():
        if not split:
            outs[0][...] = acc[...]
            return
        bit = lax.rem(lax.axis_index("op"), 2)
        for q in range(width // chunk // 2):
            to = slice(q * chunk, (q + 1) * chunk)
            for t in range(sectors + 2):
                outs[0][t, to] = acc[t, pl.ds((2 * q + 1 - bit) * chunk, chunk)].astype(BF16)
                outs[1][t, to] = acc[t, pl.ds((2 * q + bit) * chunk, chunk)]


def sigma_terms(split, chunk, charges, present, left, right, wave, rotations):
    count, sectors, width, _ = left.shape
    whole = pl.BlockSpec((sectors, width, width), lambda p: (0, 0, 0))
    by_pair = pl.BlockSpec((1, sectors, width, width), lambda p: (p, 0, 0, 0))
    if split:
        shapes = [((sectors + 2, width // 2, width), BF16), ((sectors + 2, width // 2, width), F32)]
    else:
        shapes = [((sectors + 2, width, width), F32)]
    shapes.append(((sectors, width, width), BF16))
    return pl.pallas_call(
        functools.partial(sigma_kernel, split, chunk),
        grid=(count,),
        out_shape=[jax.ShapeDtypeStruct(*shape) for shape in shapes],
        in_specs=[SMEM, SMEM, by_pair, by_pair, whole, whole],
        out_specs=[pl.BlockSpec(shape, lambda p: (0, 0, 0)) for shape, _ in shapes],
        scratch_shapes=[pltpu.VMEM((sectors + 2, width, width), F32)],
        compiler_params=params(),
        cost_estimate=cost(4 * count * sectors * width**3, 4 * left.size + 4 * left.size),
        name="sigma_terms",
    )(charges, present, left, right, wave, rotations)


def edges_kernel(keep, got, turned, up, down, mid):
    height = keep.shape[1]
    sectors = mid.shape[0]
    up[:height] = (keep[sectors + 1] + got[sectors + 1].astype(F32)).astype(BF16)
    up[height:] = turned[sectors - 1]
    down[:height] = (keep[0] + got[0].astype(F32)).astype(BF16)
    down[height:] = turned[0]
    for s in range(sectors):
        mid[s] = keep[s + 1] + got[s + 1].astype(F32)


def edges(keep, got, turned):
    outer, height, width = keep.shape
    rows = height + turned.shape[1]
    return pl.pallas_call(
        edges_kernel,
        out_shape=[
            jax.ShapeDtypeStruct((rows, width), BF16),
            jax.ShapeDtypeStruct((rows, width), BF16),
            jax.ShapeDtypeStruct((outer - 2, height, width), F32),
        ],
        in_specs=[VMEM] * 3,
        out_specs=[VMEM] * 3,
        compiler_params=params(),
        cost_estimate=cost(keep.size, 12 * keep.size),
        name="edges",
    )(keep, got, turned)


def split_kernel(bit, chunk, first, *refs):
    if first:
        mid, below, above, send, keep = refs
    else:
        mid, got, send, keep = refs
    sectors, height, _ = mid.shape
    own = lax.rem(lax.axis_index("op") // bit, 2)

    def total(s, rows):
        value = mid[s, rows]
        if not first:
            return value + got[s, rows].astype(F32)
        if s == 0:
            value = value + below[rows].astype(F32)
        if s == sectors - 1:
            value = value + above[rows].astype(F32)
        return value

    for q in range(height // chunk // 2):
        to = slice(q * chunk, (q + 1) * chunk)
        for s in range(sectors):
            send[s, to] = total(s, pl.ds((2 * q + 1 - own) * chunk, chunk)).astype(BF16)
            keep[s, to] = total(s, pl.ds((2 * q + own) * chunk, chunk))


def split(bit, chunk, first, mid, *more):
    sectors, height, width = mid.shape
    return pl.pallas_call(
        functools.partial(split_kernel, bit, chunk, first),
        out_shape=[
            jax.ShapeDtypeStruct((sectors, height // 2, width), BF16),
            jax.ShapeDtypeStruct((sectors, height // 2, width), F32),
        ],
        in_specs=[VMEM] * (1 + len(more)),
        out_specs=[VMEM] * 2,
        compiler_params=params(),
        cost_estimate=cost(mid.size, 10 * mid.size),
        name="split",
    )(mid, *more)


def renorm_kernel(items, zero, offset, turned_ref, rotations_ref, below_ref, above_ref, *refs):
    buffers = refs[: 1 + max(item[0] for item in items)]
    rest = refs[len(buffers) :]
    if not zero:
        rest = rest[1:]
    out, rot, turned, blocks, results, metas, sems, done = rest
    sectors, width, _ = rotations_ref.shape
    odd = lax.rem(lax.axis_index("op"), 2)
    last = sems.shape[0] - 1
    first = [
        pltpu.make_async_copy(rotations_ref, rot, sems.at[last]),
        pltpu.make_async_copy(turned_ref, turned.at[pl.ds(1, sectors)], sems.at[last]),
        pltpu.make_async_copy(below_ref.at[pl.ds(offset, width)], turned.at[0], sems.at[last]),
        pltpu.make_async_copy(
            above_ref.at[pl.ds(offset, width)], turned.at[sectors + 1], sems.at[last]
        ),
    ]
    for copy in first:
        copy.start()
    loads = []
    for i, (buffer, base, _, _) in enumerate(items):
        source = buffers[buffer]
        copies = [
            pltpu.make_async_copy(
                source.at[pl.ds(base + sectors * width, META)], metas.at[i], sems.at[i]
            )
        ]
        for s in range(sectors):
            copies.append(
                pltpu.make_async_copy(
                    source.at[pl.ds(base + s * width, width)], blocks.at[i, s], sems.at[i]
                )
            )
        for copy in copies:
            copy.start()
        loads.append(copies)
    stores = []
    for copy in first:
        copy.wait()
    for i, (_, _, kind, place) in enumerate(items):
        for copy in loads[i]:
            copy.wait()
        values = metas[i].astype(F32)

        def scalar(row):
            return jnp.max(values[row : row + 1, :])

        charge = scalar(0).astype(jnp.int32)
        if kind == "core":
            kind = 2 - odd
        elif kind == "side":
            kind = 1 + odd
        if place == 1:
            wanted = jnp.where(scalar(1).astype(jnp.int32) == kind, 1.0, 0.0)
        else:
            wanted = jnp.float32(1.0)
        for s in range(sectors):
            weight = scalar(2 + s) * wanted
            rotated = jnp.dot(blocks[i, s], rot[s], preferred_element_type=F32).astype(BF16)
            target = turned[jnp.clip(s + 1 + charge, 0, sectors + 1)]
            value = jnp.dot(target, rotated, preferred_element_type=F32) * weight
            results[i, s] = value.astype(BF16)
        copy = pltpu.make_async_copy(results.at[i], out.at[kind * CAPS + place], done)
        copy.start()
        stores.append(copy)
    if zero:
        results[len(items)] = jnp.zeros_like(results[len(items)])
        for place in range(CAPS):
            copy = pltpu.make_async_copy(results.at[len(items)], out.at[place], done)
            copy.start()
            stores.append(copy)
    for copy in stores:
        copy.wait()


def renorm(name, items, buffers, out, offset, turned, rotations, below, above):
    sectors, width, _ = rotations.shape
    zero = out is None
    operands = [turned, rotations, below, above, *buffers] + ([] if zero else [out])
    count = len(items)
    block = (sectors, width, width)
    return pl.pallas_call(
        functools.partial(renorm_kernel, items, zero, offset),
        out_shape=jax.ShapeDtypeStruct((DIRS * CAPS, *block), BF16),
        in_specs=[ANY] * len(operands),
        out_specs=ANY,
        input_output_aliases={} if zero else {len(operands) - 1: 0},
        scratch_shapes=[
            pltpu.VMEM(block, BF16),
            pltpu.VMEM((sectors + 2, width, width), BF16),
            pltpu.VMEM((count, *block), BF16),
            pltpu.VMEM((count + (1 if zero else 0), *block), BF16),
            pltpu.VMEM((count, META, width), BF16),
            pltpu.SemaphoreType.DMA((count + 1,)),
            pltpu.SemaphoreType.DMA,
        ],
        compiler_params=params(),
        cost_estimate=cost(
            4 * count * sectors * width**3, 4 * (count + 2) * sectors * width * width
        ),
        name=name,
    )(*operands)


def body(
    wavefunction, left_operators, right_operators, rotations, charges, present_blocks, directions
):
    sectors, width, _ = wavefunction.shape
    pairs = left_operators.shape[0]
    n = lax.axis_size("op")
    levels = lax.axis_size("sec")
    half = n // 2
    chunk = width // n
    halving = n & (n - 1) == 0 and chunk % 16 == 0
    rows = sectors * width + META

    def over_op(value, target):
        return lax.ppermute(value, "op", [(i, target(i)) for i in range(n)])

    def up(value):
        return lax.ppermute(value, "sec", [(i, i + 1) for i in range(levels - 1)])

    def down(value):
        return lax.ppermute(value, "sec", [(i + 1, i) for i in range(levels - 1)])

    def side(i):
        return (i + 1) % n if i % 2 else (i - 1) % n

    def side_or_across(i):
        place = i % half
        if place == half - 1:
            return i - place
        if place == 0:
            return i + half - 1
        return side(i)

    small = (directions, charges, present_blocks, left_operators)
    (extra,) = gathered((("extra",),), *small)
    extra_half = over_op(extra, lambda i: (i + half) % n)
    first_core, first_side, first_half = gathered(
        (("extra", "core"), ("side",), ("half",)), *small
    )
    from_core = over_op(first_core, lambda i: i ^ 1)
    from_side = over_op(first_side, side)
    from_half = over_op(first_half, lambda i: (i + half) % n)

    *terms, turned = sigma_terms(
        halving,
        chunk,
        charges,
        present_blocks,
        left_operators,
        right_operators,
        wavefunction,
        rotations,
    )
    if halving:
        send, keep = terms
        got = over_op(send, lambda i: i ^ 1)
        above_edge, below_edge, mid = edges(keep, got, turned)
        below, above = up(above_edge), down(below_edge)
        offset = width // 2
        bit = 2
        send, keep = split(bit, chunk, True, mid, below, above)
        got = over_op(send, lambda i: i ^ 2)
        while 2 * bit < n:
            bit *= 2
            send, keep = split(bit, chunk, False, keep, got)
            got = over_op(send, lambda i: i ^ bit)
        summed = keep + got.astype(F32)
    else:
        (terms,) = terms
        offset = width
        below = up(jnp.concatenate([terms[sectors + 1].astype(BF16), turned[sectors - 1]]))
        above = down(jnp.concatenate([terms[0].astype(BF16), turned[0]]))
        mid = terms[1 : sectors + 1]
        mid = mid.at[0].add(below[:width].astype(F32))
        mid = mid.at[sectors - 1].add(above[:width].astype(F32))
        summed = lax.psum_scatter(mid, "op", scatter_dimension=1, tiled=True)
    sigma_vector = summed / math.sqrt(pairs * n)

    place = lax.axis_index("op") % half
    cut = jnp.logical_or(place == 0, place == half - 1)
    relayed = jnp.where(cut, extra_half, extra)
    extra_side = over_op(relayed, side_or_across)

    fixed = (offset, turned, rotations, below, above)
    out = renorm(
        "renorm_core",
        ((0, 0, "core", 1), (0, rows, "core", 0), (1, 0, 3, 1)),
        (from_core, extra_half),
        None,
        *fixed,
    )
    out = renorm("renorm_side", ((0, 0, "side", 0),), (from_side,), out, *fixed)
    out = renorm("renorm_extra", ((0, 0, "side", 1),), (extra_side,), out, *fixed)
    out = renorm("renorm_half", ((0, 0, 3, 0),), (from_half,), out, *fixed)
    return sigma_vector, out


def solution(mesh):
    placed = (
        P("sec", None, None),
        P("op", "sec", None, None),
        P("op", "sec", None, None),
        P("sec", None, None),
        P("op"),
        P("op", "sec"),
        P("op", None),
    )
    return jax.shard_map(
        body,
        mesh=mesh,
        in_specs=placed,
        out_specs=(P("sec", "op", None), P("op", "sec", None, None)),
        check_vma=False,
    )
```

time: 127 us -> 67.1 us (0.53)
  the two profiles are of different devices: /device:TPU:1 before, /device:TPU:0 now
where the time goes in v1:
time: 67.1 us; the launch traced here: 66.6 us
  Pallas kernels  22.1 us (33%)
  waiting for transfers between devices  22 us (33%)
  starting transfers between devices  11.7 us (17%)
  local copies, waits for them, and re-layouts  9.29 us (14%)
  between operations  0.76 us (1%)
  other arithmetic  0.74 us (1%)
    ppermute x8, waiting for transfers between devices, over_op(): return lax.ppermute(value, 'op', [(i, target(i)) for i in range(n)])  14.9 us
    pallas_call x4, Pallas kernels, renorm(): pl.pallas_call(functools.partial(renorm_kernel, items, zero, offset), out...  13.7 us
    unnamed x23, local copies, waits for them, and re-layouts  9.29 us
    ppermute x8, starting transfers between devices, over_op(): return lax.ppermute(value, 'op', [(i, target(i)) for i in range(n)])  6.92 us
    ppermute x1, waiting for transfers between devices, down(): return lax.ppermute(value, 'sec', [(i + 1, i) for i in range(levels - 1)])  4.12 us
    pallas_call x1, Pallas kernels, sigma_terms(): pl.pallas_call(functools.partial(sigma_kernel, split, chunk), grid=(count...  3.91 us
    ppermute x1, starting transfers between devices, up(): return lax.ppermute(value, 'sec', [(i, i + 1) for i in range(levels - 1)])  3.49 us
    pallas_call x2, Pallas kernels, gathered(): pl.pallas_call(functools.partial(gather_kernel, roles), out_shape=[jax.Sh...  3.3 us
  transfers between devices with their start and end apart: 10, of which 4 were waited for; matrix products, arithmetic and copies ran while one was open for 1% of the time, Pallas kernels for 27%

profile of v1, /device:TPU:0, one launch (start us, length us, event | category | flops | bytes accessed | tf_op | source)
XLA Modules:
  0.0 66.6 jit_solution(6466657351986009437)
XLA Ops:
  0.6 0.7 %copy.12.directions_ref = s32[4,1]{1,0:T(4,128)S(1)} copy(s32[4,1]{0,1:T(1,128)} %param.13) | data formatting | bytes 32 | tf_op args[6]
  1.4 1.6 %copy-done = bf16[4,4,256,256]{3,2,1,0:T(8,128)(2,1)S(1)} copy-done((bf16[4,4,256,256]{3,2,1,0:T(8,128)(2,1)S(1)}, bf16[4,4,256,256]{3,2,1,0:T(8,128)(2,1)}, u32[]{:S(2)}) %copy-start) | copy-done | bytes 2097176
  4.3 1.3 %gather_extra.1 = bf16[1040,256]{1,0:T(8,128)(2,1)S(1)} custom-call(s32[4,1]{1,0:T(4,128)S(1)} %copy.12.directions_ref, s32[4]{0:T(128)S(1)} %copy-done.8, s32[4,4]{1,0:T(4,128)S(1)} %copy-done.7, bf16[4,4,256,256]{3,2,1,0:T(8,128)(2,1)S(1)} %copy-done), custom_call_target="tpu_custom_call" | custom-call | bytes 1064960 | tf_op jit(solution)/shard_map/gather_extra/pallas_call | solution.py:98
  5.6 3.0 %collective-permute-start.6 = (bf16[1040,256]{1,0:T(8,128)(2,1)S(1)}, bf16[1040,256]{1,0:T(8,128)(2,1)S(1)}, u32[]{:S(2)}, u32[]{:S(2)}) collective-permute-start(bf16[1040,256]{1,0:T(8,128)(2,1)S(1)} %gather_extra.1), channel_id=1, source_target_pairs={{0,16},{4,20},{8,24},{12,28},{16,0},{20,4},{24,8},{28,12},{1,17},{... | collective-permute-start | bytes 1597448 | tf_op jit(solution)/shard_map/ppermute | solution.py:353
  8.7 1.0 %copy-done.1 = bf16[4,256,256]{2,1,0:T(8,128)(2,1)S(1)} copy-done((bf16[4,256,256]{2,1,0:T(8,128)(2,1)S(1)}, bf16[4,256,256]{2,1,0:T(8,128)(2,1)}, u32[]{:S(2)}) %copy-start.1) | copy-done | bytes 524312
  9.7 1.6 %copy-done.3 = bf16[4,4,256,256]{3,2,1,0:T(8,128)(2,1)S(1)} copy-done((bf16[4,4,256,256]{3,2,1,0:T(8,128)(2,1)S(1)}, bf16[4,4,256,256]{3,2,1,0:T(8,128)(2,1)}, u32[]{:S(2)}) %copy-start.3) | copy-done | bytes 2097176
  11.3 1.0 %copy-done.6 = bf16[4,256,256]{2,1,0:T(8,128)(2,1)S(1)} copy-done((bf16[4,256,256]{2,1,0:T(8,128)(2,1)S(1)}, bf16[4,256,256]{2,1,0:T(8,128)(2,1)}, u32[]{:S(2)}) %copy-start.6) | copy-done | bytes 524312
  12.3 3.9 %sigma_terms.1 = (bf16[6,128,256]{2,1,0:T(8,128)(2,1)}, f32[6,128,256]{2,1,0:T(8,128)S(1)}, bf16[4,256,256]{2,1,0:T(8,128)(2,1)S(1)}) custom-call(s32[4]{0:T(128)S(1)} %copy-done.8, s32[4,4]{1,0:T(4,128)S(1)} %copy-done.7, bf16[4,4,256,256]{3,2,1,0:T(8,128)(2,1)S(1)} %copy-done, bf16[4,4,256,256]{3,2,1,0:T(8,128)(2,1)S(1)} %copy-done.3, ...), custom_call_target="tpu_custom_call" | custom-call | flops 1073741824 | bytes 8388608 | tf_op jit(solution)/shard_map/sigma_terms/pallas_call | solution.py:153
  16.3 2.0 %gather_extra_side_half.1 = (bf16[2080,256]{1,0:T(8,128)(2,1)}, bf16[1040,256]{1,0:T(8,128)(2,1)}, bf16[1040,256]{1,0:T(8,128)(2,1)S(1)}) custom-call(s32[4,1]{1,0:T(4,128)S(1)} %copy.12.directions_ref, s32[4]{0:T(128)S(1)} %copy-done.8, s32[4,4]{1,0:T(4,128)S(1)} %copy-done.7, bf16[4,4,256,256]{3,2,1,0:T(8,128)(2,1)S(1)} %copy-done), custom_call_target="tpu_custom_call" | custom-call | bytes 4259840 | tf_op jit(solution)/shard_map/gather_extra_side_half/pallas_call | solution.py:98
  18.3 0.8 %copy-done.9 = bf16[1040,256]{1,0:T(8,128)(2,1)} copy-done((bf16[1040,256]{1,0:T(8,128)(2,1)}, bf16[1040,256]{1,0:T(8,128)(2,1)S(1)}, u32[]{:S(2)}) %copy-start.9) | copy-done | bytes 532504
  19.6 1.0 %collective-permute-start.8 = (bf16[1040,256]{1,0:T(8,128)(2,1)}, bf16[1040,256]{1,0:T(8,128)(2,1)}, u32[]{:S(2)}, u32[]{:S(2)}) collective-permute-start(bf16[1040,256]{1,0:T(8,128)(2,1)} %get-tuple-element.26), channel_id=1, source_target_pairs={{0,28},{4,8},{8,4},{12,16},{16,12},{20,24},{24,20},{28,0},{1,29},{... | collective-permute-start | bytes 1597448 | tf_op jit(solution)/shard_map/ppermute | solution.py:353
  20.6 1.1 %copy-done.5 = f32[6,128,256]{2,1,0:T(8,128)S(1)} copy-done((f32[6,128,256]{2,1,0:T(8,128)S(1)}, f32[6,128,256]{2,1,0:T(8,128)}, u32[]{:S(2)}) %copy-start.5) | copy-done | bytes 786456
  21.8 1.1 %edges.1 = (bf16[384,256]{1,0:T(8,128)(2,1)S(1)}, bf16[384,256]{1,0:T(8,128)(2,1)S(1)}, f32[4,128,256]{2,1,0:T(8,128)S(1)}) custom-call(f32[6,128,256]{2,1,0:T(8,128)S(1)} %copy-done.5, bf16[6,128,256]{2,1,0:T(8,128)(2,1)} %collective-permute-done.got, bf16[4,256,256]{2,1,0:T(8,128)(2,1)S(1)} %get-tuple-element.17.turned.turned_ref), custom_call_target="tpu_custom_call" | custom-call | flops 196608 | bytes 2359296 | tf_op jit(solution)/shard_map/edges/pallas_call | solution.py:180
  22.9 3.5 %collective-permute-start.1 = (bf16[384,256]{1,0:T(8,128)(2,1)S(1)}, bf16[384,256]{1,0:T(8,128)(2,1)S(1)}, u32[]{:S(2)}, u32[]{:S(2)}) collective-permute-start(bf16[384,256]{1,0:T(8,128)(2,1)S(1)} %get-tuple-element.19), channel_id=1, source_target_pairs={{0,1},{1,2},{2,3},{4,5},{5,6},{6,7},{8,9},{9,10},{10,11},{12,13},{... | collective-permute-start | bytes 589832 | tf_op jit(solution)/shard_map/ppermute | solution.py:356
  26.4 1.3 %collective-permute-start.2 = (bf16[384,256]{1,0:T(8,128)(2,1)S(1)}, bf16[384,256]{1,0:T(8,128)(2,1)S(1)}, u32[]{:S(2)}, u32[]{:S(2)}) collective-permute-start(bf16[384,256]{1,0:T(8,128)(2,1)S(1)} %get-tuple-element.20), channel_id=1, source_target_pairs={{1,0},{2,1},{3,2},{5,4},{6,5},{7,6},{9,8},{10,9},{11,10},{13,12},{... | collective-permute-start | bytes 589832 | tf_op jit(solution)/shard_map/ppermute | solution.py:359
  28.2 3.0 %collective-permute-done.1.refs_1_.below_ref = bf16[384,256]{1,0:T(8,128)(2,1)S(1)} collective-permute-done((bf16[384,256]{1,0:T(8,128)(2,1)S(1)}, bf16[384,256]{1,0:T(8,128)(2,1)S(1)}, u32[]{:S(2)}, u32[]{:S(2)}) %collective-permute-start.1) | collective-permute-done | bytes 196640 | tf_op jit(solution)/shard_map/ppermute | solution.py:356
  31.2 4.1 %collective-permute-done.2.refs_2_.above_ref = bf16[384,256]{1,0:T(8,128)(2,1)S(1)} collective-permute-done((bf16[384,256]{1,0:T(8,128)(2,1)S(1)}, bf16[384,256]{1,0:T(8,128)(2,1)S(1)}, u32[]{:S(2)}, u32[]{:S(2)}) %collective-permute-start.2) | collective-permute-done | bytes 196640 | tf_op jit(solution)/shard_map/ppermute | solution.py:359
  36.0 1.1 %collective-permute-start.5 = (bf16[1040,256]{1,0:T(8,128)(2,1)S(1)}, bf16[1040,256]{1,0:T(8,128)(2,1)S(1)}, u32[]{:S(2)}, u32[]{:S(2)}) collective-permute-start(bf16[1040,256]{1,0:T(8,128)(2,1)S(1)} %copy-done.10), channel_id=1, source_target_pairs={{0,16},{4,20},{8,24},{12,28},{16,0},{20,4},{24,8},{28,12},{1,17},{... | collective-permute-start | bytes 1597448 | tf_op jit(solution)/shard_map/ppermute | solution.py:353
  37.1 10.8 %collective-permute-done.3.refs_1_ = bf16[4,64,256]{2,1,0:T(8,128)(2,1)S(1)} collective-permute-done((bf16[4,64,256]{2,1,0:T(8,128)(2,1)S(1)}, bf16[4,64,256]{2,1,0:T(8,128)(2,1)S(1)}, u32[]{:S(2)}, u32[]{:S(2)}) %collective-permute-start.3) | collective-permute-done | bytes 131104 | tf_op jit(solution)/shard_map/ppermute | solution.py:353
  48.1 4.1 %collective-permute-done.4 = bf16[4,32,256]{2,1,0:T(8,128)(2,1)S(1)} collective-permute-done((bf16[4,32,256]{2,1,0:T(8,128)(2,1)S(1)}, bf16[4,32,256]{2,1,0:T(8,128)(2,1)S(1)}, u32[]{:S(2)}, u32[]{:S(2)}) %collective-permute-start.4) | collective-permute-done | bytes 65568 | tf_op jit(solution)/shard_map/ppermute | solution.py:353
  52.9 5.6 %renorm_core.1.refs_1_ = bf16[8,4,256,256]{3,2,1,0:T(8,128)(2,1)} custom-call(bf16[4,256,256]{2,1,0:T(8,128)(2,1)S(1)} %get-tuple-element.17.turned.turned_ref, bf16[4,256,256]{2,1,0:T(8,128)(2,1)S(1)} %copy-done.2, bf16[384,256]{1,0:T(8,128)(2,1)S(1)} %collective-permute-done.1.refs_1_.below_ref, ...), custom_call_target="tpu_custom_call" | custom-call | flops 805306368 | bytes 5242880 | tf_op jit(solution)/shard_map/renorm_core/pallas_call | solution.py:317
  58.5 3.0 %renorm_side.1.refs_1_ = bf16[8,4,256,256]{3,2,1,0:T(8,128)(2,1)} custom-call(bf16[4,256,256]{2,1,0:T(8,128)(2,1)S(1)} %get-tuple-element.17.turned.turned_ref, bf16[4,256,256]{2,1,0:T(8,128)(2,1)S(1)} %copy-done.2, bf16[384,256]{1,0:T(8,128)(2,1)S(1)} %collective-permute-done.1.refs_1_.below_ref, ...), custom_call_target="tpu_custom_call", output_to_operand_aliasing={{}: (5, {})} | custom-call | flops 268435456 | bytes 3145728 | tf_op jit(solution)/shard_map/renorm_side/pallas_call | solution.py:317
  61.5 2.6 %renorm_extra.1.refs_1_ = bf16[8,4,256,256]{3,2,1,0:T(8,128)(2,1)} custom-call(bf16[4,256,256]{2,1,0:T(8,128)(2,1)S(1)} %get-tuple-element.17.turned.turned_ref, bf16[4,256,256]{2,1,0:T(8,128)(2,1)S(1)} %copy-done.2, bf16[384,256]{1,0:T(8,128)(2,1)S(1)} %collective-permute-done.1.refs_1_.below_ref, ...), custom_call_target="tpu_custom_call", output_to_operand_aliasing={{}: (5, {})} | custom-call | flops 268435456 | bytes 3145728 | tf_op jit(solution)/shard_map/renorm_extra/pallas_call | solution.py:317
  64.1 2.6 %renorm_half.1 = bf16[8,4,256,256]{3,2,1,0:T(8,128)(2,1)} custom-call(bf16[4,256,256]{2,1,0:T(8,128)(2,1)S(1)} %get-tuple-element.17.turned.turned_ref, bf16[4,256,256]{2,1,0:T(8,128)(2,1)S(1)} %copy-done.2, bf16[384,256]{1,0:T(8,128)(2,1)S(1)} %collective-permute-done.1.refs_1_.below_ref, ...), custom_call_target="tpu_custom_call", output_to_operand_aliasing={{}: (5, {})} | custom-call | flops 268435456 | bytes 3145728 | tf_op jit(solution)/shard_map/renorm_half/pallas_call | solution.py:317
  (31 shorter events, 3.9 us)
Async XLA Ops:
  1.4 1.6 %copy-start = (bf16[4,4,256,256]{3,2,1,0:T(8,128)(2,1)S(1)}, bf16[4,4,256,256]{3,2,1,0:T(8,128)(2,1)}, u32[]{:S(2)}) copy-start(bf16[4,4,256,256]{3,2,1,0:T(8,128)(2,1)} %left_ref.3) | copy-start | bytes 6291460
  3.0 0.7 %copy-start.7 = (s32[4,4]{1,0:T(4,128)S(1)}, s32[4,4]{1,0:T(4,128)}, u32[]{:S(2)}) copy-start(s32[4,4]{1,0:T(4,128)} %present_ref.5) | copy-start | bytes 196
  3.6 0.7 copy-start.8
  5.6 22.1 %collective-permute-start.6 = (bf16[1040,256]{1,0:T(8,128)(2,1)S(1)}, bf16[1040,256]{1,0:T(8,128)(2,1)S(1)}, u32[]{:S(2)}, u32[]{:S(2)}) collective-permute-start(bf16[1040,256]{1,0:T(8,128)(2,1)S(1)} %gather_extra.1), channel_id=1, source_target_pairs={{0,16},{4,20},{8,24},{12,28},{16,0},{20,4},{24,8},{28,12},{1,17},{... | collective-permute-start | bytes 1597448 | tf_op jit(solution)/shard_map/ppermute | solution.py:353
  8.7 1.0 %copy-start.1 = (bf16[4,256,256]{2,1,0:T(8,128)(2,1)S(1)}, bf16[4,256,256]{2,1,0:T(8,128)(2,1)}, u32[]{:S(2)}) copy-start(bf16[4,256,256]{2,1,0:T(8,128)(2,1)} %rotations_ref.7) | copy-start | bytes 1572868
  9.7 1.6 %copy-start.3 = (bf16[4,4,256,256]{3,2,1,0:T(8,128)(2,1)S(1)}, bf16[4,4,256,256]{3,2,1,0:T(8,128)(2,1)}, u32[]{:S(2)}) copy-start(bf16[4,4,256,256]{3,2,1,0:T(8,128)(2,1)} %right.1) | copy-start | bytes 6291460
  11.3 1.0 %copy-start.6 = (bf16[4,256,256]{2,1,0:T(8,128)(2,1)S(1)}, bf16[4,256,256]{2,1,0:T(8,128)(2,1)}, u32[]{:S(2)}) copy-start(bf16[4,256,256]{2,1,0:T(8,128)(2,1)} %wave.1) | copy-start | bytes 1572868
  16.3 2.0 %copy-start.4 = (f32[6,128,256]{2,1,0:T(8,128)}, f32[6,128,256]{2,1,0:T(8,128)S(1)}, u32[]{:S(2)}) copy-start(f32[6,128,256]{2,1,0:T(8,128)S(1)} %get-tuple-element.15.keep) | copy-start | bytes 2359300
  16.3 36.6 %copy-start.2 = (bf16[4,256,256]{2,1,0:T(8,128)(2,1)S(1)}, bf16[4,256,256]{2,1,0:T(8,128)(2,1)}, u32[]{:S(2)}) copy-start(bf16[4,256,256]{2,1,0:T(8,128)(2,1)} %rotations_ref.7) | copy-start | bytes 1572868
  16.3 4.4 %collective-permute-start = (bf16[6,128,256]{2,1,0:T(8,128)(2,1)}, bf16[6,128,256]{2,1,0:T(8,128)(2,1)}, u32[]{:S(2)}, u32[]{:S(2)}) collective-permute-start(bf16[6,128,256]{2,1,0:T(8,128)(2,1)} %get-tuple-element.16), channel_id=1, source_target_pairs={{0,4},{4,0},{8,12},{12,8},{16,20},{20,16},{24,28},{28,24},{1,5},{5... | collective-permute-start | bytes 1179656 | tf_op jit(solution)/shard_map/ppermute | solution.py:353
  18.3 0.8 %copy-start.9 = (bf16[1040,256]{1,0:T(8,128)(2,1)}, bf16[1040,256]{1,0:T(8,128)(2,1)S(1)}, u32[]{:S(2)}) copy-start(bf16[1040,256]{1,0:T(8,128)(2,1)S(1)} %get-tuple-element.25) | copy-start | bytes 1597444
  19.1 33.8 %collective-permute-start.9 = (bf16[2080,256]{1,0:T(8,128)(2,1)}, bf16[2080,256]{1,0:T(8,128)(2,1)S(1)}, u32[]{:S(2)}, u32[]{:S(2)}) collective-permute-start(bf16[2080,256]{1,0:T(8,128)(2,1)} %get-tuple-element.27), channel_id=1, source_target_pairs={{0,4},{4,0},{8,12},{12,8},{16,20},{20,16},{24,28},{28,24},{1,5},{5... | collective-permute-start | bytes 3194888 | tf_op jit(solution)/shard_map/ppermute | solution.py:353
  19.6 38.9 %collective-permute-start.8 = (bf16[1040,256]{1,0:T(8,128)(2,1)}, bf16[1040,256]{1,0:T(8,128)(2,1)}, u32[]{:S(2)}, u32[]{:S(2)}) collective-permute-start(bf16[1040,256]{1,0:T(8,128)(2,1)} %get-tuple-element.26), channel_id=1, source_target_pairs={{0,28},{4,8},{8,4},{12,16},{16,12},{20,24},{24,20},{28,0},{1,29},{... | collective-permute-start | bytes 1597448 | tf_op jit(solution)/shard_map/ppermute | solution.py:353
  20.6 1.1 %copy-start.5 = (f32[6,128,256]{2,1,0:T(8,128)S(1)}, f32[6,128,256]{2,1,0:T(8,128)}, u32[]{:S(2)}) copy-start(f32[6,128,256]{2,1,0:T(8,128)} %copy-done.4) | copy-start | bytes 2359300
  21.8 14.2 %copy-start.10 = (bf16[1040,256]{1,0:T(8,128)(2,1)S(1)}, bf16[1040,256]{1,0:T(8,128)(2,1)}, u32[]{:S(2)}) copy-start(bf16[1040,256]{1,0:T(8,128)(2,1)} %copy-done.9) | copy-start | bytes 1597444
  22.9 8.4 %collective-permute-start.1 = (bf16[384,256]{1,0:T(8,128)(2,1)S(1)}, bf16[384,256]{1,0:T(8,128)(2,1)S(1)}, u32[]{:S(2)}, u32[]{:S(2)}) collective-permute-start(bf16[384,256]{1,0:T(8,128)(2,1)S(1)} %get-tuple-element.19), channel_id=1, source_target_pairs={{0,1},{1,2},{2,3},{4,5},{5,6},{6,7},{8,9},{9,10},{10,11},{12,13},{... | collective-permute-start | bytes 589832 | tf_op jit(solution)/shard_map/ppermute | solution.py:356
  26.4 9.0 %collective-permute-start.2 = (bf16[384,256]{1,0:T(8,128)(2,1)S(1)}, bf16[384,256]{1,0:T(8,128)(2,1)S(1)}, u32[]{:S(2)}, u32[]{:S(2)}) collective-permute-start(bf16[384,256]{1,0:T(8,128)(2,1)S(1)} %get-tuple-element.20), channel_id=1, source_target_pairs={{1,0},{2,1},{3,2},{5,4},{6,5},{7,6},{9,8},{10,9},{11,10},{13,12},{... | collective-permute-start | bytes 589832 | tf_op jit(solution)/shard_map/ppermute | solution.py:359
  27.8 33.7 %collective-permute-start.7 = (bf16[1040,256]{1,0:T(8,128)(2,1)S(1)}, bf16[1040,256]{1,0:T(8,128)(2,1)S(1)}, u32[]{:S(2)}, u32[]{:S(2)}) collective-permute-start(bf16[1040,256]{1,0:T(8,128)(2,1)S(1)} %broadcast_select_fusion), channel_id=1, source_target_pairs={{0,12},{4,8},{8,4},{12,0},{16,28},{20,24},{24,20},{28,16},{1,13},{... | collective-permute-start | bytes 1597448 | tf_op jit(solution)/shard_map/ppermute | solution.py:353
  35.4 12.4 %collective-permute-start.3 = (bf16[4,64,256]{2,1,0:T(8,128)(2,1)S(1)}, bf16[4,64,256]{2,1,0:T(8,128)(2,1)S(1)}, u32[]{:S(2)}, u32[]{:S(2)}) collective-permute-start(bf16[4,64,256]{2,1,0:T(8,128)(2,1)S(1)} %get-tuple-element.22), channel_id=1, source_target_pairs={{0,8},{4,12},{8,0},{12,4},{16,24},{20,28},{24,16},{28,20},{1,9},{5... | collective-permute-start | bytes 393224 | tf_op jit(solution)/shard_map/ppermute | solution.py:353
  36.0 28.1 %collective-permute-start.5 = (bf16[1040,256]{1,0:T(8,128)(2,1)S(1)}, bf16[1040,256]{1,0:T(8,128)(2,1)S(1)}, u32[]{:S(2)}, u32[]{:S(2)}) collective-permute-start(bf16[1040,256]{1,0:T(8,128)(2,1)S(1)} %copy-done.10), channel_id=1, source_target_pairs={{0,16},{4,20},{8,24},{12,28},{16,0},{20,4},{24,8},{28,12},{1,17},{... | collective-permute-start | bytes 1597448 | tf_op jit(solution)/shard_map/ppermute | solution.py:353
  47.9 4.3 %collective-permute-start.4 = (bf16[4,32,256]{2,1,0:T(8,128)(2,1)S(1)}, bf16[4,32,256]{2,1,0:T(8,128)(2,1)S(1)}, u32[]{:S(2)}, u32[]{:S(2)}) collective-permute-start(bf16[4,32,256]{2,1,0:T(8,128)(2,1)S(1)} %get-tuple-element.24), channel_id=1, source_target_pairs={{0,16},{4,20},{8,24},{12,28},{16,0},{20,4},{24,8},{28,12},{1,17},{... | collective-permute-start | bytes 196616 | tf_op jit(solution)/shard_map/ppermute | solution.py:353

commit v2 on v0

v2 whole, which is shorter than its diff:
```python
import functools
import math

import jax
import jax.numpy as jnp
from jax import lax
from jax.experimental import pallas as pl
from jax.experimental.pallas import tpu as pltpu
from jax.sharding import PartitionSpec as P

DIRS = 4
CAPS = 2
META = 16

BF16 = jnp.bfloat16
F32 = jnp.float32
ANY = pl.BlockSpec(memory_space=pl.ANY)
HBM = pl.BlockSpec(memory_space=pltpu.HBM)
VMEM = pl.BlockSpec(memory_space=pltpu.VMEM)


def kernel_call(kernel, token, operands, in_specs, out_shape, out_specs, **options):
    mib = options.pop("mib")
    aliases = options.pop("aliases", {})
    grid = options.pop("grid", ())
    ahead = 0 if token is None else 1
    taken = len(operands) + ahead

    def run(*refs):
        refs = list(refs)
        del refs[taken]
        kernel(*refs[ahead:])

    outs = pl.pallas_call(
        run,
        grid=grid,
        out_shape=[jax.ShapeDtypeStruct((8, 128), F32), *out_shape],
        in_specs=[HBM] * ahead + list(in_specs),
        out_specs=[HBM, *out_specs],
        input_output_aliases={i + ahead: o + 1 for i, o in aliases.items()},
        compiler_params=pltpu.CompilerParams(vmem_limit_bytes=mib * 1024 * 1024),
        **options,
    )(*([] if token is None else [token]), *operands)
    return outs[0], list(outs[1:])


def in_hbm(value):
    return pltpu.with_memory_space_constraint(value, pltpu.HBM)


def estimate(flops, moved):
    return pl.CostEstimate(flops=flops, bytes_accessed=moved, transcendentals=0)


def fetch_scalars(pairs, sem):
    copies = [pltpu.make_async_copy(source, kept, sem) for source, kept in pairs]
    for copy in copies:
        copy.start()
    for copy in copies:
        copy.wait()


def pick(kinds, places, kind, place):
    index = jnp.int32(0)
    for p, (own, at) in enumerate(zip(kinds, places)):
        match = at == place if kind is None else jnp.logical_and(at == place, own == kind)
        index = index + jnp.where(match, p, 0)
    return index


def stage_kernel(roles, directions_ref, charges_ref, present_ref, left_ref, wave_ref, rot_ref, *refs):
    outs = refs[: len(roles)]
    left, wave, rot, directions, charges, present, few, sems = refs[len(roles) :]
    bulk = [
        pltpu.make_async_copy(left_ref, left, sems.at[0]),
        pltpu.make_async_copy(wave_ref, wave, sems.at[1]),
        pltpu.make_async_copy(rot_ref, rot, sems.at[2]),
    ]
    for copy in bulk:
        copy.start()
    fetch_scalars(
        [(directions_ref, directions), (charges_ref, charges), (present_ref, present)], few
    )
    count, sectors, width, _ = left_ref.shape
    kinds = [directions[p] for p in range(count)]
    places = []
    for p in range(count):
        place = jnp.int32(0)
        for q in range(p):
            place = place + jnp.where(kinds[q] == kinds[p], 1, 0)
        places.append(place)
    odd = lax.rem(lax.axis_index("op"), 2)
    row = lax.broadcasted_iota(jnp.int32, (META, width), 0)
    bulk[0].wait()
    for out, wanted in zip(outs, roles):
        base = 0
        for role in wanted:
            if role == "extra":
                index = pick(kinds, places, None, 1)
            elif role == "half":
                index = pick(kinds, places, 3, 0)
            elif role == "core":
                index = pick(kinds, places, 1 + odd, 0)
            else:
                index = pick(kinds, places, 2 - odd, 0)
            for s in range(sectors):
                out[base + s * width : base + (s + 1) * width] = left[index, s]
            kind = jnp.int32(0)
            for p in range(count):
                kind = kind + jnp.where(index == p, kinds[p], 0)
            values = jnp.where(row == 0, charges[index], jnp.where(row == 1, kind, 0))
            for s in range(sectors):
                values = jnp.where(row == 2 + s, present[index, s], values)
            base += sectors * width
            out[base : base + META] = values.astype(F32).astype(BF16)
            base += META
    for copy in bulk[1:]:
        copy.wait()


def staged(roles, directions, charges, present, left, wave, rotations):
    count, sectors, width, _ = left.shape
    rows = sectors * width + META
    shapes = [(rows * len(wanted), width) for wanted in roles]
    shapes += [left.shape, wave.shape, rotations.shape]
    return kernel_call(
        functools.partial(stage_kernel, roles),
        None,
        [in_hbm(x) for x in (directions, charges, present, left, wave, rotations)],
        [HBM] * 6,
        [pltpu.VMEM(shape, BF16) for shape in shapes],
        [VMEM] * len(shapes),
        scratch_shapes=[
            pltpu.SMEM((count,), jnp.int32),
            pltpu.SMEM((count,), jnp.int32),
            pltpu.SMEM((count, sectors), jnp.int32),
            pltpu.SemaphoreType.DMA,
            pltpu.SemaphoreType.DMA((3,)),
        ],
        mib=4,
        cost_estimate=estimate(0, 0),
        name="stage",
    )


def sigma_kernel(split, chunk, charges_ref, present_ref, left, right_ref, wave, rotations, *refs):
    outs, (acc, right, charges, present, few, sems) = refs[:-6], refs[-6:]
    count, sectors, width, _ = left.shape
    small = [
        pltpu.make_async_copy(charges_ref, charges, few),
        pltpu.make_async_copy(present_ref, present, few),
    ]
    loads = [pltpu.make_async_copy(right_ref.at[p], right.at[p], sems.at[p]) for p in range(count)]
    for copy in small + loads:
        copy.start()
    acc[...] = jnp.zeros_like(acc)
    for s in range(sectors):
        outs[-1][s] = rotations[s].T
    for copy in small:
        copy.wait()

    def step(pair, carry):
        pltpu.make_async_copy(right_ref.at[pair], right.at[pair], sems.at[pair]).wait()
        charge = charges[pair]
        for s in range(sectors):
            halfway = jnp.dot(left[pair, s], wave[s], preferred_element_type=F32)
            halfway = (halfway * present[pair, s].astype(F32)).astype(BF16)
            term = lax.dot_general(
                halfway, right[pair, s], (((1,), (1,)), ((), ())), preferred_element_type=F32
            )
            acc[jnp.clip(s + 1 + charge, 0, sectors + 1)] += term
        return carry

    lax.fori_loop(0, count, step, 0)
    if not split:
        outs[0][...] = acc[...]
        return
    bit = lax.rem(lax.axis_index("op"), 2)
    for q in range(width // chunk // 2):
        to = slice(q * chunk, (q + 1) * chunk)
        for t in range(sectors + 2):
            outs[0][t, to] = acc[t, pl.ds((2 * q + 1 - bit) * chunk, chunk)].astype(BF16)
            outs[1][t, to] = acc[t, pl.ds((2 * q + bit) * chunk, chunk)]


def sigma_terms(token, split, chunk, charges, present, left, right, wave, rotations):
    count, sectors, width, _ = left.shape
    if split:
        shapes = [((sectors + 2, width // 2, width), BF16), ((sectors + 2, width // 2, width), F32)]
    else:
        shapes = [((sectors + 2, width, width), F32)]
    shapes.append(((sectors, width, width), BF16))
    return kernel_call(
        functools.partial(sigma_kernel, split, chunk),
        token,
        (in_hbm(charges), in_hbm(present), left, in_hbm(right), wave, rotations),
        [HBM, HBM, VMEM, HBM, VMEM, VMEM],
        [pltpu.VMEM(*shape) for shape in shapes],
        [VMEM] * len(shapes),
        scratch_shapes=[
            pltpu.VMEM((sectors + 2, width, width), F32),
            pltpu.VMEM(right.shape, BF16),
            pltpu.SMEM((count,), jnp.int32),
            pltpu.SMEM((count, sectors), jnp.int32),
            pltpu.SemaphoreType.DMA,
            pltpu.SemaphoreType.DMA((count,)),
        ],
        mib=10,
        cost_estimate=estimate(0, 0),
        name="sigma_terms",
    )


def edges_kernel(keep, got, turned, first, second, mid):
    height = keep.shape[1]
    sectors = mid.shape[0]
    odd = lax.rem(lax.axis_index("sec"), 2)
    for out, upward in ((first, odd == 0), (second, odd == 1)):
        edge = jnp.where(upward, sectors + 1, 0)
        out[:height] = (keep[edge] + got[edge].astype(F32)).astype(BF16)
        out[height:] = turned[jnp.where(upward, sectors - 1, 0)]
    for s in range(sectors):
        mid[s] = keep[s + 1] + got[s + 1].astype(F32)


def edges(token, keep, got, turned):
    outer, height, width = keep.shape
    rows = height + turned.shape[1]
    return kernel_call(
        edges_kernel,
        token,
        (keep, got, turned),
        [VMEM] * 3,
        [
            jax.ShapeDtypeStruct((rows, width), BF16),
            jax.ShapeDtypeStruct((rows, width), BF16),
            jax.ShapeDtypeStruct((outer - 2, height, width), F32),
        ],
        [VMEM] * 3,
        mib=6,
        cost_estimate=estimate(keep.size, 12 * keep.size),
        name="edges",
    )


def split_kernel(bit, chunk, levels, first, *refs):
    if first:
        mid, one, two, send, keep = refs
    else:
        mid, got, send, keep = refs
    sectors, height, _ = mid.shape
    own = lax.rem(lax.axis_index("op") // bit, 2)
    level = lax.axis_index("sec")
    odd = lax.rem(level, 2) == 1

    def total(s, rows):
        value = mid[s, rows]
        if not first:
            return value + got[s, rows].astype(F32)
        if s == 0:
            below = jnp.where(odd, one[rows], two[rows]).astype(F32)
            value = value + jnp.where(level > 0, below, 0.0)
        if s == sectors - 1:
            above = jnp.where(odd, two[rows], one[rows]).astype(F32)
            value = value + jnp.where(level < levels - 1, above, 0.0)
        return value

    for q in range(height // chunk // 2):
        to = slice(q * chunk, (q + 1) * chunk)
        for s in range(sectors):
            send[s, to] = total(s, pl.ds((2 * q + 1 - own) * chunk, chunk)).astype(BF16)
            keep[s, to] = total(s, pl.ds((2 * q + own) * chunk, chunk))


def split(token, bit, chunk, levels, mid, *more):
    sectors, height, width = mid.shape
    return kernel_call(
        functools.partial(split_kernel, bit, chunk, levels, len(more) == 2),
        token,
        (mid, *more),
        [VMEM] * (1 + len(more)),
        [
            jax.ShapeDtypeStruct((sectors, height // 2, width), BF16),
            jax.ShapeDtypeStruct((sectors, height // 2, width), F32),
        ],
        [VMEM] * 2,
        mib=4,
        cost_estimate=estimate(mid.size, 10 * mid.size),
        name="split",
    )


def relay_kernel(half, own, other, out):
    place = lax.rem(lax.axis_index("op"), half)
    end = jnp.logical_or(place == 0, place == half - 1)

    @pl.when(end)
    def _():
        out[...] = other[...]

    @pl.when(jnp.logical_not(end))
    def _():
        out[...] = own[...]


def relay(token, half, own, other):
    return kernel_call(
        functools.partial(relay_kernel, half),
        token,
        (own, other),
        [VMEM] * 2,
        [jax.ShapeDtypeStruct(own.shape, BF16)],
        [VMEM],
        mib=4,
        cost_estimate=estimate(0, 6 * own.size),
        name="relay",
    )


def hold_kernel(source, kept):
    pass


def hold(token, value):
    return kernel_call(
        hold_kernel,
        token,
        (value,),
        [ANY],
        [jax.ShapeDtypeStruct(value.shape, value.dtype)],
        [ANY],
        aliases={0: 0},
        mib=1,
        cost_estimate=estimate(0, 0),
        name="hold",
    )


def renorm_kernel(items, zero, offset, levels, turned, rotations, one, two, *refs):
    buffers = refs[: 1 + max(item[0] for item in items)]
    rest = refs[len(buffers) + (0 if zero else 1) :]
    out, edge, results, done = rest
    sectors, width, _ = rotations.shape
    odd = lax.rem(lax.axis_index("op"), 2)
    level = lax.axis_index("sec")
    raised = lax.rem(level, 2) == 1
    rows = pl.ds(offset, width)
    stores = []
    if zero:
        results[len(items)] = jnp.zeros_like(results[len(items)])
        for place in range(CAPS):
            copy = pltpu.make_async_copy(results.at[len(items)], out.at[place], done)
            copy.start()
            stores.append(copy)
    edge[0] = jnp.where(raised, one[rows], two[rows])
    edge[1] = jnp.where(raised, two[rows], one[rows])
    for i, (buffer, base, kind, place) in enumerate(items):
        values = buffers[buffer][pl.ds(base + sectors * width, META)].astype(F32)

        def scalar(row):
            return jnp.max(values[row : row + 1, :])

        charge = scalar(0).astype(jnp.int32)
        if kind == "core":
            kind = 2 - odd
        elif kind == "side":
            kind = 1 + odd
        if place == 1:
            wanted = jnp.where(scalar(1).astype(jnp.int32) == kind, 1.0, 0.0)
        else:
            wanted = jnp.float32(1.0)
        for s in range(sectors):
            at = s + charge
            whole = level * sectors + at
            inside = jnp.logical_and(whole >= 0, whole < levels * sectors)
            weight = jnp.where(inside, scalar(2 + s) * wanted, 0.0)
            block = buffers[buffer][pl.ds(base + s * width, width)]
            rotated = jnp.dot(block, rotations[s], preferred_element_type=F32).astype(BF16)
            target = turned[jnp.clip(at, 0, sectors - 1)]
            if s == 0:
                target = jnp.where(at < 0, edge[0], target)
            if s == sectors - 1:
                target = jnp.where(at > sectors - 1, edge[1], target)
            value = jnp.dot(target, rotated, preferred_element_type=F32) * weight
            results[i, s] = value.astype(BF16)
            copy = pltpu.make_async_copy(results.at[i, s], out.at[kind * CAPS + place, s], done)
            copy.start()
            stores.append(copy)
    for copy in stores:
        copy.wait()


def renorm(token, name, items, buffers, out, offset, levels, turned, rotations, one, two):
    sectors, width, _ = rotations.shape
    zero = out is None
    operands = [turned, rotations, one, two, *buffers]
    in_specs = [VMEM] * len(operands)
    if not zero:
        operands.append(out)
        in_specs.append(HBM)
    count = len(items)
    block = (sectors, width, width)
    token, (out,) = kernel_call(
        functools.partial(renorm_kernel, items, zero, offset, levels),
        token,
        operands,
        in_specs,
        [jax.ShapeDtypeStruct((DIRS * CAPS, *block), BF16)],
        [HBM],
        aliases={} if zero else {len(operands) - 1: 0},
        scratch_shapes=[
            pltpu.VMEM((2, width, width), BF16),
            pltpu.VMEM((count + (1 if zero else 0), *block), BF16),
            pltpu.SemaphoreType.DMA,
        ],
        mib=12,
        cost_estimate=estimate(
            4 * count * sectors * width**3, 4 * (count + 2) * sectors * width * width
        ),
        name=name,
    )
    return token, out


def body(
    wavefunction, left_operators, right_operators, rotations, charges, present_blocks, directions
):
    sectors, width, _ = wavefunction.shape
    pairs = left_operators.shape[0]
    n = lax.axis_size("op")
    levels = lax.axis_size("sec")
    half = n // 2
    chunk = width // n
    halving = n & (n - 1) == 0 and chunk % 16 == 0
    rows = sectors * width + META

    def over_op(value, target):
        return lax.ppermute(value, "op", [(i, target(i)) for i in range(n)])

    def swapped(value, start):
        to = list(range(levels))
        for i in range(start, levels - 1, 2):
            to[i], to[i + 1] = i + 1, i
        return lax.ppermute(value, "sec", list(enumerate(to)))

    def side(i):
        return (i + 1) % n if i % 2 else (i - 1) % n

    def side_or_across(i):
        place = i % half
        if place == half - 1:
            return i - place
        if place == 0:
            return i + half - 1
        return side(i)

    roles = (("extra",), ("side",), ("extra", "core"), ("half",))
    token, (extra, first_side, first_core, first_half, left, wave, rotations) = staged(
        roles, directions[:, 0], charges, present_blocks, left_operators, wavefunction, rotations
    )
    extra_half = over_op(extra, lambda i: (i + half) % n)
    from_side = over_op(first_side, side)
    from_core = over_op(first_core, lambda i: i ^ 1)
    from_half = over_op(first_half, lambda i: (i + half) % n)
    token, (*terms, turned) = sigma_terms(
        token, halving, chunk, charges, present_blocks, left, right_operators, wave, rotations
    )

    if halving:
        send, keep = terms
        got = over_op(send, lambda i: i ^ 1)
        token, (first, second, mid) = edges(token, keep, got, turned)
        one, two = swapped(first, 0), swapped(second, 1)
        offset = width // 2
        token, (from_core,) = hold(token, from_core)
        token, (relayed,) = relay(token, half, extra, extra_half)
        extra_side = over_op(relayed, side_or_across)
        bit = 2
        token, (send, keep) = split(token, bit, chunk, levels, mid, one, two)
        got = over_op(send, lambda i: i ^ 2)
    else:
        (terms,) = terms
        offset = width
        odd = lax.rem(lax.axis_index("sec"), 2) == 1
        level = lax.axis_index("sec")
        upward = jnp.concatenate([terms[sectors + 1].astype(BF16), turned[sectors - 1]])
        downward = jnp.concatenate([terms[0].astype(BF16), turned[0]])
        one = swapped(jnp.where(odd, downward, upward), 0)
        two = swapped(jnp.where(odd, upward, downward), 1)
        below = jnp.where(odd, one, two)[:width].astype(F32)
        above = jnp.where(odd, two, one)[:width].astype(F32)
        mid = terms[1 : sectors + 1]
        mid = mid.at[0].add(jnp.where(level > 0, below, 0.0))
        mid = mid.at[sectors - 1].add(jnp.where(level < levels - 1, above, 0.0))
        summed = lax.psum_scatter(mid, "op", scatter_dimension=1, tiled=True)
        token, (relayed,) = relay(token, half, extra, extra_half)
        extra_side = over_op(relayed, side_or_across)

    fixed = (offset, levels, turned, rotations, one, two)
    token, out = renorm(
        token,
        "renorm_core",
        ((0, 0, "core", 1), (0, rows, "core", 0), (1, 0, 3, 1)),
        (from_core, extra_half),
        None,
        *fixed,
    )
    if halving:
        while 2 * bit < n:
            bit *= 2
            token, (send, keep) = split(token, bit, chunk, levels, keep, got)
            got = over_op(send, lambda i: i ^ bit)
        summed = keep + got.astype(F32)
    token, out = renorm(
        token, "renorm_side", ((0, 0, "side", 0),), (from_side,), out, *fixed
    )
    token, out = renorm(
        token, "renorm_extra", ((0, 0, "side", 1),), (extra_side,), out, *fixed
    )
    token, out = renorm(token, "renorm_half", ((0, 0, 3, 0),), (from_half,), out, *fixed)
    return summed / math.sqrt(pairs * n), out


def solution(mesh):
    placed = (
        P("sec", None, None),
        P("op", "sec", None, None),
        P("op", "sec", None, None),
        P("sec", None, None),
        P("op"),
        P("op", "sec"),
        P("op", None),
    )
    return jax.shard_map(
        body,
        mesh=mesh,
        in_specs=placed,
        out_specs=(P("sec", "op", None), P("op", "sec", None, None)),
        check_vma=False,
    )
```

time: 127 us -> 49.2 us (0.39)
  the two profiles are of different devices: /device:TPU:1 before, /device:TPU:0 now
where the time goes in v2:
time: 49.2 us; the launch traced here: 49 us
  waiting for transfers between devices  24.1 us (49%)
  starting transfers between devices  12.3 us (25%)
  Pallas kernels  11.2 us (23%)
  between operations  0.73 us (1%)
  other arithmetic  0.67 us (1%)
    ppermute x8, waiting for transfers between devices, over_op(): return lax.ppermute(value, 'op', [(i, target(i)) for i in range(n)])  24.1 us
    pallas_call x11, Pallas kernels, kernel_call(): pl.pallas_call(run, grid=grid, out_shape=[jax.ShapeDtypeStruct((8, 128),...  11.2 us
    ppermute x8, starting transfers between devices, over_op(): return lax.ppermute(value, 'op', [(i, target(i)) for i in range(n)])  10 us
    ppermute x2, starting transfers between devices, swapped(): return lax.ppermute(value, 'sec', list(enumerate(to)))  2.3 us
  transfers between devices with their start and end apart: 10, of which 4 were waited for; matrix products, arithmetic and copies ran while one was open for 1% of the time, Pallas kernels for 16%

profile of v2, /device:TPU:0, one launch (start us, length us, event | category | flops | bytes accessed | tf_op | source)
XLA Modules:
  0.0 49.0 jit_solution(14073520960907132480)
XLA Ops:
  0.6 1.9 %stage.1 = (f32[8,128]{1,0:T(8,128)S(1)}, bf16[1040,256]{1,0:T(8,128)(2,1)S(1)}, bf16[1040,256]{1,0:T(8,128)(2,1)S(1)}, bf16[2080,256]{1,0:T(8,128)(2,1)S(1)}, b...) custom-call(s32[4]{0:T(128)} %bitcast.1, ...), custom_call_target="tpu_custom_call" | custom-call | tf_op jit(solution)/shard_map/stage/pallas_call | solution.py:34
  2.5 0.5 %collective-permute-start.1 = (bf16[2080,256]{1,0:T(8,128)(2,1)S(1)}, bf16[2080,256]{1,0:T(8,128)(2,1)S(1)}, u32[]{:S(2)}, u32[]{:S(2)}) collective-permute-start(bf16[2080,256]{1,0:T(8,128)(2,1)S(1)} %get-tuple-element.44), channel_id=1, source_target_pairs={{0,4},{4,0},{8,12},{12,8},{16,20},{20,16},{24,28},{28,24},{1,5},{5... | collective-permute-start | bytes 3194888 | tf_op jit(solution)/shard_map/ppermute | solution.py:438
  3.0 2.6 %collective-permute-start.2 = (bf16[1040,256]{1,0:T(8,128)(2,1)S(1)}, bf16[1040,256]{1,0:T(8,128)(2,1)S(1)}, u32[]{:S(2)}, u32[]{:S(2)}) collective-permute-start(bf16[1040,256]{1,0:T(8,128)(2,1)S(1)} %get-tuple-element.46.refs_1_), channel_id=1, source_target_pairs={{0,16},{4,20},{8,24},{12,28},{16,0},{20,4},{24,8},{28,12},{1,17},{... | collective-permute-start | bytes 1597448 | tf_op jit(solution)/shard_map/ppermute | solution.py:438
  5.6 3.4 %sigma_terms.1 = (f32[8,128]{1,0:T(8,128)S(1)}, bf16[6,128,256]{2,1,0:T(8,128)(2,1)S(1)}, f32[6,128,256]{2,1,0:T(8,128)S(1)}, bf16[4,256,256]{2,1,0:T(8,128)(2,1)S(1)}) custom-call(f32[8,128]{1,0:T(8,128)S(1)} %get-tuple-element.35.refs_0_, s32[4]{0:T(128)} %refs_1_.3, s32[4,4]{1,0:T(4,128)} %refs_2_.3, ...), custom_call_target="tpu_custom_call" | custom-call | tf_op jit(solution)/shard_map/sigma_terms/pallas_call | solution.py:34
  9.0 0.2 collective-permute-start
  9.3 1.4 %collective-permute-start.7 = (bf16[1040,256]{1,0:T(8,128)(2,1)S(1)}, bf16[1040,256]{1,0:T(8,128)(2,1)S(1)}, u32[]{:S(2)}, u32[]{:S(2)}) collective-permute-start(bf16[1040,256]{1,0:T(8,128)(2,1)S(1)} %get-tuple-element.59), channel_id=1, source_target_pairs={{0,28},{4,8},{8,4},{12,16},{16,12},{20,24},{24,20},{28,0},{1,29},{... | collective-permute-start | bytes 1597448 | tf_op jit(solution)/shard_map/ppermute | solution.py:438
  10.6 0.2 collective-permute-done.refs_2_
  10.8 0.1 edges.1
  10.9 1.6 %collective-permute-start.3 = (bf16[384,256]{1,0:T(8,128)(2,1)S(1)}, bf16[384,256]{1,0:T(8,128)(2,1)S(1)}, u32[]{:S(2)}, u32[]{:S(2)}) collective-permute-start(bf16[384,256]{1,0:T(8,128)(2,1)S(1)} %get-tuple-element.49), channel_id=1, source_target_pairs={{0,1},{1,0},{2,3},{3,2},{4,5},{5,4},{6,7},{7,6},{8,9},{9,8},{10,11... | collective-permute-start | bytes 589832 | tf_op jit(solution)/shard_map/ppermute | solution.py:444
  12.5 0.7 %collective-permute-start.4 = (bf16[384,256]{1,0:T(8,128)(2,1)S(1)}, bf16[384,256]{1,0:T(8,128)(2,1)S(1)}, u32[]{:S(2)}, u32[]{:S(2)}) collective-permute-start(bf16[384,256]{1,0:T(8,128)(2,1)S(1)} %get-tuple-element.50), channel_id=1, source_target_pairs={{0,0},{1,2},{2,1},{3,3},{4,4},{5,6},{6,5},{7,7},{8,8},{9,10},{10,9... | collective-permute-start | bytes 589832 | tf_op jit(solution)/shard_map/ppermute | solution.py:444
  13.2 0.0 collective-permute-done.1.refs_1_
  13.2 10.8 %collective-permute-done.2.refs_2_.refs_6_ = bf16[1040,256]{1,0:T(8,128)(2,1)S(1)} collective-permute-done((bf16[1040,256]{1,0:T(8,128)(2,1)S(1)}, bf16[1040,256]{1,0:T(8,128)(2,1)S(1)}, u32[]{:S(2)}, u32[]{:S(2)}) %collective-permute-start.2) | collective-permute-done | bytes 532512 | tf_op jit(solution)/shard_map/ppermute | solution.py:438
  24.1 1.1 %collective-permute-start.8 = (bf16[1040,256]{1,0:T(8,128)(2,1)S(1)}, bf16[1040,256]{1,0:T(8,128)(2,1)S(1)}, u32[]{:S(2)}, u32[]{:S(2)}) collective-permute-start(bf16[1040,256]{1,0:T(8,128)(2,1)S(1)} %get-tuple-element.62), channel_id=1, source_target_pairs={{0,12},{4,8},{8,4},{12,0},{16,28},{20,24},{24,20},{28,16},{1,13},{... | collective-permute-start | bytes 1597448 | tf_op jit(solution)/shard_map/ppermute | solution.py:438
  25.1 1.5 %collective-permute-start.9 = (bf16[1040,256]{1,0:T(8,128)(2,1)S(1)}, bf16[1040,256]{1,0:T(8,128)(2,1)S(1)}, u32[]{:S(2)}, u32[]{:S(2)}) collective-permute-start(bf16[1040,256]{1,0:T(8,128)(2,1)S(1)} %get-tuple-element.65), channel_id=1, source_target_pairs={{0,16},{4,20},{8,24},{12,28},{16,0},{20,4},{24,8},{28,12},{1,17},{... | collective-permute-start | bytes 1597448 | tf_op jit(solution)/shard_map/ppermute | solution.py:438
  26.6 0.0 collective-permute-done.4.refs_3_.refs_4_
  26.7 0.9 %collective-permute-start.5 = (bf16[4,64,256]{2,1,0:T(8,128)(2,1)S(1)}, bf16[4,64,256]{2,1,0:T(8,128)(2,1)S(1)}, u32[]{:S(2)}, u32[]{:S(2)}) collective-permute-start(bf16[4,64,256]{2,1,0:T(8,128)(2,1)S(1)} %get-tuple-element.55), channel_id=1, source_target_pairs={{0,8},{4,12},{8,0},{12,4},{16,24},{20,28},{24,16},{28,20},{1,9},{5... | collective-permute-start | bytes 393224 | tf_op jit(solution)/shard_map/ppermute | solution.py:438
  27.6 1.9 %renorm_core.1 = (f32[8,128]{1,0:T(8,128)S(1)}, bf16[8,4,256,256]{3,2,1,0:T(8,128)(2,1)}) custom-call(f32[8,128]{1,0:T(8,128)S(1)} %get-tuple-element.51.refs_0_, bf16[4,256,256]{2,1,0:T(8,128)(2,1)S(1)} %get-tuple-element.42.refs_3_.refs_1_, bf16[4,256,256]{2,1,0:T(8,128)(2,1)S(1)} %get-tuple-element.38.refs_6_.refs_2_, ...), custom_call_target="tpu_custom_call" | custom-call | flops 805306368 | bytes 5242880 | tf_op jit(solution)/shard_map/renorm_core/pallas_call | solution.py:34
  29.4 11.9 %collective-permute-done.5.refs_2_ = bf16[4,64,256]{2,1,0:T(8,128)(2,1)S(1)} collective-permute-done((bf16[4,64,256]{2,1,0:T(8,128)(2,1)S(1)}, bf16[4,64,256]{2,1,0:T(8,128)(2,1)S(1)}, u32[]{:S(2)}, u32[]{:S(2)}) %collective-permute-start.5) | collective-permute-done | bytes 131104 | tf_op jit(solution)/shard_map/ppermute | solution.py:438
  41.4 1.8 %collective-permute-start.6 = (bf16[4,32,256]{2,1,0:T(8,128)(2,1)S(1)}, bf16[4,32,256]{2,1,0:T(8,128)(2,1)S(1)}, u32[]{:S(2)}, u32[]{:S(2)}) collective-permute-start(bf16[4,32,256]{2,1,0:T(8,128)(2,1)S(1)} %get-tuple-element.57), channel_id=1, source_target_pairs={{0,16},{4,20},{8,24},{12,28},{16,0},{20,4},{24,8},{28,12},{1,17},{... | collective-permute-start | bytes 196616 | tf_op jit(solution)/shard_map/ppermute | solution.py:438
  43.2 1.3 %renorm_side.1 = (f32[8,128]{1,0:T(8,128)S(1)}, bf16[8,4,256,256]{3,2,1,0:T(8,128)(2,1)}) custom-call(f32[8,128]{1,0:T(8,128)S(1)} %get-tuple-element.58.refs_0_, bf16[4,256,256]{2,1,0:T(8,128)(2,1)S(1)} %get-tuple-element.42.refs_3_.refs_1_, bf16[4,256,256]{2,1,0:T(8,128)(2,1)S(1)} %get-tuple-element.38.refs_6_.refs_2_, ...), custom_call_target="tpu_custom_call", output_to_operand_aliasing={{1}: (6, {})} | custom-call | flops 268435456 | bytes 3145728 | tf_op jit(solution)/shard_map/renorm_side/pallas_call | solution.py:34
  44.5 1.2 %collective-permute-done.6 = bf16[4,32,256]{2,1,0:T(8,128)(2,1)S(1)} collective-permute-done((bf16[4,32,256]{2,1,0:T(8,128)(2,1)S(1)}, bf16[4,32,256]{2,1,0:T(8,128)(2,1)S(1)}, u32[]{:S(2)}, u32[]{:S(2)}) %collective-permute-start.6) | collective-permute-done | bytes 65568 | tf_op jit(solution)/shard_map/ppermute | solution.py:438
  45.7 0.7 %add_multiply_fusion = f32[4,32,256]{2,1,0:T(8,128)} fusion(f32[4,32,256]{2,1,0:T(8,128)S(1)} %get-tuple-element.56, bf16[4,32,256]{2,1,0:T(8,128)(2,1)S(1)} %collective-permute-done.6), kind=kLoop, calls=%fused_computation | loop fusion | flops 98304 | bytes 327680 | tf_op jit(solution)/shard_map/div | solution.py:521
  46.4 1.3 %renorm_extra.1 = (f32[8,128]{1,0:T(8,128)S(1)}, bf16[8,4,256,256]{3,2,1,0:T(8,128)(2,1)}) custom-call(f32[8,128]{1,0:T(8,128)S(1)} %get-tuple-element.61.refs_0_, bf16[4,256,256]{2,1,0:T(8,128)(2,1)S(1)} %get-tuple-element.42.refs_3_.refs_1_, bf16[4,256,256]{2,1,0:T(8,128)(2,1)S(1)} %get-tuple-element.38.refs_6_.refs_2_, ...), custom_call_target="tpu_custom_call", output_to_operand_aliasing={{1}: (6, {})} | custom-call | flops 268435456 | bytes 3145728 | tf_op jit(solution)/shard_map/renorm_extra/pallas_call | solution.py:34
  47.7 1.3 %renorm_half.1 = (f32[8,128]{1,0:T(8,128)}, bf16[8,4,256,256]{3,2,1,0:T(8,128)(2,1)}) custom-call(f32[8,128]{1,0:T(8,128)S(1)} %get-tuple-element.64.refs_0_, bf16[4,256,256]{2,1,0:T(8,128)(2,1)S(1)} %get-tuple-element.42.refs_3_.refs_1_, bf16[4,256,256]{2,1,0:T(8,128)(2,1)S(1)} %get-tuple-element.38.refs_6_.refs_2_, ...), custom_call_target="tpu_custom_call", output_to_operand_aliasing={{1}: (6, {})} | custom-call | flops 268435456 | bytes 3145728 | tf_op jit(solution)/shard_map/renorm_half/pallas_call | solution.py:34
  (8 shorter events, 0.1 us)
Async XLA Ops:
  2.5 10.7 %collective-permute-start.1 = (bf16[2080,256]{1,0:T(8,128)(2,1)S(1)}, bf16[2080,256]{1,0:T(8,128)(2,1)S(1)}, u32[]{:S(2)}, u32[]{:S(2)}) collective-permute-start(bf16[2080,256]{1,0:T(8,128)(2,1)S(1)} %get-tuple-element.44), channel_id=1, source_target_pairs={{0,4},{4,0},{8,12},{12,8},{16,20},{20,16},{24,28},{28,24},{1,5},{5... | collective-permute-start | bytes 3194888 | tf_op jit(solution)/shard_map/ppermute | solution.py:438
  3.0 21.0 %collective-permute-start.2 = (bf16[1040,256]{1,0:T(8,128)(2,1)S(1)}, bf16[1040,256]{1,0:T(8,128)(2,1)S(1)}, u32[]{:S(2)}, u32[]{:S(2)}) collective-permute-start(bf16[1040,256]{1,0:T(8,128)(2,1)S(1)} %get-tuple-element.46.refs_1_), channel_id=1, source_target_pairs={{0,16},{4,20},{8,24},{12,28},{16,0},{20,4},{24,8},{28,12},{1,17},{... | collective-permute-start | bytes 1597448 | tf_op jit(solution)/shard_map/ppermute | solution.py:438
  9.0 1.8 %collective-permute-start = (bf16[6,128,256]{2,1,0:T(8,128)(2,1)S(1)}, bf16[6,128,256]{2,1,0:T(8,128)(2,1)S(1)}, u32[]{:S(2)}, u32[]{:S(2)}) collective-permute-start(bf16[6,128,256]{2,1,0:T(8,128)(2,1)S(1)} %get-tuple-element.41), channel_id=1, source_target_pairs={{0,4},{4,0},{8,12},{12,8},{16,20},{20,16},{24,28},{28,24},{1,5},{5... | collective-permute-start | bytes 1179656 | tf_op jit(solution)/shard_map/ppermute | solution.py:438
  9.3 33.9 %collective-permute-start.7 = (bf16[1040,256]{1,0:T(8,128)(2,1)S(1)}, bf16[1040,256]{1,0:T(8,128)(2,1)S(1)}, u32[]{:S(2)}, u32[]{:S(2)}) collective-permute-start(bf16[1040,256]{1,0:T(8,128)(2,1)S(1)} %get-tuple-element.59), channel_id=1, source_target_pairs={{0,28},{4,8},{8,4},{12,16},{16,12},{20,24},{24,20},{28,0},{1,29},{... | collective-permute-start | bytes 1597448 | tf_op jit(solution)/shard_map/ppermute | solution.py:438
  10.9 15.7 %collective-permute-start.3 = (bf16[384,256]{1,0:T(8,128)(2,1)S(1)}, bf16[384,256]{1,0:T(8,128)(2,1)S(1)}, u32[]{:S(2)}, u32[]{:S(2)}) collective-permute-start(bf16[384,256]{1,0:T(8,128)(2,1)S(1)} %get-tuple-element.49), channel_id=1, source_target_pairs={{0,1},{1,0},{2,3},{3,2},{4,5},{5,4},{6,7},{7,6},{8,9},{9,8},{10,11... | collective-permute-start | bytes 589832 | tf_op jit(solution)/shard_map/ppermute | solution.py:444
  12.5 14.1 %collective-permute-start.4 = (bf16[384,256]{1,0:T(8,128)(2,1)S(1)}, bf16[384,256]{1,0:T(8,128)(2,1)S(1)}, u32[]{:S(2)}, u32[]{:S(2)}) collective-permute-start(bf16[384,256]{1,0:T(8,128)(2,1)S(1)} %get-tuple-element.50), channel_id=1, source_target_pairs={{0,0},{1,2},{2,1},{3,3},{4,4},{5,6},{6,5},{7,7},{8,8},{9,10},{10,9... | collective-permute-start | bytes 589832 | tf_op jit(solution)/shard_map/ppermute | solution.py:444
  24.1 22.3 %collective-permute-start.8 = (bf16[1040,256]{1,0:T(8,128)(2,1)S(1)}, bf16[1040,256]{1,0:T(8,128)(2,1)S(1)}, u32[]{:S(2)}, u32[]{:S(2)}) collective-permute-start(bf16[1040,256]{1,0:T(8,128)(2,1)S(1)} %get-tuple-element.62), channel_id=1, source_target_pairs={{0,12},{4,8},{8,4},{12,0},{16,28},{20,24},{24,20},{28,16},{1,13},{... | collective-permute-start | bytes 1597448 | tf_op jit(solution)/shard_map/ppermute | solution.py:438
  25.1 22.6 %collective-permute-start.9 = (bf16[1040,256]{1,0:T(8,128)(2,1)S(1)}, bf16[1040,256]{1,0:T(8,128)(2,1)S(1)}, u32[]{:S(2)}, u32[]{:S(2)}) collective-permute-start(bf16[1040,256]{1,0:T(8,128)(2,1)S(1)} %get-tuple-element.65), channel_id=1, source_target_pairs={{0,16},{4,20},{8,24},{12,28},{16,0},{20,4},{24,8},{28,12},{1,17},{... | collective-permute-start | bytes 1597448 | tf_op jit(solution)/shard_map/ppermute | solution.py:438
  26.7 14.6 %collective-permute-start.5 = (bf16[4,64,256]{2,1,0:T(8,128)(2,1)S(1)}, bf16[4,64,256]{2,1,0:T(8,128)(2,1)S(1)}, u32[]{:S(2)}, u32[]{:S(2)}) collective-permute-start(bf16[4,64,256]{2,1,0:T(8,128)(2,1)S(1)} %get-tuple-element.55), channel_id=1, source_target_pairs={{0,8},{4,12},{8,0},{12,4},{16,24},{20,28},{24,16},{28,20},{1,9},{5... | collective-permute-start | bytes 393224 | tf_op jit(solution)/shard_map/ppermute | solution.py:438
  41.4 4.3 %collective-permute-start.6 = (bf16[4,32,256]{2,1,0:T(8,128)(2,1)S(1)}, bf16[4,32,256]{2,1,0:T(8,128)(2,1)S(1)}, u32[]{:S(2)}, u32[]{:S(2)}) collective-permute-start(bf16[4,32,256]{2,1,0:T(8,128)(2,1)S(1)} %get-tuple-element.57), channel_id=1, source_target_pairs={{0,16},{4,20},{8,24},{12,28},{16,0},{20,4},{24,8},{28,12},{1,17},{... | collective-permute-start | bytes 196616 | tf_op jit(solution)/shard_map/ppermute | solution.py:438

commit v3 on v2

--- a/solution.py
+++ b/solution.py
@@ -49,7 +49,7 @@
 
 
 def estimate(flops, moved):
-    return pl.CostEstimate(flops=flops, bytes_accessed=moved, transcendentals=0)
+    return pl.CostEstimate(flops=0, bytes_accessed=0, transcendentals=0)
 
 
 def fetch_scalars(pairs, sem):
@@ -60,6 +60,11 @@
         copy.wait()
 
 
+def at_end(half):
+    place = lax.rem(lax.axis_index("op"), half)
+    return jnp.logical_or(place == 0, place == half - 1)
+
+
 def pick(kinds, places, kind, place):
     index = jnp.int32(0)
     for p, (own, at) in enumerate(zip(kinds, places)):
@@ -68,7 +73,9 @@
     return index
 
 
-def stage_kernel(roles, directions_ref, charges_ref, present_ref, left_ref, wave_ref, rot_ref, *refs):
+def stage_kernel(
+    roles, half, directions_ref, charges_ref, present_ref, left_ref, wave_ref, rot_ref, *refs
+):
     outs = refs[: len(roles)]
     left, wave, rot, directions, charges, present, few, sems = refs[len(roles) :]
     bulk = [
@@ -90,19 +97,19 @@
             place = place + jnp.where(kinds[q] == kinds[p], 1, 0)
         places.append(place)
     odd = lax.rem(lax.axis_index("op"), 2)
+    end = at_end(half)
+    found = {
+        "extra": pick(kinds, places, None, 1),
+        "half": pick(kinds, places, 3, 0),
+        "core": pick(kinds, places, 1 + odd, 0),
+        "side": pick(kinds, places, 2 - odd, 0),
+    }
     row = lax.broadcasted_iota(jnp.int32, (META, width), 0)
     bulk[0].wait()
     for out, wanted in zip(outs, roles):
         base = 0
         for role in wanted:
-            if role == "extra":
-                index = pick(kinds, places, None, 1)
-            elif role == "half":
-                index = pick(kinds, places, 3, 0)
-            elif role == "core":
-                index = pick(kinds, places, 1 + odd, 0)
-            else:
-                index = pick(kinds, places, 2 - odd, 0)
+            index = found[role] if isinstance(role, str) else jnp.where(end, *map(found.get, role))
             for s in range(sectors):
                 out[base + s * width : base + (s + 1) * width] = left[index, s]
             kind = jnp.int32(0)
@@ -118,13 +125,13 @@
         copy.wait()
 
 
-def staged(roles, directions, charges, present, left, wave, rotations):
+def staged(roles, half, directions, charges, present, left, wave, rotations):
     count, sectors, width, _ = left.shape
     rows = sectors * width + META
     shapes = [(rows * len(wanted), width) for wanted in roles]
     shapes += [left.shape, wave.shape, rotations.shape]
     return kernel_call(
-        functools.partial(stage_kernel, roles),
+        functools.partial(stage_kernel, roles, half),
         None,
         [in_hbm(x) for x in (directions, charges, present, left, wave, rotations)],
         [HBM] * 6,
@@ -179,14 +186,22 @@
     for q in range(width // chunk // 2):
         to = slice(q * chunk, (q + 1) * chunk)
         for t in range(sectors + 2):
-            outs[0][t, to] = acc[t, pl.ds((2 * q + 1 - bit) * chunk, chunk)].astype(BF16)
-            outs[1][t, to] = acc[t, pl.ds((2 * q + bit) * chunk, chunk)]
+            away = acc[t, pl.ds((2 * q + 1 - bit) * chunk, chunk)].astype(BF16)
+            if 0 < t <= sectors:
+                outs[1][t - 1, to] = away
+            else:
+                outs[0][min(t, 1), to] = away
+            outs[2][t, to] = acc[t, pl.ds((2 * q + bit) * chunk, chunk)]
 
 
 def sigma_terms(token, split, chunk, charges, present, left, right, wave, rotations):
     count, sectors, width, _ = left.shape
     if split:
-        shapes = [((sectors + 2, width // 2, width), BF16), ((sectors + 2, width // 2, width), F32)]
+        shapes = [
+            ((2, width // 2, width), BF16),
+            ((sectors, width // 2, width), BF16),
+            ((sectors + 2, width // 2, width), F32),
+        ]
     else:
         shapes = [((sectors + 2, width, width), F32)]
     shapes.append(((sectors, width, width), BF16))
@@ -211,52 +226,45 @@
     )
 
 
-def edges_kernel(keep, got, turned, first, second, mid):
-    height = keep.shape[1]
-    sectors = mid.shape[0]
+def edges_kernel(keep, got, turned, first, second):
+    outer, height, _ = keep.shape
     odd = lax.rem(lax.axis_index("sec"), 2)
     for out, upward in ((first, odd == 0), (second, odd == 1)):
-        edge = jnp.where(upward, sectors + 1, 0)
-        out[:height] = (keep[edge] + got[edge].astype(F32)).astype(BF16)
-        out[height:] = turned[jnp.where(upward, sectors - 1, 0)]
-    for s in range(sectors):
-        mid[s] = keep[s + 1] + got[s + 1].astype(F32)
+        edge = jnp.where(upward, outer - 1, 0)
+        out[:height] = (keep[edge] + got[jnp.where(upward, 1, 0)].astype(F32)).astype(BF16)
+        out[height:] = turned[jnp.where(upward, outer - 3, 0)]
 
 
 def edges(token, keep, got, turned):
-    outer, height, width = keep.shape
-    rows = height + turned.shape[1]
+    _, height, width = keep.shape
+    shape = (height + turned.shape[1], width)
     return kernel_call(
         edges_kernel,
         token,
         (keep, got, turned),
         [VMEM] * 3,
-        [
-            jax.ShapeDtypeStruct((rows, width), BF16),
-            jax.ShapeDtypeStruct((rows, width), BF16),
-            jax.ShapeDtypeStruct((outer - 2, height, width), F32),
-        ],
-        [VMEM] * 3,
-        mib=6,
-        cost_estimate=estimate(keep.size, 12 * keep.size),
+        [jax.ShapeDtypeStruct(shape, BF16)] * 2,
+        [VMEM] * 2,
+        mib=4,
+        cost_estimate=estimate(0, 0),
         name="edges",
     )
 
 
-def split_kernel(bit, chunk, levels, first, *refs):
+def split_kernel(bit, chunk, levels, first, held, *refs):
     if first:
-        mid, one, two, send, keep = refs
+        got, one, two, send, keep = refs
     else:
-        mid, got, send, keep = refs
-    sectors, height, _ = mid.shape
+        got, send, keep = refs
+    sectors, height, _ = got.shape
     own = lax.rem(lax.axis_index("op") // bit, 2)
     level = lax.axis_index("sec")
     odd = lax.rem(level, 2) == 1
 
     def total(s, rows):
-        value = mid[s, rows]
         if not first:
-            return value + got[s, rows].astype(F32)
+            return held[s, rows] + got[s, rows].astype(F32)
+        value = held[s + 1, rows] + got[s, rows].astype(F32)
         if s == 0:
             below = jnp.where(odd, one[rows], two[rows]).astype(F32)
             value = value + jnp.where(level > 0, below, 0.0)
@@ -272,76 +280,82 @@
             keep[s, to] = total(s, pl.ds((2 * q + own) * chunk, chunk))
 
 
-def split(token, bit, chunk, levels, mid, *more):
-    sectors, height, width = mid.shape
-    return kernel_call(
-        functools.partial(split_kernel, bit, chunk, levels, len(more) == 2),
-        token,
-        (mid, *more),
-        [VMEM] * (1 + len(more)),
+def split(token, bit, chunk, levels, held, got, *edge):
+    sectors, height, width = got.shape
+    return kernel_call(
+        functools.partial(split_kernel, bit, chunk, levels, len(edge) == 2),
+        token,
+        (held, got, *edge),
+        [VMEM] * (2 + len(edge)),
         [
             jax.ShapeDtypeStruct((sectors, height // 2, width), BF16),
             jax.ShapeDtypeStruct((sectors, height // 2, width), F32),
         ],
         [VMEM] * 2,
         mib=4,
-        cost_estimate=estimate(mid.size, 10 * mid.size),
+        cost_estimate=estimate(0, 0),
         name="split",
     )
 
 
-def relay_kernel(half, own, other, out):
-    place = lax.rem(lax.axis_index("op"), half)
-    end = jnp.logical_or(place == 0, place == half - 1)
-
-    @pl.when(end)
-    def _():
-        out[...] = other[...]
-
-    @pl.when(jnp.logical_not(end))
-    def _():
-        out[...] = own[...]
-
-
-def relay(token, half, own, other):
-    return kernel_call(
-        functools.partial(relay_kernel, half),
-        token,
-        (own, other),
-        [VMEM] * 2,
-        [jax.ShapeDtypeStruct(own.shape, BF16)],
-        [VMEM],
-        mib=4,
-        cost_estimate=estimate(0, 6 * own.size),
-        name="relay",
-    )
-
-
-def hold_kernel(source, kept):
+def hold_kernel(*refs):
     pass
 
 
-def hold(token, value):
+def hold(token, *values):
     return kernel_call(
         hold_kernel,
         token,
-        (value,),
-        [ANY],
-        [jax.ShapeDtypeStruct(value.shape, value.dtype)],
-        [ANY],
-        aliases={0: 0},
+        values,
+        [ANY] * len(values),
+        [jax.ShapeDtypeStruct(value.shape, value.dtype) for value in values],
+        [ANY] * len(values),
+        aliases={i: i for i in range(len(values))},
         mib=1,
         cost_estimate=estimate(0, 0),
         name="hold",
     )
 
 
-def renorm_kernel(items, zero, offset, levels, turned, rotations, one, two, *refs):
-    buffers = refs[: 1 + max(item[0] for item in items)]
+def choose_kernel(half, first, second, out):
+    end = at_end(half)
+
+    @pl.when(end)
+    def _():
+        out[...] = first[: out.shape[0]]
+
+    @pl.when(jnp.logical_not(end))
+    def _():
+        out[...] = second[...]
+
+
+def choose(token, half, first, second):
+    return kernel_call(
+        functools.partial(choose_kernel, half),
+        token,
+        (first, second),
+        [VMEM] * 2,
+        [pltpu.VMEM(second.shape, BF16)],
+        [VMEM],
+        mib=4,
+        cost_estimate=estimate(0, 0),
+        name="choose",
+    )
+
+
+def renorm_kernel(items, zero, offset, levels, half, scale, turned, rotations, one, two, *refs):
+    if scale is not None:
+        (keep, got), refs = refs[:2], refs[2:]
+    buffers = refs[: 1 + max(buffer for sources, _, _ in items for buffer, _ in sources)]
     rest = refs[len(buffers) + (0 if zero else 1) :]
+    if scale is not None:
+        sigma, rest = rest[1], [rest[0], *rest[2:]]
+        sigma[...] = (keep[...] + got[...].astype(F32)) * scale
     out, edge, results, done = rest
     sectors, width, _ = rotations.shape
-    odd = lax.rem(lax.axis_index("op"), 2)
+    device = lax.axis_index("op")
+    odd = lax.rem(device, 2)
+    end = at_end(half)
     level = lax.axis_index("sec")
     raised = lax.rem(level, 2) == 1
     rows = pl.ds(offset, width)
@@ -354,8 +368,13 @@
             stores.append(copy)
     edge[0] = jnp.where(raised, one[rows], two[rows])
     edge[1] = jnp.where(raised, two[rows], one[rows])
-    for i, (buffer, base, kind, place) in enumerate(items):
-        values = buffers[buffer][pl.ds(base + sectors * width, META)].astype(F32)
+    for i, (sources, kind, place) in enumerate(items):
+
+        def received(at, count):
+            loaded = [buffers[buffer][pl.ds(base + at, count)] for buffer, base in sources]
+            return loaded[0] if len(loaded) == 1 else jnp.where(end, loaded[0], loaded[1])
+
+        values = received(sectors * width, META).astype(F32)
 
         def scalar(row):
             return jnp.max(values[row : row + 1, :])
@@ -374,7 +393,7 @@
             whole = level * sectors + at
             inside = jnp.logical_and(whole >= 0, whole < levels * sectors)
             weight = jnp.where(inside, scalar(2 + s) * wanted, 0.0)
-            block = buffers[buffer][pl.ds(base + s * width, width)]
+            block = received(s * width, width)
             rotated = jnp.dot(block, rotations[s], preferred_element_type=F32).astype(BF16)
             target = turned[jnp.clip(at, 0, sectors - 1)]
             if s == 0:
@@ -390,36 +409,38 @@
         copy.wait()
 
 
-def renorm(token, name, items, buffers, out, offset, levels, turned, rotations, one, two):
+def renorm(
+    token, name, items, buffers, out, offset, levels, half, turned, rotations, one, two, sums=(), scale=None
+):
     sectors, width, _ = rotations.shape
     zero = out is None
-    operands = [turned, rotations, one, two, *buffers]
+    operands = [turned, rotations, one, two, *sums, *buffers]
     in_specs = [VMEM] * len(operands)
     if not zero:
         operands.append(out)
         in_specs.append(HBM)
     count = len(items)
     block = (sectors, width, width)
-    token, (out,) = kernel_call(
-        functools.partial(renorm_kernel, items, zero, offset, levels),
+    return kernel_call(
+        functools.partial(renorm_kernel, items, zero, offset, levels, half, scale),
         token,
         operands,
         in_specs,
-        [jax.ShapeDtypeStruct((DIRS * CAPS, *block), BF16)],
-        [HBM],
+        [jax.ShapeDtypeStruct((DIRS * CAPS, *block), BF16)]
+        + [jax.ShapeDtypeStruct(x.shape, F32) for x in sums[:1]],
+        [HBM] + [VMEM] * len(sums[:1]),
         aliases={} if zero else {len(operands) - 1: 0},
         scratch_shapes=[
             pltpu.VMEM((2, width, width), BF16),
             pltpu.VMEM((count + (1 if zero else 0), *block), BF16),
             pltpu.SemaphoreType.DMA,
         ],
-        mib=12,
-        cost_estimate=estimate(
-            4 * count * sectors * width**3, 4 * (count + 2) * sectors * width * width
+        mib=8,
+        cost_estimate=pl.CostEstimate(
+            flops=8 * count * sectors * width**3 if zero else 0, bytes_accessed=0, transcendentals=0
         ),
         name=name,
     )
-    return token, out
 
 
 def body(
@@ -431,7 +452,7 @@
     levels = lax.axis_size("sec")
     half = n // 2
     chunk = width // n
-    halving = n & (n - 1) == 0 and chunk % 16 == 0
+    halving = n >= 4 and n & (n - 1) == 0 and chunk % 16 == 0
     rows = sectors * width + META
 
     def over_op(value, target):
@@ -446,38 +467,46 @@
     def side(i):
         return (i + 1) % n if i % 2 else (i - 1) % n
 
-    def side_or_across(i):
-        place = i % half
-        if place == half - 1:
-            return i - place
-        if place == 0:
-            return i + half - 1
-        return side(i)
-
-    roles = (("extra",), ("side",), ("extra", "core"), ("half",))
-    token, (extra, first_side, first_core, first_half, left, wave, rotations) = staged(
-        roles, directions[:, 0], charges, present_blocks, left_operators, wavefunction, rotations
-    )
-    extra_half = over_op(extra, lambda i: (i + half) % n)
-    from_side = over_op(first_side, side)
+    def end(i):
+        return i % half in (0, half - 1)
+
+    def opposite(i):
+        return (i + half) % n
+
+    def relay(i):
+        return i - i % half + half - 1 - i % half
+
+    roles = (
+        (("extra", "side"), ("half", "extra")),
+        (("side", "extra"),),
+        ("half",),
+        ("extra", "core"),
+    )
+    token, (ahead, behind, last, first_core, left, wave, turn) = staged(
+        roles, half, directions[:, 0], charges, present_blocks, left_operators, wavefunction, rotations
+    )
+    got_ahead = over_op(ahead, lambda i: opposite(i) if end(i) else side(i))
+    got_behind = over_op(behind, lambda i: side(i) if end(i) else opposite(i))
     from_core = over_op(first_core, lambda i: i ^ 1)
-    from_half = over_op(first_half, lambda i: (i + half) % n)
     token, (*terms, turned) = sigma_terms(
-        token, halving, chunk, charges, present_blocks, left, right_operators, wave, rotations
+        token, halving, chunk, charges, present_blocks, left, right_operators, wave, turn
     )
 
     if halving:
-        send, keep = terms
+        send_edges, send, keep = terms
+        got_edges = over_op(send_edges, lambda i: i ^ 1)
         got = over_op(send, lambda i: i ^ 1)
-        token, (first, second, mid) = edges(token, keep, got, turned)
+        token, (from_core, got) = hold(token, from_core, got)
+        token, (first, second) = edges(token, keep, got_edges, turned)
         one, two = swapped(first, 0), swapped(second, 1)
         offset = width // 2
-        token, (from_core,) = hold(token, from_core)
-        token, (relayed,) = relay(token, half, extra, extra_half)
-        extra_side = over_op(relayed, side_or_across)
         bit = 2
-        token, (send, keep) = split(token, bit, chunk, levels, mid, one, two)
+        token, (send, keep) = split(token, bit, chunk, levels, keep, got, one, two)
         got = over_op(send, lambda i: i ^ 2)
+        while 2 * bit < n:
+            bit *= 2
+            token, (send, keep) = split(token, bit, chunk, levels, keep, got)
+            got = over_op(send, lambda i, bit=bit: i ^ bit)
     else:
         (terms,) = terms
         offset = width
@@ -493,32 +522,37 @@
         mid = mid.at[0].add(jnp.where(level > 0, below, 0.0))
         mid = mid.at[sectors - 1].add(jnp.where(level < levels - 1, above, 0.0))
         summed = lax.psum_scatter(mid, "op", scatter_dimension=1, tiled=True)
-        token, (relayed,) = relay(token, half, extra, extra_half)
-        extra_side = over_op(relayed, side_or_across)
-
-    fixed = (offset, levels, turned, rotations, one, two)
-    token, out = renorm(
-        token,
-        "renorm_core",
-        ((0, 0, "core", 1), (0, rows, "core", 0), (1, 0, 3, 1)),
-        (from_core, extra_half),
+
+    token, (last,) = choose(token, half, got_ahead, last)
+    got_last = over_op(last, lambda i: relay(i) if end(i) else opposite(i))
+    fixed = (offset, levels, half, turned, turn, one, two)
+    token, (out,) = renorm(
+        token,
+        "renorm_first",
+        (
+            (((0, 0),), "core", 1),
+            (((0, rows),), "core", 0),
+            (((2, 0), (1, 0)), "side", 0),
+            (((1, 0), (2, 0)), 3, 1),
+        ),
+        (from_core, got_ahead, got_behind),
         None,
         *fixed,
     )
-    if halving:
-        while 2 * bit < n:
-            bit *= 2
-            token, (send, keep) = split(token, bit, chunk, levels, keep, got)
-            got = over_op(send, lambda i: i ^ bit)
-        summed = keep + got.astype(F32)
-    token, out = renorm(
-        token, "renorm_side", ((0, 0, "side", 0),), (from_side,), out, *fixed
-    )
-    token, out = renorm(
-        token, "renorm_extra", ((0, 0, "side", 1),), (extra_side,), out, *fixed
-    )
-    token, out = renorm(token, "renorm_half", ((0, 0, 3, 0),), (from_half,), out, *fixed)
-    return summed / math.sqrt(pairs * n), out
+    scale = 1.0 / math.sqrt(pairs * n)
+    token, (out, *sigma_vector) = renorm(
+        token,
+        "renorm_last",
+        ((((1, 0), (0, rows)), "side", 1), (((0, rows), (1, 0)), 3, 0)),
+        (got_ahead, got_last),
+        out,
+        *fixed,
+        sums=(keep, got) if halving else (),
+        scale=scale if halving else None,
+    )
+    if not halving:
+        sigma_vector = [summed * scale]
+    return sigma_vector[0], out
 
 
 def solution(mesh):

time: 49.2 us -> 39.3 us (0.80)
  the two profiles are of different devices: /device:TPU:0 before, /device:TPU:1 now
where the time goes in v3:
time: 39.3 us; the launch traced here: 39.1 us
  waiting for transfers between devices  18.3 us (47%)
  starting transfers between devices  10.1 us (26%)
  Pallas kernels  9.95 us (25%)
  between operations  0.7 us (2%)
    ppermute x8, waiting for transfers between devices, over_op(): return lax.ppermute(value, 'op', [(i, target(i)) for i in range(n)])  15.5 us
    pallas_call x9, Pallas kernels, kernel_call(): pl.pallas_call(run, grid=grid, out_shape=[jax.ShapeDtypeStruct((8, 128),...  9.95 us
    ppermute x8, starting transfers between devices, over_op(): return lax.ppermute(value, 'op', [(i, target(i)) for i in range(n)])  8.06 us
    ppermute x2, waiting for transfers between devices, swapped(): return lax.ppermute(value, 'sec', list(enumerate(to)))  2.9 us
    ppermute x2, starting transfers between devices, swapped(): return lax.ppermute(value, 'sec', list(enumerate(to)))  2.02 us
  transfers between devices with their start and end apart: 10, of which 6 were waited for; matrix products, arithmetic and copies ran while one was open for 0% of the time, Pallas kernels for 15%

profile of v3, /device:TPU:1, one launch (start us, length us, event | category | flops | bytes accessed | tf_op | source)
XLA Modules:
  0.0 39.1 jit_solution(5921080083362338419)
XLA Ops:
  0.6 1.9 %stage.1 = (f32[8,128]{1,0:T(8,128)S(1)}, bf16[2080,256]{1,0:T(8,128)(2,1)S(1)}, bf16[1040,256]{1,0:T(8,128)(2,1)S(1)}, bf16[1040,256]{1,0:T(8,128)(2,1)S(1)}, b...) custom-call(s32[4]{0:T(128)} %bitcast.1, ...), custom_call_target="tpu_custom_call" | custom-call | tf_op jit(solution)/shard_map/stage/pallas_call | solution.py:34
  2.5 0.1 collective-permute-start
  2.6 2.6 %collective-permute-start.6 = (bf16[2080,256]{1,0:T(8,128)(2,1)S(1)}, bf16[2080,256]{1,0:T(8,128)(2,1)S(1)}, u32[]{:S(2)}, u32[]{:S(2)}) collective-permute-start(bf16[2080,256]{1,0:T(8,128)(2,1)S(1)} %get-tuple-element.52), channel_id=1, source_target_pairs={{0,16},{4,8},{8,4},{12,28},{16,0},{20,24},{24,20},{28,12},{1,17},{... | collective-permute-start | bytes 3194888 | tf_op jit(solution)/shard_map/ppermute | solution.py:459
  5.3 3.4 %sigma_terms.1 = (f32[8,128]{1,0:T(8,128)S(1)}, bf16[2,128,256]{2,1,0:T(8,128)(2,1)S(1)}, bf16[4,128,256]{2,1,0:T(8,128)(2,1)S(1)}, f32[6,128,256]{2,1,0:T(8,128)S(1)}, bf16[4,256,256]{2,1,0:T(8,128)(2,1)S(1)}) custom-call(f32[8,128]{1,0:T(8,128)S(1)} %get-tuple-element.33.refs_0_, s32[4]{0:T(128)} %refs_1_.3, s32[4,4]{1,0:T(4,128)} %refs_2_.3, ...), custom_call_target="tpu_custom_call" | custom-call | tf_op jit(solution)/shard_map/sigma_terms/pallas_call | solution.py:34
  8.6 0.5 %collective-permute-start.1 = (bf16[4,128,256]{2,1,0:T(8,128)(2,1)S(1)}, bf16[4,128,256]{2,1,0:T(8,128)(2,1)S(1)}, u32[]{:S(2)}, u32[]{:S(2)}) collective-permute-start(bf16[4,128,256]{2,1,0:T(8,128)(2,1)S(1)} %get-tuple-element.39), channel_id=1, source_target_pairs={{0,4},{4,0},{8,12},{12,8},{16,20},{20,16},{24,28},{28,24},{1,5},{5... | collective-permute-start | bytes 786440 | tf_op jit(solution)/shard_map/ppermute | solution.py:459
  9.1 0.1 collective-permute-start.2
  9.2 1.1 %collective-permute-done.1.refs_2_ = bf16[4,128,256]{2,1,0:T(8,128)(2,1)S(1)} collective-permute-done((bf16[4,128,256]{2,1,0:T(8,128)(2,1)S(1)}, bf16[4,128,256]{2,1,0:T(8,128)(2,1)S(1)}, u32[]{:S(2)}, u32[]{:S(2)}) %collective-permute-start.1) | collective-permute-done | bytes 262176 | tf_op jit(solution)/shard_map/ppermute | solution.py:459
  10.3 0.0 collective-permute-done.refs_1_
  10.3 0.2 collective-permute-done.2.refs_2_
  10.5 1.4 %collective-permute-start.3 = (bf16[384,256]{1,0:T(8,128)(2,1)S(1)}, bf16[384,256]{1,0:T(8,128)(2,1)S(1)}, u32[]{:S(2)}, u32[]{:S(2)}) collective-permute-start(bf16[384,256]{1,0:T(8,128)(2,1)S(1)} %get-tuple-element.46), channel_id=1, source_target_pairs={{0,1},{1,0},{2,3},{3,2},{4,5},{5,4},{6,7},{7,6},{8,9},{9,8},{10,11... | collective-permute-start | bytes 589832 | tf_op jit(solution)/shard_map/ppermute | solution.py:465
  11.9 0.7 %collective-permute-start.4 = (bf16[384,256]{1,0:T(8,128)(2,1)S(1)}, bf16[384,256]{1,0:T(8,128)(2,1)S(1)}, u32[]{:S(2)}, u32[]{:S(2)}) collective-permute-start(bf16[384,256]{1,0:T(8,128)(2,1)S(1)} %get-tuple-element.47), channel_id=1, source_target_pairs={{0,0},{1,2},{2,1},{3,3},{4,4},{5,6},{6,5},{7,7},{8,8},{9,10},{10,9... | collective-permute-start | bytes 589832 | tf_op jit(solution)/shard_map/ppermute | solution.py:465
  12.6 1.3 %collective-permute-start.7 = (bf16[1040,256]{1,0:T(8,128)(2,1)S(1)}, bf16[1040,256]{1,0:T(8,128)(2,1)S(1)}, u32[]{:S(2)}, u32[]{:S(2)}) collective-permute-start(bf16[1040,256]{1,0:T(8,128)(2,1)S(1)} %get-tuple-element.56), channel_id=1, source_target_pairs={{0,28},{4,20},{8,24},{12,16},{16,12},{20,4},{24,8},{28,0},{1,29},{... | collective-permute-start | bytes 1597448 | tf_op jit(solution)/shard_map/ppermute | solution.py:459
  13.8 2.9 %collective-permute-done.3.refs_3_ = bf16[384,256]{1,0:T(8,128)(2,1)S(1)} collective-permute-done((bf16[384,256]{1,0:T(8,128)(2,1)S(1)}, bf16[384,256]{1,0:T(8,128)(2,1)S(1)}, u32[]{:S(2)}, u32[]{:S(2)}) %collective-permute-start.3) | collective-permute-done | bytes 196640 | tf_op jit(solution)/shard_map/ppermute | solution.py:465
  16.7 0.1 split.2
  16.8 1.5 %collective-permute-start.5 = (bf16[4,64,256]{2,1,0:T(8,128)(2,1)S(1)}, bf16[4,64,256]{2,1,0:T(8,128)(2,1)S(1)}, u32[]{:S(2)}, u32[]{:S(2)}) collective-permute-start(bf16[4,64,256]{2,1,0:T(8,128)(2,1)S(1)} %get-tuple-element.50), channel_id=1, source_target_pairs={{0,8},{4,12},{8,0},{12,4},{16,24},{20,28},{24,16},{28,20},{1,9},{5... | collective-permute-start | bytes 393224 | tf_op jit(solution)/shard_map/ppermute | solution.py:459
  18.4 8.4 %collective-permute-done.5.refs_2_ = bf16[4,64,256]{2,1,0:T(8,128)(2,1)S(1)} collective-permute-done((bf16[4,64,256]{2,1,0:T(8,128)(2,1)S(1)}, bf16[4,64,256]{2,1,0:T(8,128)(2,1)S(1)}, u32[]{:S(2)}, u32[]{:S(2)}) %collective-permute-start.5) | collective-permute-done | bytes 131104 | tf_op jit(solution)/shard_map/ppermute | solution.py:459
  26.8 0.1 choose.1
  26.9 1.9 %collective-permute-start.9 = (bf16[1040,256]{1,0:T(8,128)(2,1)S(1)}, bf16[1040,256]{1,0:T(8,128)(2,1)S(1)}, u32[]{:S(2)}, u32[]{:S(2)}) collective-permute-start(bf16[1040,256]{1,0:T(8,128)(2,1)S(1)} %get-tuple-element.60), channel_id=1, source_target_pairs={{0,12},{4,20},{8,24},{12,0},{16,28},{20,4},{24,8},{28,16},{1,13},{... | collective-permute-start | bytes 1597448 | tf_op jit(solution)/shard_map/ppermute | solution.py:459
  28.7 0.1 collective-permute-start.8
  28.8 0.5 %collective-permute-done.7.refs_7_ = bf16[1040,256]{1,0:T(8,128)(2,1)S(1)} collective-permute-done((bf16[1040,256]{1,0:T(8,128)(2,1)S(1)}, bf16[1040,256]{1,0:T(8,128)(2,1)S(1)}, u32[]{:S(2)}, u32[]{:S(2)}) %collective-permute-start.7) | collective-permute-done | bytes 532512 | tf_op jit(solution)/shard_map/ppermute | solution.py:459
  29.4 2.2 %renorm_first.1 = (f32[8,128]{1,0:T(8,128)S(1)}, bf16[8,4,256,256]{3,2,1,0:T(8,128)(2,1)}) custom-call(f32[8,128]{1,0:T(8,128)S(1)} %get-tuple-element.54.refs_0_, bf16[4,256,256]{2,1,0:T(8,128)(2,1)S(1)} %get-tuple-element.43.refs_3_.refs_1_, bf16[4,256,256]{2,1,0:T(8,128)(2,1)S(1)} %get-tuple-element.36.refs_6_.refs_2_, ...), custom_call_target="tpu_custom_call" | custom-call | flops 2147483648 | tf_op jit(solution)/shard_map/renorm_first/pallas_call | solution.py:34
  31.6 5.2 %collective-permute-done.8.refs_6_ = bf16[4,32,256]{2,1,0:T(8,128)(2,1)S(1)} collective-permute-done((bf16[4,32,256]{2,1,0:T(8,128)(2,1)S(1)}, bf16[4,32,256]{2,1,0:T(8,128)(2,1)S(1)}, u32[]{:S(2)}, u32[]{:S(2)}) %collective-permute-start.8) | collective-permute-done | bytes 65568 | tf_op jit(solution)/shard_map/ppermute | solution.py:459
  36.8 0.0 collective-permute-done.9.refs_8_
  36.8 2.3 %renorm_last.1 = (f32[8,128]{1,0:T(8,128)}, bf16[8,4,256,256]{3,2,1,0:T(8,128)(2,1)}, f32[4,32,256]{2,1,0:T(8,128)}) custom-call(f32[8,128]{1,0:T(8,128)S(1)} %get-tuple-element.57.refs_0_, bf16[4,256,256]{2,1,0:T(8,128)(2,1)S(1)} %get-tuple-element.43.refs_3_.refs_1_, ...), custom_call_target="tpu_custom_call", output_to_operand_aliasing={{1}: (9, {})} | custom-call | tf_op jit(solution)/shard_map/renorm_last/pallas_call | solution.py:34
  (5 shorter events, 0.1 us)
Async XLA Ops:
  2.5 7.8 %collective-permute-start = (bf16[2080,256]{1,0:T(8,128)(2,1)S(1)}, bf16[2080,256]{1,0:T(8,128)(2,1)S(1)}, u32[]{:S(2)}, u32[]{:S(2)}) collective-permute-start(bf16[2080,256]{1,0:T(8,128)(2,1)S(1)} %get-tuple-element.38), channel_id=1, source_target_pairs={{0,4},{4,0},{8,12},{12,8},{16,20},{20,16},{24,28},{28,24},{1,5},{5... | collective-permute-start | bytes 3194888 | tf_op jit(solution)/shard_map/ppermute | solution.py:459
  2.6 24.2 %collective-permute-start.6 = (bf16[2080,256]{1,0:T(8,128)(2,1)S(1)}, bf16[2080,256]{1,0:T(8,128)(2,1)S(1)}, u32[]{:S(2)}, u32[]{:S(2)}) collective-permute-start(bf16[2080,256]{1,0:T(8,128)(2,1)S(1)} %get-tuple-element.52), channel_id=1, source_target_pairs={{0,16},{4,8},{8,4},{12,28},{16,0},{20,24},{24,20},{28,12},{1,17},{... | collective-permute-start | bytes 3194888 | tf_op jit(solution)/shard_map/ppermute | solution.py:459
  8.6 1.7 %collective-permute-start.1 = (bf16[4,128,256]{2,1,0:T(8,128)(2,1)S(1)}, bf16[4,128,256]{2,1,0:T(8,128)(2,1)S(1)}, u32[]{:S(2)}, u32[]{:S(2)}) collective-permute-start(bf16[4,128,256]{2,1,0:T(8,128)(2,1)S(1)} %get-tuple-element.39), channel_id=1, source_target_pairs={{0,4},{4,0},{8,12},{12,8},{16,20},{20,16},{24,28},{28,24},{1,5},{5... | collective-permute-start | bytes 786440 | tf_op jit(solution)/shard_map/ppermute | solution.py:459
  9.1 1.3 %collective-permute-start.2 = (bf16[2,128,256]{2,1,0:T(8,128)(2,1)S(1)}, bf16[2,128,256]{2,1,0:T(8,128)(2,1)S(1)}, u32[]{:S(2)}, u32[]{:S(2)}) collective-permute-start(bf16[2,128,256]{2,1,0:T(8,128)(2,1)S(1)} %get-tuple-element.42), channel_id=1, source_target_pairs={{0,4},{4,0},{8,12},{12,8},{16,20},{20,16},{24,28},{28,24},{1,5},{5... | collective-permute-start | bytes 393224 | tf_op jit(solution)/shard_map/ppermute | solution.py:459
  10.5 6.2 %collective-permute-start.3 = (bf16[384,256]{1,0:T(8,128)(2,1)S(1)}, bf16[384,256]{1,0:T(8,128)(2,1)S(1)}, u32[]{:S(2)}, u32[]{:S(2)}) collective-permute-start(bf16[384,256]{1,0:T(8,128)(2,1)S(1)} %get-tuple-element.46), channel_id=1, source_target_pairs={{0,1},{1,0},{2,3},{3,2},{4,5},{5,4},{6,7},{7,6},{8,9},{9,8},{10,11... | collective-permute-start | bytes 589832 | tf_op jit(solution)/shard_map/ppermute | solution.py:465
  11.9 4.8 %collective-permute-start.4 = (bf16[384,256]{1,0:T(8,128)(2,1)S(1)}, bf16[384,256]{1,0:T(8,128)(2,1)S(1)}, u32[]{:S(2)}, u32[]{:S(2)}) collective-permute-start(bf16[384,256]{1,0:T(8,128)(2,1)S(1)} %get-tuple-element.47), channel_id=1, source_target_pairs={{0,0},{1,2},{2,1},{3,3},{4,4},{5,6},{6,5},{7,7},{8,8},{9,10},{10,9... | collective-permute-start | bytes 589832 | tf_op jit(solution)/shard_map/ppermute | solution.py:465
  12.6 16.8 %collective-permute-start.7 = (bf16[1040,256]{1,0:T(8,128)(2,1)S(1)}, bf16[1040,256]{1,0:T(8,128)(2,1)S(1)}, u32[]{:S(2)}, u32[]{:S(2)}) collective-permute-start(bf16[1040,256]{1,0:T(8,128)(2,1)S(1)} %get-tuple-element.56), channel_id=1, source_target_pairs={{0,28},{4,20},{8,24},{12,16},{16,12},{20,4},{24,8},{28,0},{1,29},{... | collective-permute-start | bytes 1597448 | tf_op jit(solution)/shard_map/ppermute | solution.py:459
  16.8 10.0 %collective-permute-start.5 = (bf16[4,64,256]{2,1,0:T(8,128)(2,1)S(1)}, bf16[4,64,256]{2,1,0:T(8,128)(2,1)S(1)}, u32[]{:S(2)}, u32[]{:S(2)}) collective-permute-start(bf16[4,64,256]{2,1,0:T(8,128)(2,1)S(1)} %get-tuple-element.50), channel_id=1, source_target_pairs={{0,8},{4,12},{8,0},{12,4},{16,24},{20,28},{24,16},{28,20},{1,9},{5... | collective-permute-start | bytes 393224 | tf_op jit(solution)/shard_map/ppermute | solution.py:459
  26.9 9.9 %collective-permute-start.9 = (bf16[1040,256]{1,0:T(8,128)(2,1)S(1)}, bf16[1040,256]{1,0:T(8,128)(2,1)S(1)}, u32[]{:S(2)}, u32[]{:S(2)}) collective-permute-start(bf16[1040,256]{1,0:T(8,128)(2,1)S(1)} %get-tuple-element.60), channel_id=1, source_target_pairs={{0,12},{4,20},{8,24},{12,0},{16,28},{20,4},{24,8},{28,16},{1,13},{... | collective-permute-start | bytes 1597448 | tf_op jit(solution)/shard_map/ppermute | solution.py:459
  28.7 8.1 %collective-permute-start.8 = (bf16[4,32,256]{2,1,0:T(8,128)(2,1)S(1)}, bf16[4,32,256]{2,1,0:T(8,128)(2,1)S(1)}, u32[]{:S(2)}, u32[]{:S(2)}) collective-permute-start(bf16[4,32,256]{2,1,0:T(8,128)(2,1)S(1)} %get-tuple-element.59), channel_id=1, source_target_pairs={{0,16},{4,20},{8,24},{12,28},{16,0},{20,4},{24,8},{28,12},{1,17},{... | collective-permute-start | bytes 196616 | tf_op jit(solution)/shard_map/ppermute | solution.py:459

commit v4 on v3

--- a/solution.py
+++ b/solution.py
@@ -73,22 +73,8 @@
     return index
 
 
-def stage_kernel(
-    roles, half, directions_ref, charges_ref, present_ref, left_ref, wave_ref, rot_ref, *refs
-):
-    outs = refs[: len(roles)]
-    left, wave, rot, directions, charges, present, few, sems = refs[len(roles) :]
-    bulk = [
-        pltpu.make_async_copy(left_ref, left, sems.at[0]),
-        pltpu.make_async_copy(wave_ref, wave, sems.at[1]),
-        pltpu.make_async_copy(rot_ref, rot, sems.at[2]),
-    ]
-    for copy in bulk:
-        copy.start()
-    fetch_scalars(
-        [(directions_ref, directions), (charges_ref, charges), (present_ref, present)], few
-    )
-    count, sectors, width, _ = left_ref.shape
+def copy_pairs(roles, half, outs, left, directions, charges, present):
+    count, sectors, width, _ = left.shape
     kinds = [directions[p] for p in range(count)]
     places = []
     for p in range(count):
@@ -105,7 +91,6 @@
         "side": pick(kinds, places, 2 - odd, 0),
     }
     row = lax.broadcasted_iota(jnp.int32, (META, width), 0)
-    bulk[0].wait()
     for out, wanted in zip(outs, roles):
         base = 0
         for role in wanted:
@@ -121,20 +106,52 @@
             base += sectors * width
             out[base : base + META] = values.astype(F32).astype(BF16)
             base += META
-    for copy in bulk[1:]:
+
+
+def stage_kernel(roles, half, directions_ref, charges_ref, present_ref, left_ref, *refs):
+    outs = refs[: len(roles)]
+    left, directions, charges, present, few, sem = refs[len(roles) :]
+    bulk = pltpu.make_async_copy(left_ref, left, sem)
+    bulk.start()
+    fetch_scalars(
+        [(directions_ref, directions), (charges_ref, charges), (present_ref, present)], few
+    )
+    bulk.wait()
+    copy_pairs(roles, half, outs, left, directions, charges, present)
+
+
+def restage_kernel(
+    roles, half, directions_ref, charges_ref, present_ref, left, wave_ref, rot_ref, *refs
+):
+    outs = refs[: len(roles)]
+    wave, rot, directions, charges, present, few, sems = refs[len(roles) :]
+    bulk = [
+        pltpu.make_async_copy(wave_ref, wave, sems.at[0]),
+        pltpu.make_async_copy(rot_ref, rot, sems.at[1]),
+    ]
+    for copy in bulk:
+        copy.start()
+    fetch_scalars(
+        [(directions_ref, directions), (charges_ref, charges), (present_ref, present)], few
+    )
+    copy_pairs(roles, half, outs, left, directions, charges, present)
+    for copy in bulk:
         copy.wait()
 
 
-def staged(roles, half, directions, charges, present, left, wave, rotations):
+def staged(token, roles, half, directions, charges, present, left, *more):
     count, sectors, width, _ = left.shape
     rows = sectors * width + META
+    parts = [(0, sectors // 2), (sectors // 2, sectors)] if sectors > 1 else [(0, 1)]
     shapes = [(rows * len(wanted), width) for wanted in roles]
-    shapes += [left.shape, wave.shape, rotations.shape]
+    shapes += [x.shape for x in more] if more else [left.shape]
+    operands = [in_hbm(x) for x in (directions, charges, present)]
+    operands += [left, *map(in_hbm, more)] if more else [in_hbm(left)]
     return kernel_call(
-        functools.partial(stage_kernel, roles, half),
-        None,
-        [in_hbm(x) for x in (directions, charges, present, left, wave, rotations)],
-        [HBM] * 6,
+        functools.partial(restage_kernel if more else stage_kernel, roles, half),
+        token,
+        operands,
+        [HBM] * 3 + ([VMEM] + [HBM] * len(more) if more else [HBM]),
         [pltpu.VMEM(shape, BF16) for shape in shapes],
         [VMEM] * len(shapes),
         scratch_shapes=[
@@ -142,11 +159,11 @@
             pltpu.SMEM((count,), jnp.int32),
             pltpu.SMEM((count, sectors), jnp.int32),
             pltpu.SemaphoreType.DMA,
-            pltpu.SemaphoreType.DMA((3,)),
+            pltpu.SemaphoreType.DMA((len(more),)) if more else pltpu.SemaphoreType.DMA,
         ],
         mib=4,
         cost_estimate=estimate(0, 0),
-        name="stage",
+        name="restage" if more else "stage",
     )
 
 
@@ -293,7 +310,7 @@
         ],
         [VMEM] * 2,
         mib=4,
-        cost_estimate=estimate(0, 0),
+        cost_estimate=pl.CostEstimate(flops=0 if edge else 2000000000, bytes_accessed=0, transcendentals=0),
         name="split",
     )
 
@@ -302,7 +319,7 @@
     pass
 
 
-def hold(token, *values):
+def hold(token, *values, cost=0):
     return kernel_call(
         hold_kernel,
         token,
@@ -312,31 +329,42 @@
         [ANY] * len(values),
         aliases={i: i for i in range(len(values))},
         mib=1,
-        cost_estimate=estimate(0, 0),
+        cost_estimate=pl.CostEstimate(flops=cost, bytes_accessed=0, transcendentals=0),
         name="hold",
     )
 
 
-def choose_kernel(half, first, second, out):
+def choose_kernel(half, cuts, first, second, *outs):
     end = at_end(half)
+
+    def fill(source):
+        for out, (at, size) in zip(outs, cuts):
+            out[:size] = source[at : at + size]
+            if out.shape[0] > size:
+                out[size:] = source[second.shape[0] - META : second.shape[0]]
 
     @pl.when(end)
     def _():
-        out[...] = first[: out.shape[0]]
+        fill(first)
 
     @pl.when(jnp.logical_not(end))
     def _():
-        out[...] = second[...]
-
-
-def choose(token, half, first, second):
+        fill(second)
+
+
+def choose(token, half, parts, first, second):
+    width = second.shape[1]
+    cuts = [(begin * width, (stop - begin) * width) for begin, stop in parts]
     return kernel_call(
-        functools.partial(choose_kernel, half),
+        functools.partial(choose_kernel, half, cuts),
         token,
         (first, second),
         [VMEM] * 2,
-        [pltpu.VMEM(second.shape, BF16)],
-        [VMEM],
+        [
+            pltpu.VMEM((size + (META if i == 0 else 0), width), BF16)
+            for i, (_, size) in enumerate(cuts)
+        ],
+        [VMEM] * len(cuts),
         mib=4,
         cost_estimate=estimate(0, 0),
         name="choose",
@@ -346,11 +374,11 @@
 def renorm_kernel(items, zero, offset, levels, half, scale, turned, rotations, one, two, *refs):
     if scale is not None:
         (keep, got), refs = refs[:2], refs[2:]
-    buffers = refs[: 1 + max(buffer for sources, _, _ in items for buffer, _ in sources)]
+    buffers = refs[: 1 + max(max(source[::2]) for item in items for source in item[0])]
     rest = refs[len(buffers) + (0 if zero else 1) :]
     if scale is not None:
-        sigma, rest = rest[1], [rest[0], *rest[2:]]
-        sigma[...] = (keep[...] + got[...].astype(F32)) * scale
+        sigma, *rest, total = [rest[1], rest[0], *rest[2:]]
+        total[...] = (keep[...] + got[...].astype(F32)) * scale
     out, edge, results, done = rest
     sectors, width, _ = rotations.shape
     device = lax.axis_index("op")
@@ -360,6 +388,10 @@
     raised = lax.rem(level, 2) == 1
     rows = pl.ds(offset, width)
     stores = []
+    if scale is not None:
+        copy = pltpu.make_async_copy(total, sigma, done)
+        copy.start()
+        stores.append(copy)
     if zero:
         results[len(items)] = jnp.zeros_like(results[len(items)])
         for place in range(CAPS):
@@ -368,13 +400,13 @@
             stores.append(copy)
     edge[0] = jnp.where(raised, one[rows], two[rows])
     edge[1] = jnp.where(raised, two[rows], one[rows])
-    for i, (sources, kind, place) in enumerate(items):
-
-        def received(at, count):
-            loaded = [buffers[buffer][pl.ds(base + at, count)] for buffer, base in sources]
+    for i, (sources, kind, place, begin, stop) in enumerate(items):
+
+        def received(places, count):
+            loaded = [buffers[buffer][pl.ds(at, count)] for buffer, at in places]
             return loaded[0] if len(loaded) == 1 else jnp.where(end, loaded[0], loaded[1])
 
-        values = received(sectors * width, META).astype(F32)
+        values = received([source[2:] for source in sources], META).astype(F32)
 
         def scalar(row):
             return jnp.max(values[row : row + 1, :])
@@ -388,12 +420,12 @@
             wanted = jnp.where(scalar(1).astype(jnp.int32) == kind, 1.0, 0.0)
         else:
             wanted = jnp.float32(1.0)
-        for s in range(sectors):
+        for s in range(begin, stop):
             at = s + charge
             whole = level * sectors + at
             inside = jnp.logical_and(whole >= 0, whole < levels * sectors)
             weight = jnp.where(inside, scalar(2 + s) * wanted, 0.0)
-            block = received(s * width, width)
+            block = received([(x[0], x[1] + (s - begin) * width) for x in sources], width)
             rotated = jnp.dot(block, rotations[s], preferred_element_type=F32).astype(BF16)
             target = turned[jnp.clip(at, 0, sectors - 1)]
             if s == 0:
@@ -410,7 +442,7 @@
 
 
 def renorm(
-    token, name, items, buffers, out, offset, levels, half, turned, rotations, one, two, sums=(), scale=None
+    token, name, items, buffers, out, offset, levels, half, turned, rotations, one, two, sums=(), scale=None, cost=0
 ):
     sectors, width, _ = rotations.shape
     zero = out is None
@@ -428,16 +460,17 @@
         in_specs,
         [jax.ShapeDtypeStruct((DIRS * CAPS, *block), BF16)]
         + [jax.ShapeDtypeStruct(x.shape, F32) for x in sums[:1]],
-        [HBM] + [VMEM] * len(sums[:1]),
+        [HBM] * (1 + len(sums[:1])),
         aliases={} if zero else {len(operands) - 1: 0},
         scratch_shapes=[
             pltpu.VMEM((2, width, width), BF16),
             pltpu.VMEM((count + (1 if zero else 0), *block), BF16),
             pltpu.SemaphoreType.DMA,
+            *[pltpu.VMEM(x.shape, F32) for x in sums[:1]],
         ],
         mib=8,
         cost_estimate=pl.CostEstimate(
-            flops=8 * count * sectors * width**3 if zero else 0, bytes_accessed=0, transcendentals=0
+            flops=cost, bytes_accessed=0, transcendentals=0
         ),
         name=name,
     )
@@ -454,6 +487,7 @@
     chunk = width // n
     halving = n >= 4 and n & (n - 1) == 0 and chunk % 16 == 0
     rows = sectors * width + META
+    parts = [(0, sectors // 2), (sectors // 2, sectors)] if sectors > 1 else [(0, 1)]
 
     def over_op(value, target):
         return lax.ppermute(value, "op", [(i, target(i)) for i in range(n)])
@@ -476,14 +510,18 @@
     def relay(i):
         return i - i % half + half - 1 - i % half
 
-    roles = (
-        (("extra", "side"), ("half", "extra")),
-        (("side", "extra"),),
-        ("half",),
-        ("extra", "core"),
-    )
-    token, (ahead, behind, last, first_core, left, wave, turn) = staged(
-        roles, half, directions[:, 0], charges, present_blocks, left_operators, wavefunction, rotations
+    small = (directions[:, 0], charges, present_blocks)
+    token, (ahead, left) = staged(
+        None, ((("extra", "side"), ("half", "extra")),), half, *small, left_operators
+    )
+    token, (behind, last, first_core, wave, turn) = staged(
+        token,
+        ((("side", "extra"),), ("half",), ("extra", "core")),
+        half,
+        *small,
+        left,
+        wavefunction,
+        rotations,
     )
     got_ahead = over_op(ahead, lambda i: opposite(i) if end(i) else side(i))
     got_behind = over_op(behind, lambda i: side(i) if end(i) else opposite(i))
@@ -496,13 +534,15 @@
         send_edges, send, keep = terms
         got_edges = over_op(send_edges, lambda i: i ^ 1)
         got = over_op(send, lambda i: i ^ 1)
-        token, (from_core, got) = hold(token, from_core, got)
+        token, (got,) = hold(token, got)
         token, (first, second) = edges(token, keep, got_edges, turned)
         one, two = swapped(first, 0), swapped(second, 1)
         offset = width // 2
+        token, (one,) = hold(token, one, cost=1200000000)
         bit = 2
         token, (send, keep) = split(token, bit, chunk, levels, keep, got, one, two)
         got = over_op(send, lambda i: i ^ 2)
+        token, last = choose(token, half, parts, got_ahead, last)
         while 2 * bit < n:
             bit *= 2
             token, (send, keep) = split(token, bit, chunk, levels, keep, got)
@@ -522,37 +562,58 @@
         mid = mid.at[0].add(jnp.where(level > 0, below, 0.0))
         mid = mid.at[sectors - 1].add(jnp.where(level < levels - 1, above, 0.0))
         summed = lax.psum_scatter(mid, "op", scatter_dimension=1, tiled=True)
-
-    token, (last,) = choose(token, half, got_ahead, last)
-    got_last = over_op(last, lambda i: relay(i) if end(i) else opposite(i))
+        token, last = choose(token, half, parts, got_ahead, last)
+
+    if len(last) > 1:
+        token, last[1:] = hold(token, *last[1:])
+    got_last = [over_op(x, lambda i: relay(i) if end(i) else opposite(i)) for x in last]
     fixed = (offset, levels, half, turned, turn, one, two)
+    meta = sectors * width
+    whole = (0, sectors)
     token, (out,) = renorm(
         token,
         "renorm_first",
         (
-            (((0, 0),), "core", 1),
-            (((0, rows),), "core", 0),
-            (((2, 0), (1, 0)), "side", 0),
-            (((1, 0), (2, 0)), 3, 1),
+            (((0, 0, 0, meta),), "core", 1, *whole),
+            (((0, rows, 0, rows + meta),), "core", 0, *whole),
+            (((2, 0, 2, meta), (1, 0, 1, meta)), "side", 0, *whole),
+            (((1, 0, 1, meta), (2, 0, 2, meta)), 3, 1, *whole),
         ),
         (from_core, got_ahead, got_behind),
         None,
         *fixed,
+        cost=2100000000,
     )
     scale = 1.0 / math.sqrt(pairs * n)
-    token, (out, *sigma_vector) = renorm(
-        token,
-        "renorm_last",
-        ((((1, 0), (0, rows)), "side", 1), (((0, rows), (1, 0)), 3, 0)),
-        (got_ahead, got_last),
-        out,
-        *fixed,
-        sums=(keep, got) if halving else (),
-        scale=scale if halving else None,
-    )
+    for i, (begin, stop) in enumerate(parts):
+        final = i == len(parts) - 1
+        piece = begin * width
+        behind_first = (parts[0][1] - parts[0][0]) * width
+        token, (out, *sums) = renorm(
+            token,
+            "renorm_last",
+            (
+                (
+                    ((1, 0, 2, behind_first), (0, rows + piece, 0, rows + meta)),
+                    "side",
+                    1,
+                    begin,
+                    stop,
+                ),
+                (((0, rows + piece, 0, rows + meta), (1, 0, 2, behind_first)), 3, 0, begin, stop),
+            ),
+            (got_ahead, got_last[i], got_last[0]),
+            out,
+            *fixed,
+            sums=(keep, got) if halving and i == 0 else (),
+            scale=scale if halving and i == 0 else None,
+            cost=0 if final else 2000000000,
+        )
+        if sums:
+            (sigma_vector,) = sums
     if not halving:
-        sigma_vector = [summed * scale]
-    return sigma_vector[0], out
+        sigma_vector = summed * scale
+    return sigma_vector, out
 
 
 def solution(mesh):

time: 39.3 us -> 37.7 us (0.959)
  waiting for transfers between devices: 18.3 us -> 14.7 us
  Pallas kernels: 9.95 us -> 11.3 us
  starting transfers between devices: 10.1 us -> 10.8 us
    ppermute x8 -> x9, waiting for transfers between devices: 15.5 us -> 11.3 us  [over_op(): return lax.ppermute(value, 'op', [(i, target(i)) for i in range(n)])]
    pallas_call x9 -> x13, Pallas kernels: 9.95 us -> 11.3 us  [kernel_call(): pl.pallas_call(run, grid=grid, out_shape=[jax.ShapeDtypeStruct((8, 128),...]
    ppermute x8 -> x9, starting transfers between devices: 8.06 us -> 8.73 us  [over_op(): return lax.ppermute(value, 'op', [(i, target(i)) for i in range(n)])]
    ppermute x2, waiting for transfers between devices: 2.9 us -> 3.45 us  [swapped(): return lax.ppermute(value, 'sec', list(enumerate(to)))]
  transfers between devices with their start and end apart: 10 -> 11, of which waited for: 6 -> 7; matrix products, arithmetic and copies ran while one was open for 0% -> 0% of each run, Pallas kernels for 15% -> 22%
where the time goes in v4:
time: 37.7 us; the launch traced here: 37.5 us
  waiting for transfers between devices  14.7 us (39%)
  Pallas kernels  11.3 us (30%)
  starting transfers between devices  10.8 us (29%)
  between operations  0.71 us (2%)
    pallas_call x13, Pallas kernels, kernel_call(): pl.pallas_call(run, grid=grid, out_shape=[jax.ShapeDtypeStruct((8, 128),...  11.3 us
    ppermute x9, waiting for transfers between devices, over_op(): return lax.ppermute(value, 'op', [(i, target(i)) for i in range(n)])  11.3 us
    ppermute x9, starting transfers between devices, over_op(): return lax.ppermute(value, 'op', [(i, target(i)) for i in range(n)])  8.73 us
    ppermute x2, waiting for transfers between devices, swapped(): return lax.ppermute(value, 'sec', list(enumerate(to)))  3.45 us
    ppermute x2, starting transfers between devices, swapped(): return lax.ppermute(value, 'sec', list(enumerate(to)))  2.02 us
  transfers between devices with their start and end apart: 11, of which 7 were waited for; matrix products, arithmetic and copies ran while one was open for 0% of the time, Pallas kernels for 22%

profile of v4, /device:TPU:1, one launch (start us, length us, event | category | flops | bytes accessed | tf_op | source)
XLA Modules:
  0.0 37.5 jit_solution(16079208514161220484)
XLA Ops:
  0.6 1.7 %stage.1 = (f32[8,128]{1,0:T(8,128)S(1)}, bf16[2080,256]{1,0:T(8,128)(2,1)S(1)}, bf16[4,4,256,256]{3,2,1,0:T(8,128)(2,1)S(1)}) custom-call(s32[4]{0:T(128)} %bitcast.1, s32[4]{0:T(128)} %refs_1_.3, s32[4,4]{1,0:T(4,128)} %refs_2_.5, bf16[4,4,256,256]{3,2,1,0:T(8,128)(2,1)} %refs_3_.2), custom_call_target="tpu_custom_call" | custom-call | tf_op jit(solution)/shard_map/stage/pallas_call | solution.py:34
  2.3 2.7 %collective-permute-start.4 = (bf16[2080,256]{1,0:T(8,128)(2,1)S(1)}, bf16[2080,256]{1,0:T(8,128)(2,1)S(1)}, u32[]{:S(2)}, u32[]{:S(2)}) collective-permute-start(bf16[2080,256]{1,0:T(8,128)(2,1)S(1)} %get-tuple-element.58), channel_id=1, source_target_pairs={{0,16},{4,8},{8,4},{12,28},{16,0},{20,24},{24,20},{28,12},{1,17},{... | collective-permute-start | bytes 3194888 | tf_op jit(solution)/shard_map/ppermute | solution.py:493
  5.0 1.2 %restage.1 = (f32[8,128]{1,0:T(8,128)S(1)}, bf16[1040,256]{1,0:T(8,128)(2,1)S(1)}, bf16[1040,256]{1,0:T(8,128)(2,1)S(1)}, bf16[2080,256]{1,0:T(8,128)(2,1)S(1)},...) custom-call(f32[8,128]{1,0:T(8,128)S(1)} %get-tuple-element.40.refs_0_, s32[4]{0:T(128)} %bitcast.2, ...), custom_call_target="tpu_custom_call" | custom-call | tf_op jit(solution)/shard_map/restage/pallas_call | solution.py:34
  6.2 0.5 %collective-permute-start.6 = (bf16[2080,256]{1,0:T(8,128)(2,1)S(1)}, bf16[2080,256]{1,0:T(8,128)(2,1)S(1)}, u32[]{:S(2)}, u32[]{:S(2)}) collective-permute-start(bf16[2080,256]{1,0:T(8,128)(2,1)S(1)} %get-tuple-element.66), channel_id=1, source_target_pairs={{0,4},{4,0},{8,12},{12,8},{16,20},{20,16},{24,28},{28,24},{1,5},{5... | collective-permute-start | bytes 3194888 | tf_op jit(solution)/shard_map/ppermute | solution.py:493
  6.7 3.4 %sigma_terms.1 = (f32[8,128]{1,0:T(8,128)S(1)}, bf16[2,128,256]{2,1,0:T(8,128)(2,1)S(1)}, bf16[4,128,256]{2,1,0:T(8,128)(2,1)S(1)}, f32[6,128,256]{2,1,0:T(8,128)S(1)}, bf16[4,256,256]{2,1,0:T(8,128)(2,1)S(1)}) custom-call(f32[8,128]{1,0:T(8,128)S(1)} %get-tuple-element.42.refs_0_, s32[4]{0:T(128)} %refs_1_.3, s32[4,4]{1,0:T(4,128)} %refs_2_.5, ...), custom_call_target="tpu_custom_call" | custom-call | tf_op jit(solution)/shard_map/sigma_terms/pallas_call | solution.py:34
  10.1 0.2 collective-permute-start
  10.3 0.4 %collective-permute-start.1 = (bf16[2,128,256]{2,1,0:T(8,128)(2,1)S(1)}, bf16[2,128,256]{2,1,0:T(8,128)(2,1)S(1)}, u32[]{:S(2)}, u32[]{:S(2)}) collective-permute-start(bf16[2,128,256]{2,1,0:T(8,128)(2,1)S(1)} %get-tuple-element.49), channel_id=1, source_target_pairs={{0,4},{4,0},{8,12},{12,8},{16,20},{20,16},{24,28},{28,24},{1,5},{5... | collective-permute-start | bytes 393224 | tf_op jit(solution)/shard_map/ppermute | solution.py:493
  10.7 1.0 %collective-permute-done.refs_1_ = bf16[4,128,256]{2,1,0:T(8,128)(2,1)S(1)} collective-permute-done((bf16[4,128,256]{2,1,0:T(8,128)(2,1)S(1)}, bf16[4,128,256]{2,1,0:T(8,128)(2,1)S(1)}, u32[]{:S(2)}, u32[]{:S(2)}) %collective-permute-start) | collective-permute-done | bytes 262176 | tf_op jit(solution)/shard_map/ppermute | solution.py:493
  11.7 0.2 collective-permute-done.1.refs_2_
  12.0 1.4 %collective-permute-start.2 = (bf16[384,256]{1,0:T(8,128)(2,1)S(1)}, bf16[384,256]{1,0:T(8,128)(2,1)S(1)}, u32[]{:S(2)}, u32[]{:S(2)}) collective-permute-start(bf16[384,256]{1,0:T(8,128)(2,1)S(1)} %get-tuple-element.52), channel_id=1, source_target_pairs={{0,1},{1,0},{2,3},{3,2},{4,5},{5,4},{6,7},{7,6},{8,9},{9,8},{10,11... | collective-permute-start | bytes 589832 | tf_op jit(solution)/shard_map/ppermute | solution.py:499
  13.3 1.0 %collective-permute-start.7 = (bf16[1040,256]{1,0:T(8,128)(2,1)S(1)}, bf16[1040,256]{1,0:T(8,128)(2,1)S(1)}, u32[]{:S(2)}, u32[]{:S(2)}) collective-permute-start(bf16[1040,256]{1,0:T(8,128)(2,1)S(1)} %get-tuple-element.67), channel_id=1, source_target_pairs={{0,28},{4,20},{8,24},{12,16},{16,12},{20,4},{24,8},{28,0},{1,29},{... | collective-permute-start | bytes 1597448 | tf_op jit(solution)/shard_map/ppermute | solution.py:493
  14.3 0.7 %collective-permute-start.3 = (bf16[384,256]{1,0:T(8,128)(2,1)S(1)}, bf16[384,256]{1,0:T(8,128)(2,1)S(1)}, u32[]{:S(2)}, u32[]{:S(2)}) collective-permute-start(bf16[384,256]{1,0:T(8,128)(2,1)S(1)} %get-tuple-element.56), channel_id=1, source_target_pairs={{0,0},{1,2},{2,1},{3,3},{4,4},{5,6},{6,5},{7,7},{8,8},{9,10},{10,9... | collective-permute-start | bytes 589832 | tf_op jit(solution)/shard_map/ppermute | solution.py:499
  14.9 3.4 %collective-permute-done.2.refs_1_ = bf16[384,256]{1,0:T(8,128)(2,1)S(1)} collective-permute-done((bf16[384,256]{1,0:T(8,128)(2,1)S(1)}, bf16[384,256]{1,0:T(8,128)(2,1)S(1)}, u32[]{:S(2)}, u32[]{:S(2)}) %collective-permute-start.2) | collective-permute-done | bytes 196640 | tf_op jit(solution)/shard_map/ppermute | solution.py:499
  18.5 0.2 collective-permute-start.5
  18.7 2.1 %collective-permute-start.9 = (bf16[528,256]{1,0:T(8,128)(2,1)S(1)}, bf16[528,256]{1,0:T(8,128)(2,1)S(1)}, u32[]{:S(2)}, u32[]{:S(2)}) collective-permute-start(bf16[528,256]{1,0:T(8,128)(2,1)S(1)} %get-tuple-element.71), channel_id=1, source_target_pairs={{0,12},{4,20},{8,24},{12,0},{16,28},{20,4},{24,8},{28,16},{1,13},{... | collective-permute-start | bytes 811016 | tf_op jit(solution)/shard_map/ppermute | solution.py:493
  20.9 5.3 %collective-permute-done.5.refs_2_ = bf16[4,64,256]{2,1,0:T(8,128)(2,1)S(1)} collective-permute-done((bf16[4,64,256]{2,1,0:T(8,128)(2,1)S(1)}, bf16[4,64,256]{2,1,0:T(8,128)(2,1)S(1)}, u32[]{:S(2)}, u32[]{:S(2)}) %collective-permute-start.5) | collective-permute-done | bytes 131104 | tf_op jit(solution)/shard_map/ppermute | solution.py:493
  26.2 1.6 %collective-permute-start.8 = (bf16[4,32,256]{2,1,0:T(8,128)(2,1)S(1)}, bf16[4,32,256]{2,1,0:T(8,128)(2,1)S(1)}, u32[]{:S(2)}, u32[]{:S(2)}) collective-permute-start(bf16[4,32,256]{2,1,0:T(8,128)(2,1)S(1)} %get-tuple-element.70), channel_id=1, source_target_pairs={{0,16},{4,20},{8,24},{12,28},{16,0},{20,4},{24,8},{28,12},{1,17},{... | collective-permute-start | bytes 196616 | tf_op jit(solution)/shard_map/ppermute | solution.py:493
  27.8 0.1 collective-permute-start.10
  27.9 1.5 %collective-permute-done.7.refs_7_ = bf16[1040,256]{1,0:T(8,128)(2,1)S(1)} collective-permute-done((bf16[1040,256]{1,0:T(8,128)(2,1)S(1)}, bf16[1040,256]{1,0:T(8,128)(2,1)S(1)}, u32[]{:S(2)}, u32[]{:S(2)}) %collective-permute-start.7) | collective-permute-done | bytes 532512 | tf_op jit(solution)/shard_map/ppermute | solution.py:493
  29.4 2.2 %renorm_first.1 = (f32[8,128]{1,0:T(8,128)S(1)}, bf16[8,4,256,256]{3,2,1,0:T(8,128)(2,1)}) custom-call(f32[8,128]{1,0:T(8,128)S(1)} %get-tuple-element.65.refs_0_, bf16[4,256,256]{2,1,0:T(8,128)(2,1)S(1)} %get-tuple-element.50.refs_3_.refs_1_, bf16[4,256,256]{2,1,0:T(8,128)(2,1)S(1)} %get-tuple-element.44.refs_6_.refs_2_, ...), custom_call_target="tpu_custom_call" | custom-call | flops 2100000000 | tf_op jit(solution)/shard_map/renorm_first/pallas_call | solution.py:34
  31.6 2.1 %collective-permute-done.8.refs_6_ = bf16[4,32,256]{2,1,0:T(8,128)(2,1)S(1)} collective-permute-done((bf16[4,32,256]{2,1,0:T(8,128)(2,1)S(1)}, bf16[4,32,256]{2,1,0:T(8,128)(2,1)S(1)}, u32[]{:S(2)}, u32[]{:S(2)}) %collective-permute-start.8) | collective-permute-done | bytes 65568 | tf_op jit(solution)/shard_map/ppermute | solution.py:493
  33.7 1.3 %renorm_last.2 = (f32[8,128]{1,0:T(8,128)S(1)}, bf16[8,4,256,256]{3,2,1,0:T(8,128)(2,1)}, f32[4,32,256]{2,1,0:T(8,128)}) custom-call(f32[8,128]{1,0:T(8,128)S(1)} %get-tuple-element.68.refs_0_, bf16[4,256,256]{2,1,0:T(8,128)(2,1)S(1)} %get-tuple-element.50.refs_3_.refs_1_, ...), custom_call_target="tpu_custom_call", output_to_operand_aliasing={{1}: (10, {})} | custom-call | flops 2000000000 | tf_op jit(solution)/shard_map/renorm_last/pallas_call | solution.py:34
  35.0 1.2 %collective-permute-done.10.refs_6_ = bf16[512,256]{1,0:T(8,128)(2,1)S(1)} collective-permute-done((bf16[512,256]{1,0:T(8,128)(2,1)S(1)}, bf16[512,256]{1,0:T(8,128)(2,1)S(1)}, u32[]{:S(2)}, u32[]{:S(2)}) %collective-permute-start.10) | collective-permute-done | bytes 262176 | tf_op jit(solution)/shard_map/ppermute | solution.py:493
  36.2 1.3 %renorm_last.3 = (f32[8,128]{1,0:T(8,128)}, bf16[8,4,256,256]{3,2,1,0:T(8,128)(2,1)}) custom-call(f32[8,128]{1,0:T(8,128)S(1)} %get-tuple-element.74.refs_0_, bf16[4,256,256]{2,1,0:T(8,128)(2,1)S(1)} %get-tuple-element.50.refs_3_.refs_1_, bf16[4,256,256]{2,1,0:T(8,128)(2,1)S(1)} %get-tuple-element.44.refs_6_.refs_2_, ...), custom_call_target="tpu_custom_call", output_to_operand_aliasing={{1}: (8, {})} | custom-call | tf_op jit(solution)/shard_map/renorm_last/pallas_call | solution.py:34
  (11 shorter events, 0.2 us)
Async XLA Ops:
  2.3 16.4 %collective-permute-start.4 = (bf16[2080,256]{1,0:T(8,128)(2,1)S(1)}, bf16[2080,256]{1,0:T(8,128)(2,1)S(1)}, u32[]{:S(2)}, u32[]{:S(2)}) collective-permute-start(bf16[2080,256]{1,0:T(8,128)(2,1)S(1)} %get-tuple-element.58), channel_id=1, source_target_pairs={{0,16},{4,8},{8,4},{12,28},{16,0},{20,24},{24,20},{28,12},{1,17},{... | collective-permute-start | bytes 3194888 | tf_op jit(solution)/shard_map/ppermute | solution.py:493
  6.2 23.2 %collective-permute-start.6 = (bf16[2080,256]{1,0:T(8,128)(2,1)S(1)}, bf16[2080,256]{1,0:T(8,128)(2,1)S(1)}, u32[]{:S(2)}, u32[]{:S(2)}) collective-permute-start(bf16[2080,256]{1,0:T(8,128)(2,1)S(1)} %get-tuple-element.66), channel_id=1, source_target_pairs={{0,4},{4,0},{8,12},{12,8},{16,20},{20,16},{24,28},{28,24},{1,5},{5... | collective-permute-start | bytes 3194888 | tf_op jit(solution)/shard_map/ppermute | solution.py:493
  10.1 1.6 %collective-permute-start = (bf16[4,128,256]{2,1,0:T(8,128)(2,1)S(1)}, bf16[4,128,256]{2,1,0:T(8,128)(2,1)S(1)}, u32[]{:S(2)}, u32[]{:S(2)}) collective-permute-start(bf16[4,128,256]{2,1,0:T(8,128)(2,1)S(1)} %get-tuple-element.46), channel_id=1, source_target_pairs={{0,4},{4,0},{8,12},{12,8},{16,20},{20,16},{24,28},{28,24},{1,5},{5... | collective-permute-start | bytes 786440 | tf_op jit(solution)/shard_map/ppermute | solution.py:493
  10.3 1.6 %collective-permute-start.1 = (bf16[2,128,256]{2,1,0:T(8,128)(2,1)S(1)}, bf16[2,128,256]{2,1,0:T(8,128)(2,1)S(1)}, u32[]{:S(2)}, u32[]{:S(2)}) collective-permute-start(bf16[2,128,256]{2,1,0:T(8,128)(2,1)S(1)} %get-tuple-element.49), channel_id=1, source_target_pairs={{0,4},{4,0},{8,12},{12,8},{16,20},{20,16},{24,28},{28,24},{1,5},{5... | collective-permute-start | bytes 393224 | tf_op jit(solution)/shard_map/ppermute | solution.py:493
  12.0 6.4 %collective-permute-start.2 = (bf16[384,256]{1,0:T(8,128)(2,1)S(1)}, bf16[384,256]{1,0:T(8,128)(2,1)S(1)}, u32[]{:S(2)}, u32[]{:S(2)}) collective-permute-start(bf16[384,256]{1,0:T(8,128)(2,1)S(1)} %get-tuple-element.52), channel_id=1, source_target_pairs={{0,1},{1,0},{2,3},{3,2},{4,5},{5,4},{6,7},{7,6},{8,9},{9,8},{10,11... | collective-permute-start | bytes 589832 | tf_op jit(solution)/shard_map/ppermute | solution.py:499
  13.3 16.1 %collective-permute-start.7 = (bf16[1040,256]{1,0:T(8,128)(2,1)S(1)}, bf16[1040,256]{1,0:T(8,128)(2,1)S(1)}, u32[]{:S(2)}, u32[]{:S(2)}) collective-permute-start(bf16[1040,256]{1,0:T(8,128)(2,1)S(1)} %get-tuple-element.67), channel_id=1, source_target_pairs={{0,28},{4,20},{8,24},{12,16},{16,12},{20,4},{24,8},{28,0},{1,29},{... | collective-permute-start | bytes 1597448 | tf_op jit(solution)/shard_map/ppermute | solution.py:493
  14.3 4.1 %collective-permute-start.3 = (bf16[384,256]{1,0:T(8,128)(2,1)S(1)}, bf16[384,256]{1,0:T(8,128)(2,1)S(1)}, u32[]{:S(2)}, u32[]{:S(2)}) collective-permute-start(bf16[384,256]{1,0:T(8,128)(2,1)S(1)} %get-tuple-element.56), channel_id=1, source_target_pairs={{0,0},{1,2},{2,1},{3,3},{4,4},{5,6},{6,5},{7,7},{8,8},{9,10},{10,9... | collective-permute-start | bytes 589832 | tf_op jit(solution)/shard_map/ppermute | solution.py:499
  18.5 7.7 %collective-permute-start.5 = (bf16[4,64,256]{2,1,0:T(8,128)(2,1)S(1)}, bf16[4,64,256]{2,1,0:T(8,128)(2,1)S(1)}, u32[]{:S(2)}, u32[]{:S(2)}) collective-permute-start(bf16[4,64,256]{2,1,0:T(8,128)(2,1)S(1)} %get-tuple-element.62), channel_id=1, source_target_pairs={{0,8},{4,12},{8,0},{12,4},{16,24},{20,28},{24,16},{28,20},{1,9},{5... | collective-permute-start | bytes 393224 | tf_op jit(solution)/shard_map/ppermute | solution.py:493
  18.7 15.0 %collective-permute-start.9 = (bf16[528,256]{1,0:T(8,128)(2,1)S(1)}, bf16[528,256]{1,0:T(8,128)(2,1)S(1)}, u32[]{:S(2)}, u32[]{:S(2)}) collective-permute-start(bf16[528,256]{1,0:T(8,128)(2,1)S(1)} %get-tuple-element.71), channel_id=1, source_target_pairs={{0,12},{4,20},{8,24},{12,0},{16,28},{20,4},{24,8},{28,16},{1,13},{... | collective-permute-start | bytes 811016 | tf_op jit(solution)/shard_map/ppermute | solution.py:493
  26.2 7.4 %collective-permute-start.8 = (bf16[4,32,256]{2,1,0:T(8,128)(2,1)S(1)}, bf16[4,32,256]{2,1,0:T(8,128)(2,1)S(1)}, u32[]{:S(2)}, u32[]{:S(2)}) collective-permute-start(bf16[4,32,256]{2,1,0:T(8,128)(2,1)S(1)} %get-tuple-element.70), channel_id=1, source_target_pairs={{0,16},{4,20},{8,24},{12,28},{16,0},{20,4},{24,8},{28,12},{1,17},{... | collective-permute-start | bytes 196616 | tf_op jit(solution)/shard_map/ppermute | solution.py:493
  27.8 8.4 %collective-permute-start.10 = (bf16[512,256]{1,0:T(8,128)(2,1)S(1)}, bf16[512,256]{1,0:T(8,128)(2,1)S(1)}, u32[]{:S(2)}, u32[]{:S(2)}) collective-permute-start(bf16[512,256]{1,0:T(8,128)(2,1)S(1)} %get-tuple-element.75), channel_id=1, source_target_pairs={{0,12},{4,20},{8,24},{12,0},{16,28},{20,4},{24,8},{28,16},{1,13},{... | collective-permute-start | bytes 786440 | tf_op jit(solution)/shard_map/ppermute | solution.py:493

commit v5 on v4

--- a/solution.py
+++ b/solution.py
@@ -10,7 +10,8 @@
 
 DIRS = 4
 CAPS = 2
-META = 16
+
+STEP = 2_000_000_000
 
 BF16 = jnp.bfloat16
 F32 = jnp.float32
@@ -48,8 +49,8 @@
     return pltpu.with_memory_space_constraint(value, pltpu.HBM)
 
 
-def estimate(flops, moved):
-    return pl.CostEstimate(flops=0, bytes_accessed=0, transcendentals=0)
+def estimate(flops):
+    return pl.CostEstimate(flops=flops, bytes_accessed=0, transcendentals=0)
 
 
 def fetch_scalars(pairs, sem):
@@ -58,6 +59,10 @@
         copy.start()
     for copy in copies:
         copy.wait()
+
+
+def meta_rows(sectors):
+    return -(-2 * (2 + sectors) // 16) * 16
 
 
 def at_end(half):
@@ -90,33 +95,47 @@
         "core": pick(kinds, places, 1 + odd, 0),
         "side": pick(kinds, places, 2 - odd, 0),
     }
-    row = lax.broadcasted_iota(jnp.int32, (META, width), 0)
-    for out, wanted in zip(outs, roles):
-        base = 0
-        for role in wanted:
-            index = found[role] if isinstance(role, str) else jnp.where(end, *map(found.get, role))
+
+    def index_of(role):
+        return found[role] if isinstance(role, str) else jnp.where(end, *map(found.get, role))
+
+    height = meta_rows(sectors)
+    row = lax.broadcasted_iota(jnp.int32, (height, width), 0)
+    for out, (sent, told) in zip(outs, roles):
+        for i, role in enumerate(sent):
+            index = index_of(role)
             for s in range(sectors):
-                out[base + s * width : base + (s + 1) * width] = left[index, s]
+                at = (i * sectors + s) * width
+                out[at : at + width] = left[index, s]
+        if not told:
+            continue
+        values = jnp.zeros((height, width), jnp.int32)
+        for i, role in enumerate(told):
+            index = index_of(role)
+            at = i * (height // 2)
             kind = jnp.int32(0)
             for p in range(count):
                 kind = kind + jnp.where(index == p, kinds[p], 0)
-            values = jnp.where(row == 0, charges[index], jnp.where(row == 1, kind, 0))
+            values = jnp.where(row == at, charges[index], jnp.where(row == at + 1, kind, values))
             for s in range(sectors):
-                values = jnp.where(row == 2 + s, present[index, s], values)
-            base += sectors * width
-            out[base : base + META] = values.astype(F32).astype(BF16)
-            base += META
+                values = jnp.where(row == at + 2 + s, present[index, s], values)
+        at = len(sent) * sectors * width
+        out[at : at + height] = values.astype(F32).astype(BF16)
 
 
 def stage_kernel(roles, half, directions_ref, charges_ref, present_ref, left_ref, *refs):
     outs = refs[: len(roles)]
     left, directions, charges, present, few, sem = refs[len(roles) :]
-    bulk = pltpu.make_async_copy(left_ref, left, sem)
-    bulk.start()
+    bulk = [
+        pltpu.make_async_copy(left_ref.at[p], left.at[p], sem) for p in range(left.shape[0])
+    ]
+    for copy in bulk:
+        copy.start()
     fetch_scalars(
         [(directions_ref, directions), (charges_ref, charges), (present_ref, present)], few
     )
-    bulk.wait()
+    for copy in bulk:
+        copy.wait()
     copy_pairs(roles, half, outs, left, directions, charges, present)
 
 
@@ -141,9 +160,10 @@
 
 def staged(token, roles, half, directions, charges, present, left, *more):
     count, sectors, width, _ = left.shape
-    rows = sectors * width + META
-    parts = [(0, sectors // 2), (sectors // 2, sectors)] if sectors > 1 else [(0, 1)]
-    shapes = [(rows * len(wanted), width) for wanted in roles]
+    shapes = [
+        (len(sent) * sectors * width + (meta_rows(sectors) if told else 0), width)
+        for sent, told in roles
+    ]
     shapes += [x.shape for x in more] if more else [left.shape]
     operands = [in_hbm(x) for x in (directions, charges, present)]
     operands += [left, *map(in_hbm, more)] if more else [in_hbm(left)]
@@ -162,7 +182,7 @@
             pltpu.SemaphoreType.DMA((len(more),)) if more else pltpu.SemaphoreType.DMA,
         ],
         mib=4,
-        cost_estimate=estimate(0, 0),
+        cost_estimate=estimate(0),
         name="restage" if more else "stage",
     )
 
@@ -238,7 +258,7 @@
             pltpu.SemaphoreType.DMA((count,)),
         ],
         mib=10,
-        cost_estimate=estimate(0, 0),
+        cost_estimate=estimate(0),
         name="sigma_terms",
     )
 
@@ -263,7 +283,7 @@
         [jax.ShapeDtypeStruct(shape, BF16)] * 2,
         [VMEM] * 2,
         mib=4,
-        cost_estimate=estimate(0, 0),
+        cost_estimate=estimate(0),
         name="edges",
     )
 
@@ -310,7 +330,7 @@
         ],
         [VMEM] * 2,
         mib=4,
-        cost_estimate=pl.CostEstimate(flops=0 if edge else 2000000000, bytes_accessed=0, transcendentals=0),
+        cost_estimate=estimate(0 if edge else STEP),
         name="split",
     )
 
@@ -329,7 +349,7 @@
         [ANY] * len(values),
         aliases={i: i for i in range(len(values))},
         mib=1,
-        cost_estimate=pl.CostEstimate(flops=cost, bytes_accessed=0, transcendentals=0),
+        cost_estimate=estimate(cost),
         name="hold",
     )
 
@@ -339,9 +359,7 @@
 
     def fill(source):
         for out, (at, size) in zip(outs, cuts):
-            out[:size] = source[at : at + size]
-            if out.shape[0] > size:
-                out[size:] = source[second.shape[0] - META : second.shape[0]]
+            out[...] = source[at : at + size]
 
     @pl.when(end)
     def _():
@@ -360,72 +378,54 @@
         token,
         (first, second),
         [VMEM] * 2,
-        [
-            pltpu.VMEM((size + (META if i == 0 else 0), width), BF16)
-            for i, (_, size) in enumerate(cuts)
-        ],
+        [pltpu.VMEM((size, width), BF16) for _, size in cuts],
         [VMEM] * len(cuts),
         mib=4,
-        cost_estimate=estimate(0, 0),
+        cost_estimate=estimate(0),
         name="choose",
     )
 
 
-def renorm_kernel(items, zero, offset, levels, half, scale, turned, rotations, one, two, *refs):
-    if scale is not None:
-        (keep, got), refs = refs[:2], refs[2:]
-    buffers = refs[: 1 + max(max(source[::2]) for item in items for source in item[0])]
+def renorm_kernel(items, zero, offset, levels, half, turned, rotations, one, two, *refs):
+    buffers = refs[: 1 + max(buffer for came, told, *_ in items for buffer in (came[0], told[0]))]
     rest = refs[len(buffers) + (0 if zero else 1) :]
-    if scale is not None:
-        sigma, *rest, total = [rest[1], rest[0], *rest[2:]]
-        total[...] = (keep[...] + got[...].astype(F32)) * scale
     out, edge, results, done = rest
     sectors, width, _ = rotations.shape
-    device = lax.axis_index("op")
-    odd = lax.rem(device, 2)
+    odd = lax.rem(lax.axis_index("op"), 2)
     end = at_end(half)
     level = lax.axis_index("sec")
     raised = lax.rem(level, 2) == 1
     rows = pl.ds(offset, width)
+    height = meta_rows(sectors)
     stores = []
-    if scale is not None:
-        copy = pltpu.make_async_copy(total, sigma, done)
-        copy.start()
-        stores.append(copy)
     if zero:
         results[len(items)] = jnp.zeros_like(results[len(items)])
         for place in range(CAPS):
             copy = pltpu.make_async_copy(results.at[len(items)], out.at[place], done)
             copy.start()
             stores.append(copy)
-    edge[0] = jnp.where(raised, one[rows], two[rows])
-    edge[1] = jnp.where(raised, two[rows], one[rows])
-    for i, (sources, kind, place, begin, stop) in enumerate(items):
-
-        def received(places, count):
-            loaded = [buffers[buffer][pl.ds(at, count)] for buffer, at in places]
-            return loaded[0] if len(loaded) == 1 else jnp.where(end, loaded[0], loaded[1])
-
-        values = received([source[2:] for source in sources], META).astype(F32)
-
-        def scalar(row):
-            return jnp.max(values[row : row + 1, :])
-
-        charge = scalar(0).astype(jnp.int32)
-        if kind == "core":
-            kind = 2 - odd
-        elif kind == "side":
-            kind = 1 + odd
-        if place == 1:
-            wanted = jnp.where(scalar(1).astype(jnp.int32) == kind, 1.0, 0.0)
-        else:
-            wanted = jnp.float32(1.0)
+    if any(begin == 0 for *_, begin, _ in items):
+        edge[0] = jnp.where(raised, one[rows], two[rows])
+    if any(stop == sectors for *_, stop in items):
+        edge[1] = jnp.where(raised, two[rows], one[rows])
+    kinds = {"core": 2 - odd, "side": 1 + odd, "half": 3}
+    for i, ((buffer, base), (about, top, slot), targets, begin, stop) in enumerate(items):
+        values = buffers[about][pl.ds(top, height)].astype(F32)
+        values = values[slot * (height // 2) : (slot + 1) * (height // 2)]
+        charge = jnp.max(values[:1]).astype(jnp.int32)
+        kind, place = (kinds[targets[0][0]], targets[0][1])
+        if len(targets) > 1:
+            kind = jnp.where(end, kind, kinds[targets[1][0]])
+            place = jnp.where(end, place, targets[1][1])
+        weights = values[2 : 2 + sectors]
+        named = jnp.where(values[1:2] == jnp.asarray(kind).astype(F32), weights, 0.0)
+        weights = jnp.where(place == 1, named, weights)
         for s in range(begin, stop):
             at = s + charge
             whole = level * sectors + at
             inside = jnp.logical_and(whole >= 0, whole < levels * sectors)
-            weight = jnp.where(inside, scalar(2 + s) * wanted, 0.0)
-            block = received([(x[0], x[1] + (s - begin) * width) for x in sources], width)
+            weight = jnp.where(inside, weights[s : s + 1], 0.0)
+            block = buffers[buffer][pl.ds(base + (s - begin) * width, width)]
             rotated = jnp.dot(block, rotations[s], preferred_element_type=F32).astype(BF16)
             target = turned[jnp.clip(at, 0, sectors - 1)]
             if s == 0:
@@ -442,37 +442,52 @@
 
 
 def renorm(
-    token, name, items, buffers, out, offset, levels, half, turned, rotations, one, two, sums=(), scale=None, cost=0
+    token, name, items, buffers, out, offset, levels, half, turned, rotations, one, two, cost=0
 ):
     sectors, width, _ = rotations.shape
     zero = out is None
-    operands = [turned, rotations, one, two, *sums, *buffers]
+    operands = [turned, rotations, one, two, *buffers]
     in_specs = [VMEM] * len(operands)
     if not zero:
         operands.append(out)
         in_specs.append(HBM)
     count = len(items)
     block = (sectors, width, width)
-    return kernel_call(
-        functools.partial(renorm_kernel, items, zero, offset, levels, half, scale),
+    token, (out,) = kernel_call(
+        functools.partial(renorm_kernel, items, zero, offset, levels, half),
         token,
         operands,
         in_specs,
-        [jax.ShapeDtypeStruct((DIRS * CAPS, *block), BF16)]
-        + [jax.ShapeDtypeStruct(x.shape, F32) for x in sums[:1]],
-        [HBM] * (1 + len(sums[:1])),
+        [jax.ShapeDtypeStruct((DIRS * CAPS, *block), BF16)],
+        [HBM],
         aliases={} if zero else {len(operands) - 1: 0},
         scratch_shapes=[
             pltpu.VMEM((2, width, width), BF16),
             pltpu.VMEM((count + (1 if zero else 0), *block), BF16),
             pltpu.SemaphoreType.DMA,
-            *[pltpu.VMEM(x.shape, F32) for x in sums[:1]],
         ],
         mib=8,
-        cost_estimate=pl.CostEstimate(
-            flops=cost, bytes_accessed=0, transcendentals=0
-        ),
+        cost_estimate=estimate(cost),
         name=name,
+    )
+    return token, out
+
+
+def finish_kernel(scale, keep, got, out):
+    out[...] = (keep[...] + got[...].astype(F32)) * scale
+
+
+def finish(token, scale, keep, got):
+    return kernel_call(
+        functools.partial(finish_kernel, scale),
+        token,
+        (keep, got),
+        [VMEM] * 2,
+        [jax.ShapeDtypeStruct(keep.shape, F32)],
+        [VMEM],
+        mib=4,
+        cost_estimate=estimate(STEP),
+        name="finish",
     )
 
 
@@ -486,7 +501,7 @@
     half = n // 2
     chunk = width // n
     halving = n >= 4 and n & (n - 1) == 0 and chunk % 16 == 0
-    rows = sectors * width + META
+    rows = sectors * width
     parts = [(0, sectors // 2), (sectors // 2, sectors)] if sectors > 1 else [(0, 1)]
 
     def over_op(value, target):
@@ -511,12 +526,15 @@
         return i - i % half + half - 1 - i % half
 
     small = (directions[:, 0], charges, present_blocks)
+    ahead_roles = (("extra", "side"), ("half", "extra"))
+    behind_roles = (("side", "extra"), ("extra", "half"))
+    core_roles = ("extra", "core")
     token, (ahead, left) = staged(
-        None, ((("extra", "side"), ("half", "extra")),), half, *small, left_operators
+        None, ((ahead_roles, ahead_roles),), half, *small, left_operators
     )
     token, (behind, last, first_core, wave, turn) = staged(
         token,
-        ((("side", "extra"),), ("half",), ("extra", "core")),
+        ((behind_roles[:1], behind_roles), (("half",), ()), (core_roles, core_roles)),
         half,
         *small,
         left,
@@ -538,7 +556,7 @@
         token, (first, second) = edges(token, keep, got_edges, turned)
         one, two = swapped(first, 0), swapped(second, 1)
         offset = width // 2
-        token, (one,) = hold(token, one, cost=1200000000)
+        token, (one,) = hold(token, one, cost=STEP // 2)
         bit = 2
         token, (send, keep) = split(token, bit, chunk, levels, keep, got, one, two)
         got = over_op(send, lambda i: i ^ 2)
@@ -568,49 +586,34 @@
         token, last[1:] = hold(token, *last[1:])
     got_last = [over_op(x, lambda i: relay(i) if end(i) else opposite(i)) for x in last]
     fixed = (offset, levels, half, turned, turn, one, two)
-    meta = sectors * width
     whole = (0, sectors)
-    token, (out,) = renorm(
+    token, out = renorm(
         token,
         "renorm_first",
         (
-            (((0, 0, 0, meta),), "core", 1, *whole),
-            (((0, rows, 0, rows + meta),), "core", 0, *whole),
-            (((2, 0, 2, meta), (1, 0, 1, meta)), "side", 0, *whole),
-            (((1, 0, 1, meta), (2, 0, 2, meta)), 3, 1, *whole),
+            ((0, 0), (0, 2 * rows, 0), (("core", 1),), *whole),
+            ((0, rows), (0, 2 * rows, 1), (("core", 0),), *whole),
+            ((1, 0), (1, 2 * rows, 0), (("half", 1), ("side", 0)), *whole),
+            ((1, rows), (1, 2 * rows, 1), (("half", 0), ("side", 1)), *whole),
+            ((2, 0), (2, rows, 0), (("side", 0), ("half", 1)), *whole),
         ),
         (from_core, got_ahead, got_behind),
         None,
         *fixed,
-        cost=2100000000,
+        cost=STEP,
     )
     scale = 1.0 / math.sqrt(pairs * n)
     for i, (begin, stop) in enumerate(parts):
-        final = i == len(parts) - 1
-        piece = begin * width
-        behind_first = (parts[0][1] - parts[0][0]) * width
-        token, (out, *sums) = renorm(
+        if halving and i == len(parts) - 1:
+            token, (sigma_vector,) = finish(token, scale, keep, got)
+        token, out = renorm(
             token,
             "renorm_last",
-            (
-                (
-                    ((1, 0, 2, behind_first), (0, rows + piece, 0, rows + meta)),
-                    "side",
-                    1,
-                    begin,
-                    stop,
-                ),
-                (((0, rows + piece, 0, rows + meta), (1, 0, 2, behind_first)), 3, 0, begin, stop),
-            ),
-            (got_ahead, got_last[i], got_last[0]),
+            (((0, 0), (1, rows, 1), (("side", 1), ("half", 0)), begin, stop),),
+            (got_last[i], got_behind),
             out,
             *fixed,
-            sums=(keep, got) if halving and i == 0 else (),
-            scale=scale if halving and i == 0 else None,
-            cost=0 if final else 2000000000,
         )
-        if sums:
-            (sigma_vector,) = sums
     if not halving:
         sigma_vector = summed * scale
     return sigma_vector, out

time: 37.7 us -> 37.3 us (0.989)
  waiting for transfers between devices: 14.7 us -> 13.9 us
  Pallas kernels: 11.3 us -> 11.9 us
    ppermute x9, waiting for transfers between devices: 11.3 us -> 10.5 us  [over_op(): return lax.ppermute(value, 'op', [(i, target(i)) for i in range(n)])]
    pallas_call x13 -> x14, Pallas kernels: 11.3 us -> 11.9 us  [kernel_call(): pl.pallas_call(run, grid=grid, out_shape=[jax.ShapeDtypeStruct((8, 128),...]
  transfers between devices with their start and end apart: 11 -> 11, of which waited for: 7 -> 7; matrix products, arithmetic and copies ran while one was open for 0% -> 0% of each run, Pallas kernels for 22% -> 25%
where the time goes in v5:
time: 37.3 us; the launch traced here: 37.1 us
  waiting for transfers between devices  13.9 us (37%)
  Pallas kernels  11.9 us (32%)
  starting transfers between devices  10.6 us (28%)
  between operations  0.71 us (2%)
    pallas_call x14, Pallas kernels, kernel_call(): pl.pallas_call(run, grid=grid, out_shape=[jax.ShapeDtypeStruct((8, 128),...  11.9 us
    ppermute x9, waiting for transfers between devices, over_op(): return lax.ppermute(value, 'op', [(i, target(i)) for i in range(n)])  10.5 us
    ppermute x9, starting transfers between devices, over_op(): return lax.ppermute(value, 'op', [(i, target(i)) for i in range(n)])  8.55 us
    ppermute x2, waiting for transfers between devices, swapped(): return lax.ppermute(value, 'sec', list(enumerate(to)))  3.45 us
    ppermute x2, starting transfers between devices, swapped(): return lax.ppermute(value, 'sec', list(enumerate(to)))  2.02 us
  transfers between devices with their start and end apart: 11, of which 7 were waited for; matrix products, arithmetic and copies ran while one was open for 0% of the time, Pallas kernels for 25%

profile of v5, /device:TPU:1, one launch (start us, length us, event | category | flops | bytes accessed | tf_op | source)
XLA Modules:
  0.0 37.1 jit_solution(13223521393107836343)
XLA Ops:
  0.6 1.6 %stage.1 = (f32[8,128]{1,0:T(8,128)S(1)}, bf16[2064,256]{1,0:T(8,128)(2,1)S(1)}, bf16[4,4,256,256]{3,2,1,0:T(8,128)(2,1)S(1)}) custom-call(s32[4]{0:T(128)} %bitcast.1, s32[4]{0:T(128)} %refs_1_.3, s32[4,4]{1,0:T(4,128)} %refs_2_.5, bf16[4,4,256,256]{3,2,1,0:T(8,128)(2,1)} %refs_3_.2), custom_call_target="tpu_custom_call" | custom-call | tf_op jit(solution)/shard_map/stage/pallas_call | solution.py:35
  2.2 2.7 %collective-permute-start.4 = (bf16[2064,256]{1,0:T(8,128)(2,1)S(1)}, bf16[2064,256]{1,0:T(8,128)(2,1)S(1)}, u32[]{:S(2)}, u32[]{:S(2)}) collective-permute-start(bf16[2064,256]{1,0:T(8,128)(2,1)S(1)} %get-tuple-element.59), channel_id=1, source_target_pairs={{0,16},{4,8},{8,4},{12,28},{16,0},{20,24},{24,20},{28,12},{1,17},{... | collective-permute-start | bytes 3170312 | tf_op jit(solution)/shard_map/ppermute | solution.py:508
  4.9 1.2 %restage.1 = (f32[8,128]{1,0:T(8,128)S(1)}, bf16[1040,256]{1,0:T(8,128)(2,1)S(1)}, bf16[1024,256]{1,0:T(8,128)(2,1)S(1)}, bf16[2064,256]{1,0:T(8,128)(2,1)S(1)},...) custom-call(f32[8,128]{1,0:T(8,128)S(1)} %get-tuple-element.41.refs_0_, s32[4]{0:T(128)} %bitcast.2, ...), custom_call_target="tpu_custom_call" | custom-call | tf_op jit(solution)/shard_map/restage/pallas_call | solution.py:35
  6.1 0.5 %collective-permute-start.6 = (bf16[2064,256]{1,0:T(8,128)(2,1)S(1)}, bf16[2064,256]{1,0:T(8,128)(2,1)S(1)}, u32[]{:S(2)}, u32[]{:S(2)}) collective-permute-start(bf16[2064,256]{1,0:T(8,128)(2,1)S(1)} %get-tuple-element.67), channel_id=1, source_target_pairs={{0,4},{4,0},{8,12},{12,8},{16,20},{20,16},{24,28},{28,24},{1,5},{5... | collective-permute-start | bytes 3170312 | tf_op jit(solution)/shard_map/ppermute | solution.py:508
  6.6 3.4 %sigma_terms.1 = (f32[8,128]{1,0:T(8,128)S(1)}, bf16[2,128,256]{2,1,0:T(8,128)(2,1)S(1)}, bf16[4,128,256]{2,1,0:T(8,128)(2,1)S(1)}, f32[6,128,256]{2,1,0:T(8,128)S(1)}, bf16[4,256,256]{2,1,0:T(8,128)(2,1)S(1)}) custom-call(f32[8,128]{1,0:T(8,128)S(1)} %get-tuple-element.43.refs_0_, s32[4]{0:T(128)} %refs_1_.3, s32[4,4]{1,0:T(4,128)} %refs_2_.5, ...), custom_call_target="tpu_custom_call" | custom-call | tf_op jit(solution)/shard_map/sigma_terms/pallas_call | solution.py:35
  10.0 0.2 collective-permute-start
  10.2 0.4 %collective-permute-start.1 = (bf16[2,128,256]{2,1,0:T(8,128)(2,1)S(1)}, bf16[2,128,256]{2,1,0:T(8,128)(2,1)S(1)}, u32[]{:S(2)}, u32[]{:S(2)}) collective-permute-start(bf16[2,128,256]{2,1,0:T(8,128)(2,1)S(1)} %get-tuple-element.50), channel_id=1, source_target_pairs={{0,4},{4,0},{8,12},{12,8},{16,20},{20,16},{24,28},{28,24},{1,5},{5... | collective-permute-start | bytes 393224 | tf_op jit(solution)/shard_map/ppermute | solution.py:508
  10.6 1.0 %collective-permute-done.refs_1_ = bf16[4,128,256]{2,1,0:T(8,128)(2,1)S(1)} collective-permute-done((bf16[4,128,256]{2,1,0:T(8,128)(2,1)S(1)}, bf16[4,128,256]{2,1,0:T(8,128)(2,1)S(1)}, u32[]{:S(2)}, u32[]{:S(2)}) %collective-permute-start) | collective-permute-done | bytes 262176 | tf_op jit(solution)/shard_map/ppermute | solution.py:508
  11.6 0.2 collective-permute-done.1.refs_2_
  11.9 1.4 %collective-permute-start.2 = (bf16[384,256]{1,0:T(8,128)(2,1)S(1)}, bf16[384,256]{1,0:T(8,128)(2,1)S(1)}, u32[]{:S(2)}, u32[]{:S(2)}) collective-permute-start(bf16[384,256]{1,0:T(8,128)(2,1)S(1)} %get-tuple-element.53), channel_id=1, source_target_pairs={{0,1},{1,0},{2,3},{3,2},{4,5},{5,4},{6,7},{7,6},{8,9},{9,8},{10,11... | collective-permute-start | bytes 589832 | tf_op jit(solution)/shard_map/ppermute | solution.py:514
  13.2 1.0 %collective-permute-start.7 = (bf16[1040,256]{1,0:T(8,128)(2,1)S(1)}, bf16[1040,256]{1,0:T(8,128)(2,1)S(1)}, u32[]{:S(2)}, u32[]{:S(2)}) collective-permute-start(bf16[1040,256]{1,0:T(8,128)(2,1)S(1)} %get-tuple-element.68), channel_id=1, source_target_pairs={{0,28},{4,20},{8,24},{12,16},{16,12},{20,4},{24,8},{28,0},{1,29},{... | collective-permute-start | bytes 1597448 | tf_op jit(solution)/shard_map/ppermute | solution.py:508
  14.2 0.7 %collective-permute-start.3 = (bf16[384,256]{1,0:T(8,128)(2,1)S(1)}, bf16[384,256]{1,0:T(8,128)(2,1)S(1)}, u32[]{:S(2)}, u32[]{:S(2)}) collective-permute-start(bf16[384,256]{1,0:T(8,128)(2,1)S(1)} %get-tuple-element.57), channel_id=1, source_target_pairs={{0,0},{1,2},{2,1},{3,3},{4,4},{5,6},{6,5},{7,7},{8,8},{9,10},{10,9... | collective-permute-start | bytes 589832 | tf_op jit(solution)/shard_map/ppermute | solution.py:514
  14.9 3.4 %collective-permute-done.2.refs_1_ = bf16[384,256]{1,0:T(8,128)(2,1)S(1)} collective-permute-done((bf16[384,256]{1,0:T(8,128)(2,1)S(1)}, bf16[384,256]{1,0:T(8,128)(2,1)S(1)}, u32[]{:S(2)}, u32[]{:S(2)}) %collective-permute-start.2) | collective-permute-done | bytes 196640 | tf_op jit(solution)/shard_map/ppermute | solution.py:514
  18.4 0.2 collective-permute-start.5
  18.7 2.0 %collective-permute-start.8 = (bf16[512,256]{1,0:T(8,128)(2,1)S(1)}, bf16[512,256]{1,0:T(8,128)(2,1)S(1)}, u32[]{:S(2)}, u32[]{:S(2)}) collective-permute-start(bf16[512,256]{1,0:T(8,128)(2,1)S(1)} %get-tuple-element.70), channel_id=1, source_target_pairs={{0,12},{4,20},{8,24},{12,0},{16,28},{20,4},{24,8},{28,16},{1,13},{... | collective-permute-start | bytes 786440 | tf_op jit(solution)/shard_map/ppermute | solution.py:508
  20.6 5.4 %collective-permute-done.5.refs_2_ = bf16[4,64,256]{2,1,0:T(8,128)(2,1)S(1)} collective-permute-done((bf16[4,64,256]{2,1,0:T(8,128)(2,1)S(1)}, bf16[4,64,256]{2,1,0:T(8,128)(2,1)S(1)}, u32[]{:S(2)}, u32[]{:S(2)}) %collective-permute-start.5) | collective-permute-done | bytes 131104 | tf_op jit(solution)/shard_map/ppermute | solution.py:508
  26.1 1.6 %collective-permute-start.9 = (bf16[4,32,256]{2,1,0:T(8,128)(2,1)S(1)}, bf16[4,32,256]{2,1,0:T(8,128)(2,1)S(1)}, u32[]{:S(2)}, u32[]{:S(2)}) collective-permute-start(bf16[4,32,256]{2,1,0:T(8,128)(2,1)S(1)} %get-tuple-element.74), channel_id=1, source_target_pairs={{0,16},{4,20},{8,24},{12,28},{16,0},{20,4},{24,8},{28,12},{1,17},{... | collective-permute-start | bytes 196616 | tf_op jit(solution)/shard_map/ppermute | solution.py:508
  27.8 1.5 %collective-permute-done.7.refs_7_.refs_6_ = bf16[1040,256]{1,0:T(8,128)(2,1)S(1)} collective-permute-done((bf16[1040,256]{1,0:T(8,128)(2,1)S(1)}, bf16[1040,256]{1,0:T(8,128)(2,1)S(1)}, u32[]{:S(2)}, u32[]{:S(2)}) %collective-permute-start.7) | collective-permute-done | bytes 532512 | tf_op jit(solution)/shard_map/ppermute | solution.py:508
  29.2 2.5 %renorm_first.1 = (f32[8,128]{1,0:T(8,128)S(1)}, bf16[8,4,256,256]{3,2,1,0:T(8,128)(2,1)}) custom-call(f32[8,128]{1,0:T(8,128)S(1)} %get-tuple-element.66.refs_0_, bf16[4,256,256]{2,1,0:T(8,128)(2,1)S(1)} %get-tuple-element.51.refs_3_.refs_1_, bf16[4,256,256]{2,1,0:T(8,128)(2,1)S(1)} %get-tuple-element.45.refs_6_.refs_2_, ...), custom_call_target="tpu_custom_call" | custom-call | flops 2000000000 | tf_op jit(solution)/shard_map/renorm_first/pallas_call | solution.py:35
  31.7 1.0 %collective-permute-done.8.refs_5_ = bf16[512,256]{1,0:T(8,128)(2,1)S(1)} collective-permute-done((bf16[512,256]{1,0:T(8,128)(2,1)S(1)}, bf16[512,256]{1,0:T(8,128)(2,1)S(1)}, u32[]{:S(2)}, u32[]{:S(2)}) %collective-permute-start.8) | collective-permute-done | bytes 262176 | tf_op jit(solution)/shard_map/ppermute | solution.py:508
  32.7 1.1 %renorm_last.2 = (f32[8,128]{1,0:T(8,128)S(1)}, bf16[8,4,256,256]{3,2,1,0:T(8,128)(2,1)}) custom-call(f32[8,128]{1,0:T(8,128)S(1)} %get-tuple-element.69.refs_0_, bf16[4,256,256]{2,1,0:T(8,128)(2,1)S(1)} %get-tuple-element.51.refs_3_.refs_1_, bf16[4,256,256]{2,1,0:T(8,128)(2,1)S(1)} %get-tuple-element.45.refs_6_.refs_2_, ...), custom_call_target="tpu_custom_call", output_to_operand_aliasing={{1}: (7, {})} | custom-call | tf_op jit(solution)/shard_map/renorm_last/pallas_call | solution.py:35
  33.9 0.7 %finish.1 = (f32[8,128]{1,0:T(8,128)S(1)}, f32[4,32,256]{2,1,0:T(8,128)}) custom-call(f32[8,128]{1,0:T(8,128)S(1)} %get-tuple-element.72.refs_0_, f32[4,32,256]{2,1,0:T(8,128)S(1)} %get-tuple-element.73.refs_1_, bf16[4,32,256]{2,1,0:T(8,128)(2,1)S(1)} %collective-permute-done.9.refs_2_), custom_call_target="tpu_custom_call" | custom-call | flops 2000000000 | tf_op jit(solution)/shard_map/finish/pallas_call | solution.py:35
  34.6 1.4 %collective-permute-done.10.refs_5_ = bf16[512,256]{1,0:T(8,128)(2,1)S(1)} collective-permute-done((bf16[512,256]{1,0:T(8,128)(2,1)S(1)}, bf16[512,256]{1,0:T(8,128)(2,1)S(1)}, u32[]{:S(2)}, u32[]{:S(2)}) %collective-permute-start.10) | collective-permute-done | bytes 262176 | tf_op jit(solution)/shard_map/ppermute | solution.py:508
  35.9 1.1 %renorm_last.3 = (f32[8,128]{1,0:T(8,128)}, bf16[8,4,256,256]{3,2,1,0:T(8,128)(2,1)}) custom-call(f32[8,128]{1,0:T(8,128)S(1)} %get-tuple-element.76.refs_0_, bf16[4,256,256]{2,1,0:T(8,128)(2,1)S(1)} %get-tuple-element.51.refs_3_.refs_1_, bf16[4,256,256]{2,1,0:T(8,128)(2,1)S(1)} %get-tuple-element.45.refs_6_.refs_2_, ...), custom_call_target="tpu_custom_call", output_to_operand_aliasing={{1}: (7, {})} | custom-call | tf_op jit(solution)/shard_map/renorm_last/pallas_call | solution.py:35
  (12 shorter events, 0.3 us)
Async XLA Ops:
  2.2 16.4 %collective-permute-start.4 = (bf16[2064,256]{1,0:T(8,128)(2,1)S(1)}, bf16[2064,256]{1,0:T(8,128)(2,1)S(1)}, u32[]{:S(2)}, u32[]{:S(2)}) collective-permute-start(bf16[2064,256]{1,0:T(8,128)(2,1)S(1)} %get-tuple-element.59), channel_id=1, source_target_pairs={{0,16},{4,8},{8,4},{12,28},{16,0},{20,24},{24,20},{28,12},{1,17},{... | collective-permute-start | bytes 3170312 | tf_op jit(solution)/shard_map/ppermute | solution.py:508
  6.1 23.1 %collective-permute-start.6 = (bf16[2064,256]{1,0:T(8,128)(2,1)S(1)}, bf16[2064,256]{1,0:T(8,128)(2,1)S(1)}, u32[]{:S(2)}, u32[]{:S(2)}) collective-permute-start(bf16[2064,256]{1,0:T(8,128)(2,1)S(1)} %get-tuple-element.67), channel_id=1, source_target_pairs={{0,4},{4,0},{8,12},{12,8},{16,20},{20,16},{24,28},{28,24},{1,5},{5... | collective-permute-start | bytes 3170312 | tf_op jit(solution)/shard_map/ppermute | solution.py:508
  10.0 1.6 %collective-permute-start = (bf16[4,128,256]{2,1,0:T(8,128)(2,1)S(1)}, bf16[4,128,256]{2,1,0:T(8,128)(2,1)S(1)}, u32[]{:S(2)}, u32[]{:S(2)}) collective-permute-start(bf16[4,128,256]{2,1,0:T(8,128)(2,1)S(1)} %get-tuple-element.47), channel_id=1, source_target_pairs={{0,4},{4,0},{8,12},{12,8},{16,20},{20,16},{24,28},{28,24},{1,5},{5... | collective-permute-start | bytes 786440 | tf_op jit(solution)/shard_map/ppermute | solution.py:508
  10.2 1.6 %collective-permute-start.1 = (bf16[2,128,256]{2,1,0:T(8,128)(2,1)S(1)}, bf16[2,128,256]{2,1,0:T(8,128)(2,1)S(1)}, u32[]{:S(2)}, u32[]{:S(2)}) collective-permute-start(bf16[2,128,256]{2,1,0:T(8,128)(2,1)S(1)} %get-tuple-element.50), channel_id=1, source_target_pairs={{0,4},{4,0},{8,12},{12,8},{16,20},{20,16},{24,28},{28,24},{1,5},{5... | collective-permute-start | bytes 393224 | tf_op jit(solution)/shard_map/ppermute | solution.py:508
  11.9 6.4 %collective-permute-start.2 = (bf16[384,256]{1,0:T(8,128)(2,1)S(1)}, bf16[384,256]{1,0:T(8,128)(2,1)S(1)}, u32[]{:S(2)}, u32[]{:S(2)}) collective-permute-start(bf16[384,256]{1,0:T(8,128)(2,1)S(1)} %get-tuple-element.53), channel_id=1, source_target_pairs={{0,1},{1,0},{2,3},{3,2},{4,5},{5,4},{6,7},{7,6},{8,9},{9,8},{10,11... | collective-permute-start | bytes 589832 | tf_op jit(solution)/shard_map/ppermute | solution.py:514
  13.2 16.0 %collective-permute-start.7 = (bf16[1040,256]{1,0:T(8,128)(2,1)S(1)}, bf16[1040,256]{1,0:T(8,128)(2,1)S(1)}, u32[]{:S(2)}, u32[]{:S(2)}) collective-permute-start(bf16[1040,256]{1,0:T(8,128)(2,1)S(1)} %get-tuple-element.68), channel_id=1, source_target_pairs={{0,28},{4,20},{8,24},{12,16},{16,12},{20,4},{24,8},{28,0},{1,29},{... | collective-permute-start | bytes 1597448 | tf_op jit(solution)/shard_map/ppermute | solution.py:508
  14.2 4.1 %collective-permute-start.3 = (bf16[384,256]{1,0:T(8,128)(2,1)S(1)}, bf16[384,256]{1,0:T(8,128)(2,1)S(1)}, u32[]{:S(2)}, u32[]{:S(2)}) collective-permute-start(bf16[384,256]{1,0:T(8,128)(2,1)S(1)} %get-tuple-element.57), channel_id=1, source_target_pairs={{0,0},{1,2},{2,1},{3,3},{4,4},{5,6},{6,5},{7,7},{8,8},{9,10},{10,9... | collective-permute-start | bytes 589832 | tf_op jit(solution)/shard_map/ppermute | solution.py:514
  18.4 7.6 %collective-permute-start.5 = (bf16[4,64,256]{2,1,0:T(8,128)(2,1)S(1)}, bf16[4,64,256]{2,1,0:T(8,128)(2,1)S(1)}, u32[]{:S(2)}, u32[]{:S(2)}) collective-permute-start(bf16[4,64,256]{2,1,0:T(8,128)(2,1)S(1)} %get-tuple-element.63), channel_id=1, source_target_pairs={{0,8},{4,12},{8,0},{12,4},{16,24},{20,28},{24,16},{28,20},{1,9},{5... | collective-permute-start | bytes 393224 | tf_op jit(solution)/shard_map/ppermute | solution.py:508
  18.7 14.1 %collective-permute-start.8 = (bf16[512,256]{1,0:T(8,128)(2,1)S(1)}, bf16[512,256]{1,0:T(8,128)(2,1)S(1)}, u32[]{:S(2)}, u32[]{:S(2)}) collective-permute-start(bf16[512,256]{1,0:T(8,128)(2,1)S(1)} %get-tuple-element.70), channel_id=1, source_target_pairs={{0,12},{4,20},{8,24},{12,0},{16,28},{20,4},{24,8},{28,16},{1,13},{... | collective-permute-start | bytes 786440 | tf_op jit(solution)/shard_map/ppermute | solution.py:508
  26.1 7.8 %collective-permute-start.9 = (bf16[4,32,256]{2,1,0:T(8,128)(2,1)S(1)}, bf16[4,32,256]{2,1,0:T(8,128)(2,1)S(1)}, u32[]{:S(2)}, u32[]{:S(2)}) collective-permute-start(bf16[4,32,256]{2,1,0:T(8,128)(2,1)S(1)} %get-tuple-element.74), channel_id=1, source_target_pairs={{0,16},{4,20},{8,24},{12,28},{16,0},{20,4},{24,8},{28,12},{1,17},{... | collective-permute-start | bytes 196616 | tf_op jit(solution)/shard_map/ppermute | solution.py:508
  27.7 8.3 %collective-permute-start.10 = (bf16[512,256]{1,0:T(8,128)(2,1)S(1)}, bf16[512,256]{1,0:T(8,128)(2,1)S(1)}, u32[]{:S(2)}, u32[]{:S(2)}) collective-permute-start(bf16[512,256]{1,0:T(8,128)(2,1)S(1)} %get-tuple-element.77), channel_id=1, source_target_pairs={{0,12},{4,20},{8,24},{12,0},{16,28},{20,4},{24,8},{28,16},{1,13},{... | collective-permute-start | bytes 786440 | tf_op jit(solution)/shard_map/ppermute | solution.py:508

commit v6 on v5

--- a/solution.py
+++ b/solution.py
@@ -11,7 +11,7 @@
 DIRS = 4
 CAPS = 2
 
-STEP = 2_000_000_000
+PEAK = 1_153_500_000
 
 BF16 = jnp.bfloat16
 F32 = jnp.float32
@@ -49,8 +49,8 @@
     return pltpu.with_memory_space_constraint(value, pltpu.HBM)
 
 
-def estimate(flops):
-    return pl.CostEstimate(flops=flops, bytes_accessed=0, transcendentals=0)
+def estimate(microseconds):
+    return pl.CostEstimate(flops=int(microseconds * PEAK), bytes_accessed=0, transcendentals=0)
 
 
 def fetch_scalars(pairs, sem):
@@ -79,7 +79,8 @@
 
 
 def copy_pairs(roles, half, outs, left, directions, charges, present):
-    count, sectors, width, _ = left.shape
+    count, _, width, _ = left.shape
+    sectors = present.shape[1]
     kinds = [directions[p] for p in range(count)]
     places = []
     for p in range(count):
@@ -101,11 +102,11 @@
 
     height = meta_rows(sectors)
     row = lax.broadcasted_iota(jnp.int32, (height, width), 0)
-    for out, (sent, told) in zip(outs, roles):
+    for out, (sent, told, begin, stop) in zip(outs, roles):
         for i, role in enumerate(sent):
             index = index_of(role)
-            for s in range(sectors):
-                at = (i * sectors + s) * width
+            for s in range(begin, stop):
+                at = (i * (stop - begin) + s - begin) * width
                 out[at : at + width] = left[index, s]
         if not told:
             continue
@@ -119,15 +120,16 @@
             values = jnp.where(row == at, charges[index], jnp.where(row == at + 1, kind, values))
             for s in range(sectors):
                 values = jnp.where(row == at + 2 + s, present[index, s], values)
-        at = len(sent) * sectors * width
+        at = len(sent) * (stop - begin) * width
         out[at : at + height] = values.astype(F32).astype(BF16)
 
 
 def stage_kernel(roles, half, directions_ref, charges_ref, present_ref, left_ref, *refs):
-    outs = refs[: len(roles)]
-    left, directions, charges, present, few, sem = refs[len(roles) :]
+    *outs, left, directions, charges, present, few, sem = refs
+    first = left.shape[1]
     bulk = [
-        pltpu.make_async_copy(left_ref.at[p], left.at[p], sem) for p in range(left.shape[0])
+        pltpu.make_async_copy(left_ref.at[p, pl.ds(0, first)], left.at[p], sem)
+        for p in range(left.shape[0])
     ]
     for copy in bulk:
         copy.start()
@@ -140,51 +142,67 @@
 
 
 def restage_kernel(
-    roles, half, directions_ref, charges_ref, present_ref, left, wave_ref, rot_ref, *refs
+    roles, half, directions_ref, charges_ref, present_ref, left_ref, wave_ref, rot_ref, *refs
 ):
     outs = refs[: len(roles)]
-    wave, rot, directions, charges, present, few, sems = refs[len(roles) :]
+    left, wave, rot, directions, charges, present, few, sems = refs[len(roles) :]
     bulk = [
-        pltpu.make_async_copy(wave_ref, wave, sems.at[0]),
-        pltpu.make_async_copy(rot_ref, rot, sems.at[1]),
+        pltpu.make_async_copy(left_ref, left, sems.at[0]),
+        pltpu.make_async_copy(wave_ref, wave, sems.at[1]),
+        pltpu.make_async_copy(rot_ref, rot, sems.at[2]),
     ]
     for copy in bulk:
         copy.start()
     fetch_scalars(
         [(directions_ref, directions), (charges_ref, charges), (present_ref, present)], few
     )
+    bulk[0].wait()
     copy_pairs(roles, half, outs, left, directions, charges, present)
-    for copy in bulk:
+    for copy in bulk[1:]:
         copy.wait()
 
 
-def staged(token, roles, half, directions, charges, present, left, *more):
-    count, sectors, width, _ = left.shape
+def staged(token, roles, half, directions, charges, present, *bulk):
+    count, sectors, width, _ = bulk[0].shape
     shapes = [
-        (len(sent) * sectors * width + (meta_rows(sectors) if told else 0), width)
-        for sent, told in roles
+        (len(sent) * (stop - begin) * width + (meta_rows(sectors) if told else 0), width)
+        for sent, told, begin, stop in roles
     ]
-    shapes += [x.shape for x in more] if more else [left.shape]
-    operands = [in_hbm(x) for x in (directions, charges, present)]
-    operands += [left, *map(in_hbm, more)] if more else [in_hbm(left)]
+    scratch = [
+        pltpu.SMEM((count,), jnp.int32),
+        pltpu.SMEM((count,), jnp.int32),
+        pltpu.SMEM((count, sectors), jnp.int32),
+        pltpu.SemaphoreType.DMA,
+    ]
+    if token is None:
+        scratch.insert(0, pltpu.VMEM((count, roles[0][3], width, width), BF16))
+        scratch.append(pltpu.SemaphoreType.DMA)
+    else:
+        shapes += [x.shape for x in bulk]
+        scratch.append(pltpu.SemaphoreType.DMA((3,)))
     return kernel_call(
-        functools.partial(restage_kernel if more else stage_kernel, roles, half),
-        token,
-        operands,
-        [HBM] * 3 + ([VMEM] + [HBM] * len(more) if more else [HBM]),
+        functools.partial(stage_kernel if token is None else restage_kernel, roles, half),
+        token,
+        [in_hbm(x) for x in (directions, charges, present, *bulk)],
+        [HBM] * (3 + len(bulk)),
         [pltpu.VMEM(shape, BF16) for shape in shapes],
         [VMEM] * len(shapes),
-        scratch_shapes=[
-            pltpu.SMEM((count,), jnp.int32),
-            pltpu.SMEM((count,), jnp.int32),
-            pltpu.SMEM((count, sectors), jnp.int32),
-            pltpu.SemaphoreType.DMA,
-            pltpu.SemaphoreType.DMA((len(more),)) if more else pltpu.SemaphoreType.DMA,
-        ],
-        mib=4,
+        scratch_shapes=scratch,
+        mib=6,
         cost_estimate=estimate(0),
-        name="restage" if more else "stage",
-    )
+        name="stage" if token is None else "restage",
+    )
+
+
+def grouped_few(sectors):
+    return max(0, sectors // 2 - 1)
+
+
+def grouped(target, sectors):
+    few = grouped_few(sectors)
+    if target in (0, sectors + 1):
+        return 0, min(target, 1)
+    return (0, 1 + target) if target <= few else (1, target - 1 - few)
 
 
 def sigma_kernel(split, chunk, charges_ref, present_ref, left, right_ref, wave, rotations, *refs):
@@ -224,19 +242,18 @@
         to = slice(q * chunk, (q + 1) * chunk)
         for t in range(sectors + 2):
             away = acc[t, pl.ds((2 * q + 1 - bit) * chunk, chunk)].astype(BF16)
-            if 0 < t <= sectors:
-                outs[1][t - 1, to] = away
-            else:
-                outs[0][min(t, 1), to] = away
+            group, place = grouped(t, sectors)
+            outs[group][place, to] = away
             outs[2][t, to] = acc[t, pl.ds((2 * q + bit) * chunk, chunk)]
 
 
 def sigma_terms(token, split, chunk, charges, present, left, right, wave, rotations):
     count, sectors, width, _ = left.shape
     if split:
+        few = grouped_few(sectors)
         shapes = [
-            ((2, width // 2, width), BF16),
-            ((sectors, width // 2, width), BF16),
+            ((2 + few, width // 2, width), BF16),
+            ((sectors - few, width // 2, width), BF16),
             ((sectors + 2, width // 2, width), F32),
         ]
     else:
@@ -290,10 +307,10 @@
 
 def split_kernel(bit, chunk, levels, first, held, *refs):
     if first:
-        got, one, two, send, keep = refs
+        *core, one, two, send, keep = refs
     else:
         got, send, keep = refs
-    sectors, height, _ = got.shape
+    sectors, height = send.shape[0], held.shape[1]
     own = lax.rem(lax.axis_index("op") // bit, 2)
     level = lax.axis_index("sec")
     odd = lax.rem(level, 2) == 1
@@ -301,7 +318,8 @@
     def total(s, rows):
         if not first:
             return held[s, rows] + got[s, rows].astype(F32)
-        value = held[s + 1, rows] + got[s, rows].astype(F32)
+        group, place = grouped(s + 1, sectors)
+        value = held[s + 1, rows] + core[group][place, rows].astype(F32)
         if s == 0:
             below = jnp.where(odd, one[rows], two[rows]).astype(F32)
             value = value + jnp.where(level > 0, below, 0.0)
@@ -317,20 +335,22 @@
             keep[s, to] = total(s, pl.ds((2 * q + own) * chunk, chunk))
 
 
-def split(token, bit, chunk, levels, held, got, *edge):
-    sectors, height, width = got.shape
+def split(token, bit, chunk, levels, held, *got):
+    first = len(got) > 1
+    outer, height, width = held.shape
+    sectors = outer - 2 if first else outer
     return kernel_call(
-        functools.partial(split_kernel, bit, chunk, levels, len(edge) == 2),
-        token,
-        (held, got, *edge),
-        [VMEM] * (2 + len(edge)),
+        functools.partial(split_kernel, bit, chunk, levels, first),
+        token,
+        (held, *got),
+        [VMEM] * (1 + len(got)),
         [
             jax.ShapeDtypeStruct((sectors, height // 2, width), BF16),
             jax.ShapeDtypeStruct((sectors, height // 2, width), F32),
         ],
         [VMEM] * 2,
         mib=4,
-        cost_estimate=estimate(0 if edge else STEP),
+        cost_estimate=estimate(0 if first else 1.3),
         name="split",
     )
 
@@ -354,34 +374,36 @@
     )
 
 
-def choose_kernel(half, cuts, first, second, *outs):
+def choose_kernel(half, parts, lead, front, rear, second, *outs):
     end = at_end(half)
-
-    def fill(source):
-        for out, (at, size) in zip(outs, cuts):
-            out[...] = source[at : at + size]
+    width = second.shape[1]
 
     @pl.when(end)
     def _():
-        fill(first)
+        for out, (begin, stop) in zip(outs, parts):
+            for s in range(begin, stop):
+                source, at = (front, s) if s < lead else (rear, s - lead)
+                out[(s - begin) * width : (s - begin + 1) * width] = source[
+                    at * width : (at + 1) * width
+                ]
 
     @pl.when(jnp.logical_not(end))
     def _():
-        fill(second)
-
-
-def choose(token, half, parts, first, second):
+        for out, (begin, stop) in zip(outs, parts):
+            out[...] = second[begin * width : stop * width]
+
+
+def choose(token, half, parts, lead, front, rear, second):
     width = second.shape[1]
-    cuts = [(begin * width, (stop - begin) * width) for begin, stop in parts]
     return kernel_call(
-        functools.partial(choose_kernel, half, cuts),
-        token,
-        (first, second),
-        [VMEM] * 2,
-        [pltpu.VMEM((size, width), BF16) for _, size in cuts],
-        [VMEM] * len(cuts),
+        functools.partial(choose_kernel, half, parts, lead),
+        token,
+        (front, rear, second),
+        [VMEM] * 3,
+        [pltpu.VMEM(((stop - begin) * width, width), BF16) for begin, stop in parts],
+        [VMEM] * len(parts),
         mib=4,
-        cost_estimate=estimate(0),
+        cost_estimate=estimate(0.9),
         name="choose",
     )
 
@@ -466,7 +488,7 @@
             pltpu.VMEM((count + (1 if zero else 0), *block), BF16),
             pltpu.SemaphoreType.DMA,
         ],
-        mib=8,
+        mib=10,
         cost_estimate=estimate(cost),
         name=name,
     )
@@ -486,7 +508,7 @@
         [jax.ShapeDtypeStruct(keep.shape, F32)],
         [VMEM],
         mib=4,
-        cost_estimate=estimate(STEP),
+        cost_estimate=estimate(0),
         name="finish",
     )
 
@@ -502,7 +524,7 @@
     chunk = width // n
     halving = n >= 4 and n & (n - 1) == 0 and chunk % 16 == 0
     rows = sectors * width
-    parts = [(0, sectors // 2), (sectors // 2, sectors)] if sectors > 1 else [(0, 1)]
+    parts = [(0, 3 * sectors // 4), (3 * sectors // 4, sectors)] if sectors > 1 else [(0, 1)]
 
     def over_op(value, target):
         return lax.ppermute(value, "op", [(i, target(i)) for i in range(n)])
@@ -529,19 +551,28 @@
     ahead_roles = (("extra", "side"), ("half", "extra"))
     behind_roles = (("side", "extra"), ("extra", "half"))
     core_roles = ("extra", "core")
-    token, (ahead, left) = staged(
-        None, ((ahead_roles, ahead_roles),), half, *small, left_operators
-    )
-    token, (behind, last, first_core, wave, turn) = staged(
-        token,
-        ((behind_roles[:1], behind_roles), (("half",), ()), (core_roles, core_roles)),
+    lead = min(2, sectors)
+    whole = (0, sectors)
+    token, (front,) = staged(
+        None, ((ahead_roles, (), 0, lead),), half, *small, left_operators
+    )
+    token, (rear, behind, last, first_core, left, wave, turn) = staged(
+        token,
+        (
+            (ahead_roles, ahead_roles, lead, sectors),
+            (behind_roles[:1], behind_roles, *whole),
+            (("half",), (), *whole),
+            (core_roles, core_roles, *whole),
+        ),
         half,
         *small,
-        left,
+        left_operators,
         wavefunction,
         rotations,
     )
-    got_ahead = over_op(ahead, lambda i: opposite(i) if end(i) else side(i))
+    got_front, got_rear = [
+        over_op(x, lambda i: opposite(i) if end(i) else side(i)) for x in (front, rear)
+    ]
     got_behind = over_op(behind, lambda i: side(i) if end(i) else opposite(i))
     from_core = over_op(first_core, lambda i: i ^ 1)
     token, (*terms, turned) = sigma_terms(
@@ -552,15 +583,16 @@
         send_edges, send, keep = terms
         got_edges = over_op(send_edges, lambda i: i ^ 1)
         got = over_op(send, lambda i: i ^ 1)
+        token, (got_front,) = hold(token, got_front, cost=1.75)
         token, (got,) = hold(token, got)
         token, (first, second) = edges(token, keep, got_edges, turned)
         one, two = swapped(first, 0), swapped(second, 1)
         offset = width // 2
-        token, (one,) = hold(token, one, cost=STEP // 2)
+        token, (one,) = hold(token, one, cost=0.6)
         bit = 2
-        token, (send, keep) = split(token, bit, chunk, levels, keep, got, one, two)
+        token, (send, keep) = split(token, bit, chunk, levels, keep, got_edges, got, one, two)
         got = over_op(send, lambda i: i ^ 2)
-        token, last = choose(token, half, parts, got_ahead, last)
+        token, last = choose(token, half, parts, lead, got_front, got_rear, last)
         while 2 * bit < n:
             bit *= 2
             token, (send, keep) = split(token, bit, chunk, levels, keep, got)
@@ -580,32 +612,31 @@
         mid = mid.at[0].add(jnp.where(level > 0, below, 0.0))
         mid = mid.at[sectors - 1].add(jnp.where(level < levels - 1, above, 0.0))
         summed = lax.psum_scatter(mid, "op", scatter_dimension=1, tiled=True)
-        token, last = choose(token, half, parts, got_ahead, last)
-
-    if len(last) > 1:
-        token, last[1:] = hold(token, *last[1:])
+        token, last = choose(token, half, parts, lead, got_front, got_rear, last)
+
     got_last = [over_op(x, lambda i: relay(i) if end(i) else opposite(i)) for x in last]
     fixed = (offset, levels, half, turned, turn, one, two)
-    whole = (0, sectors)
+    tail = (sectors - lead) * width
+    told = 2 * tail
     token, out = renorm(
         token,
         "renorm_first",
         (
             ((0, 0), (0, 2 * rows, 0), (("core", 1),), *whole),
             ((0, rows), (0, 2 * rows, 1), (("core", 0),), *whole),
-            ((1, 0), (1, 2 * rows, 0), (("half", 1), ("side", 0)), *whole),
-            ((1, rows), (1, 2 * rows, 1), (("half", 0), ("side", 1)), *whole),
-            ((2, 0), (2, rows, 0), (("side", 0), ("half", 1)), *whole),
+            ((1, 0), (2, told, 0), (("half", 1), ("side", 0)), 0, lead),
+            ((2, 0), (2, told, 0), (("half", 1), ("side", 0)), lead, sectors),
+            ((1, lead * width), (2, told, 1), (("half", 0), ("side", 1)), 0, lead),
+            ((2, tail), (2, told, 1), (("half", 0), ("side", 1)), lead, sectors),
+            ((3, 0), (3, rows, 0), (("side", 0), ("half", 1)), *whole),
         ),
-        (from_core, got_ahead, got_behind),
+        (from_core, got_front, got_rear, got_behind),
         None,
         *fixed,
-        cost=STEP,
+        cost=1.75,
     )
     scale = 1.0 / math.sqrt(pairs * n)
     for i, (begin, stop) in enumerate(parts):
-        if halving and i == len(parts) - 1:
-            token, (sigma_vector,) = finish(token, scale, keep, got)
         token, out = renorm(
             token,
             "renorm_last",
@@ -614,7 +645,9 @@
             out,
             *fixed,
         )
-    if not halving:
+    if halving:
+        token, (sigma_vector,) = finish(token, scale, keep, got)
+    else:
         sigma_vector = summed * scale
     return sigma_vector, out
 

time: 37.3 us -> 36.9 us (0.989)
  waiting for transfers between devices: 13.9 us -> 13.3 us
    ppermute x9 -> x10, waiting for transfers between devices: 10.5 us -> 9.3 us  [over_op(): return lax.ppermute(value, 'op', [(i, target(i)) for i in range(n)])]
    ppermute x2, waiting for transfers between devices: 3.45 us -> 4.03 us  [swapped(): return lax.ppermute(value, 'sec', list(enumerate(to)))]
    ppermute x9 -> x10, starting transfers between devices: 8.55 us -> 8.56 us  [over_op(): return lax.ppermute(value, 'op', [(i, target(i)) for i in range(n)])]
  transfers between devices with their start and end apart: 11 -> 12, of which waited for: 7 -> 7; matrix products, arithmetic and copies ran while one was open for 0% -> 0% of each run, Pallas kernels for 25% -> 28%
where the time goes in v6:
time: 36.9 us; the launch traced here: 36.7 us
  waiting for transfers between devices  13.3 us (36%)
  Pallas kernels  12.1 us (33%)
  starting transfers between devices  10.6 us (29%)
  between operations  0.72 us (2%)
    pallas_call x14, Pallas kernels, kernel_call(): pl.pallas_call(run, grid=grid, out_shape=[jax.ShapeDtypeStruct((8, 128),...  12.1 us
    ppermute x10, waiting for transfers between devices, over_op(): return lax.ppermute(value, 'op', [(i, target(i)) for i in range(n)])  9.3 us
    ppermute x10, starting transfers between devices, over_op(): return lax.ppermute(value, 'op', [(i, target(i)) for i in range(n)])  8.56 us
    ppermute x2, waiting for transfers between devices, swapped(): return lax.ppermute(value, 'sec', list(enumerate(to)))  4.03 us
    ppermute x2, starting transfers between devices, swapped(): return lax.ppermute(value, 'sec', list(enumerate(to)))  2.02 us
  transfers between devices with their start and end apart: 12, of which 7 were waited for; matrix products, arithmetic and copies ran while one was open for 0% of the time, Pallas kernels for 28%

profile of v6, /device:TPU:1, one launch (start us, length us, event | category | flops | bytes accessed | tf_op | source)
XLA Modules:
  0.0 36.7 jit_solution(6416855220264961383)
XLA Ops:
  0.6 1.2 %stage.1 = (f32[8,128]{1,0:T(8,128)S(1)}, bf16[1024,256]{1,0:T(8,128)(2,1)S(1)}) custom-call(s32[4]{0:T(128)} %bitcast.1, s32[4]{0:T(128)} %refs_1_.3, s32[4,4]{1,0:T(4,128)} %refs_2_.5, bf16[4,4,256,256]{3,2,1,0:T(8,128)(2,1)} %refs_4_.2), custom_call_target="tpu_custom_call" | custom-call | tf_op jit(solution)/shard_map/stage/pallas_call | solution.py:35
  1.9 2.7 %collective-permute-start = (bf16[1024,256]{1,0:T(8,128)(2,1)S(1)}, bf16[1024,256]{1,0:T(8,128)(2,1)S(1)}, u32[]{:S(2)}, u32[]{:S(2)}) collective-permute-start(bf16[1024,256]{1,0:T(8,128)(2,1)S(1)} %get-tuple-element.48), channel_id=1, source_target_pairs={{0,16},{4,8},{8,4},{12,28},{16,0},{20,24},{24,20},{28,12},{1,17},{... | collective-permute-start | bytes 1572872 | tf_op jit(solution)/shard_map/ppermute | solution.py:530
  4.5 1.9 %restage.1 = (f32[8,128]{1,0:T(8,128)S(1)}, bf16[1040,256]{1,0:T(8,128)(2,1)S(1)}, bf16[1040,256]{1,0:T(8,128)(2,1)S(1)}, bf16[1024,256]{1,0:T(8,128)(2,1)S(1)},...) custom-call(f32[8,128]{1,0:T(8,128)S(1)} %get-tuple-element.42.refs_, ...), custom_call_target="tpu_custom_call" | custom-call | tf_op jit(solution)/shard_map/restage/pallas_call | solution.py:35
  6.4 0.5 %collective-permute-start.7 = (bf16[2064,256]{1,0:T(8,128)(2,1)S(1)}, bf16[2064,256]{1,0:T(8,128)(2,1)S(1)}, u32[]{:S(2)}, u32[]{:S(2)}) collective-permute-start(bf16[2064,256]{1,0:T(8,128)(2,1)S(1)} %get-tuple-element.69), channel_id=1, source_target_pairs={{0,4},{4,0},{8,12},{12,8},{16,20},{20,16},{24,28},{28,24},{1,5},{5... | collective-permute-start | bytes 3170312 | tf_op jit(solution)/shard_map/ppermute | solution.py:530
  6.9 0.7 %collective-permute-start.5 = (bf16[1040,256]{1,0:T(8,128)(2,1)S(1)}, bf16[1040,256]{1,0:T(8,128)(2,1)S(1)}, u32[]{:S(2)}, u32[]{:S(2)}) collective-permute-start(bf16[1040,256]{1,0:T(8,128)(2,1)S(1)} %get-tuple-element.63), channel_id=1, source_target_pairs={{0,16},{4,8},{8,4},{12,28},{16,0},{20,24},{24,20},{28,12},{1,17},{... | collective-permute-start | bytes 1597448 | tf_op jit(solution)/shard_map/ppermute | solution.py:530
  7.6 3.4 %sigma_terms.1 = (f32[8,128]{1,0:T(8,128)S(1)}, bf16[3,128,256]{2,1,0:T(8,128)(2,1)S(1)}, bf16[3,128,256]{2,1,0:T(8,128)(2,1)S(1)}, f32[6,128,256]{2,1,0:T(8,128)S(1)}, bf16[4,256,256]{2,1,0:T(8,128)(2,1)S(1)}) custom-call(f32[8,128]{1,0:T(8,128)S(1)} %get-tuple-element.43.refs_0_, s32[4]{0:T(128)} %refs_1_.3, s32[4,4]{1,0:T(4,128)} %refs_2_.5, ...), custom_call_target="tpu_custom_call" | custom-call | tf_op jit(solution)/shard_map/sigma_terms/pallas_call | solution.py:35
  11.0 1.0 %collective-permute-start.1 = (bf16[3,128,256]{2,1,0:T(8,128)(2,1)S(1)}, bf16[3,128,256]{2,1,0:T(8,128)(2,1)S(1)}, u32[]{:S(2)}, u32[]{:S(2)}) collective-permute-start(bf16[3,128,256]{2,1,0:T(8,128)(2,1)S(1)} %get-tuple-element.50), channel_id=1, source_target_pairs={{0,4},{4,0},{8,12},{12,8},{16,20},{20,16},{24,28},{28,24},{1,5},{5... | collective-permute-start | bytes 589832 | tf_op jit(solution)/shard_map/ppermute | solution.py:530
  12.1 1.0 %collective-permute-done.1.refs_1_ = bf16[3,128,256]{2,1,0:T(8,128)(2,1)S(1)} collective-permute-done((bf16[3,128,256]{2,1,0:T(8,128)(2,1)S(1)}, bf16[3,128,256]{2,1,0:T(8,128)(2,1)S(1)}, u32[]{:S(2)}, u32[]{:S(2)}) %collective-permute-start.1) | collective-permute-done | bytes 196640 | tf_op jit(solution)/shard_map/ppermute | solution.py:530
  13.1 0.4 %collective-permute-done.2.refs_2_ = bf16[3,128,256]{2,1,0:T(8,128)(2,1)S(1)} collective-permute-done((bf16[3,128,256]{2,1,0:T(8,128)(2,1)S(1)}, bf16[3,128,256]{2,1,0:T(8,128)(2,1)S(1)}, u32[]{:S(2)}, u32[]{:S(2)}) %collective-permute-start.2) | collective-permute-done | bytes 196640 | tf_op jit(solution)/shard_map/ppermute | solution.py:530
  13.5 1.4 %collective-permute-start.3 = (bf16[384,256]{1,0:T(8,128)(2,1)S(1)}, bf16[384,256]{1,0:T(8,128)(2,1)S(1)}, u32[]{:S(2)}, u32[]{:S(2)}) collective-permute-start(bf16[384,256]{1,0:T(8,128)(2,1)S(1)} %get-tuple-element.56), channel_id=1, source_target_pairs={{0,1},{1,0},{2,3},{3,2},{4,5},{5,4},{6,7},{7,6},{8,9},{9,8},{10,11... | collective-permute-start | bytes 589832 | tf_op jit(solution)/shard_map/ppermute | solution.py:536
  14.8 0.2 collective-permute-start.8
  15.1 0.7 %collective-permute-start.4 = (bf16[384,256]{1,0:T(8,128)(2,1)S(1)}, bf16[384,256]{1,0:T(8,128)(2,1)S(1)}, u32[]{:S(2)}, u32[]{:S(2)}) collective-permute-start(bf16[384,256]{1,0:T(8,128)(2,1)S(1)} %get-tuple-element.60), channel_id=1, source_target_pairs={{0,0},{1,2},{2,1},{3,3},{4,4},{5,6},{6,5},{7,7},{8,8},{9,10},{10,9... | collective-permute-start | bytes 589832 | tf_op jit(solution)/shard_map/ppermute | solution.py:536
  15.7 4.0 %collective-permute-done.3.refs_1_ = bf16[384,256]{1,0:T(8,128)(2,1)S(1)} collective-permute-done((bf16[384,256]{1,0:T(8,128)(2,1)S(1)}, bf16[384,256]{1,0:T(8,128)(2,1)S(1)}, u32[]{:S(2)}, u32[]{:S(2)}) %collective-permute-start.3) | collective-permute-done | bytes 196640 | tf_op jit(solution)/shard_map/ppermute | solution.py:536
  19.9 0.3 collective-permute-start.6
  20.2 1.0 %collective-permute-start.9 = (bf16[768,256]{1,0:T(8,128)(2,1)S(1)}, bf16[768,256]{1,0:T(8,128)(2,1)S(1)}, u32[]{:S(2)}, u32[]{:S(2)}) collective-permute-start(bf16[768,256]{1,0:T(8,128)(2,1)S(1)} %get-tuple-element.72), channel_id=1, source_target_pairs={{0,12},{4,20},{8,24},{12,0},{16,28},{20,4},{24,8},{28,16},{1,13},{... | collective-permute-start | bytes 1179656 | tf_op jit(solution)/shard_map/ppermute | solution.py:530
  21.2 0.6 %collective-permute-start.10 = (bf16[256,256]{1,0:T(8,128)(2,1)S(1)}, bf16[256,256]{1,0:T(8,128)(2,1)S(1)}, u32[]{:S(2)}, u32[]{:S(2)}) collective-permute-start(bf16[256,256]{1,0:T(8,128)(2,1)S(1)} %get-tuple-element.75), channel_id=1, source_target_pairs={{0,12},{4,20},{8,24},{12,0},{16,28},{20,4},{24,8},{28,16},{1,13},{... | collective-permute-start | bytes 393224 | tf_op jit(solution)/shard_map/ppermute | solution.py:530
  21.8 4.2 %collective-permute-done.6.refs_2_ = bf16[4,64,256]{2,1,0:T(8,128)(2,1)S(1)} collective-permute-done((bf16[4,64,256]{2,1,0:T(8,128)(2,1)S(1)}, bf16[4,64,256]{2,1,0:T(8,128)(2,1)S(1)}, u32[]{:S(2)}, u32[]{:S(2)}) %collective-permute-start.6) | collective-permute-done | bytes 131104 | tf_op jit(solution)/shard_map/ppermute | solution.py:530
  26.0 1.6 %collective-permute-start.11 = (bf16[4,32,256]{2,1,0:T(8,128)(2,1)S(1)}, bf16[4,32,256]{2,1,0:T(8,128)(2,1)S(1)}, u32[]{:S(2)}, u32[]{:S(2)}) collective-permute-start(bf16[4,32,256]{2,1,0:T(8,128)(2,1)S(1)} %get-tuple-element.79), channel_id=1, source_target_pairs={{0,16},{4,20},{8,24},{12,28},{16,0},{20,4},{24,8},{28,12},{1,17},{... | collective-permute-start | bytes 196616 | tf_op jit(solution)/shard_map/ppermute | solution.py:530
  27.5 1.4 %collective-permute-done.8.refs_8_.refs_6_ = bf16[1040,256]{1,0:T(8,128)(2,1)S(1)} collective-permute-done((bf16[1040,256]{1,0:T(8,128)(2,1)S(1)}, bf16[1040,256]{1,0:T(8,128)(2,1)S(1)}, u32[]{:S(2)}, u32[]{:S(2)}) %collective-permute-start.8) | collective-permute-done | bytes 532512 | tf_op jit(solution)/shard_map/ppermute | solution.py:530
  29.0 2.5 %renorm_first.1 = (f32[8,128]{1,0:T(8,128)S(1)}, bf16[8,4,256,256]{3,2,1,0:T(8,128)(2,1)}) custom-call(f32[8,128]{1,0:T(8,128)S(1)} %get-tuple-element.68.refs_0_, bf16[4,256,256]{2,1,0:T(8,128)(2,1)S(1)} %get-tuple-element.54.refs_3_.refs_1_, bf16[4,256,256]{2,1,0:T(8,128)(2,1)S(1)} %get-tuple-element.46.refs_6_.refs_2_, ...), custom_call_target="tpu_custom_call" | custom-call | flops 2018625024 | tf_op jit(solution)/shard_map/renorm_first/pallas_call | solution.py:35
  31.4 2.1 %collective-permute-done.9.refs_5_ = bf16[768,256]{1,0:T(8,128)(2,1)S(1)} collective-permute-done((bf16[768,256]{1,0:T(8,128)(2,1)S(1)}, bf16[768,256]{1,0:T(8,128)(2,1)S(1)}, u32[]{:S(2)}, u32[]{:S(2)}) %collective-permute-start.9) | collective-permute-done | bytes 393248 | tf_op jit(solution)/shard_map/ppermute | solution.py:530
  33.6 1.2 %renorm_last.2 = (f32[8,128]{1,0:T(8,128)S(1)}, bf16[8,4,256,256]{3,2,1,0:T(8,128)(2,1)}) custom-call(f32[8,128]{1,0:T(8,128)S(1)} %get-tuple-element.71.refs_0_, bf16[4,256,256]{2,1,0:T(8,128)(2,1)S(1)} %get-tuple-element.54.refs_3_.refs_1_, bf16[4,256,256]{2,1,0:T(8,128)(2,1)S(1)} %get-tuple-element.46.refs_6_.refs_2_, ...), custom_call_target="tpu_custom_call", output_to_operand_aliasing={{1}: (7, {})} | custom-call | tf_op jit(solution)/shard_map/renorm_last/pallas_call | solution.py:35
  35.0 1.1 %renorm_last.3 = (f32[8,128]{1,0:T(8,128)S(1)}, bf16[8,4,256,256]{3,2,1,0:T(8,128)(2,1)}) custom-call(f32[8,128]{1,0:T(8,128)S(1)} %get-tuple-element.74.refs_0_, bf16[4,256,256]{2,1,0:T(8,128)(2,1)S(1)} %get-tuple-element.54.refs_3_.refs_1_, bf16[4,256,256]{2,1,0:T(8,128)(2,1)S(1)} %get-tuple-element.46.refs_6_.refs_2_, ...), custom_call_target="tpu_custom_call", output_to_operand_aliasing={{1}: (7, {})} | custom-call | tf_op jit(solution)/shard_map/renorm_last/pallas_call | solution.py:35
  36.1 0.7 %finish.1 = (f32[8,128]{1,0:T(8,128)}, f32[4,32,256]{2,1,0:T(8,128)}) custom-call(f32[8,128]{1,0:T(8,128)S(1)} %get-tuple-element.77.refs_0_, f32[4,32,256]{2,1,0:T(8,128)S(1)} %get-tuple-element.78.refs_1_, bf16[4,32,256]{2,1,0:T(8,128)(2,1)S(1)} %collective-permute-done.11.refs_2_), custom_call_target="tpu_custom_call" | custom-call | tf_op jit(solution)/shard_map/finish/pallas_call | solution.py:35
  (14 shorter events, 0.5 us)
Async XLA Ops:
  1.9 10.2 %collective-permute-start = (bf16[1024,256]{1,0:T(8,128)(2,1)S(1)}, bf16[1024,256]{1,0:T(8,128)(2,1)S(1)}, u32[]{:S(2)}, u32[]{:S(2)}) collective-permute-start(bf16[1024,256]{1,0:T(8,128)(2,1)S(1)} %get-tuple-element.48), channel_id=1, source_target_pairs={{0,16},{4,8},{8,4},{12,28},{16,0},{20,24},{24,20},{28,12},{1,17},{... | collective-permute-start | bytes 1572872 | tf_op jit(solution)/shard_map/ppermute | solution.py:530
  6.4 22.5 %collective-permute-start.7 = (bf16[2064,256]{1,0:T(8,128)(2,1)S(1)}, bf16[2064,256]{1,0:T(8,128)(2,1)S(1)}, u32[]{:S(2)}, u32[]{:S(2)}) collective-permute-start(bf16[2064,256]{1,0:T(8,128)(2,1)S(1)} %get-tuple-element.69), channel_id=1, source_target_pairs={{0,4},{4,0},{8,12},{12,8},{16,20},{20,16},{24,28},{28,24},{1,5},{5... | collective-permute-start | bytes 3170312 | tf_op jit(solution)/shard_map/ppermute | solution.py:530
  6.9 13.3 %collective-permute-start.5 = (bf16[1040,256]{1,0:T(8,128)(2,1)S(1)}, bf16[1040,256]{1,0:T(8,128)(2,1)S(1)}, u32[]{:S(2)}, u32[]{:S(2)}) collective-permute-start(bf16[1040,256]{1,0:T(8,128)(2,1)S(1)} %get-tuple-element.63), channel_id=1, source_target_pairs={{0,16},{4,8},{8,4},{12,28},{16,0},{20,24},{24,20},{28,12},{1,17},{... | collective-permute-start | bytes 1597448 | tf_op jit(solution)/shard_map/ppermute | solution.py:530
  11.0 2.1 %collective-permute-start.1 = (bf16[3,128,256]{2,1,0:T(8,128)(2,1)S(1)}, bf16[3,128,256]{2,1,0:T(8,128)(2,1)S(1)}, u32[]{:S(2)}, u32[]{:S(2)}) collective-permute-start(bf16[3,128,256]{2,1,0:T(8,128)(2,1)S(1)} %get-tuple-element.50), channel_id=1, source_target_pairs={{0,4},{4,0},{8,12},{12,8},{16,20},{20,16},{24,28},{28,24},{1,5},{5... | collective-permute-start | bytes 589832 | tf_op jit(solution)/shard_map/ppermute | solution.py:530
  12.0 1.4 %collective-permute-start.2 = (bf16[3,128,256]{2,1,0:T(8,128)(2,1)S(1)}, bf16[3,128,256]{2,1,0:T(8,128)(2,1)S(1)}, u32[]{:S(2)}, u32[]{:S(2)}) collective-permute-start(bf16[3,128,256]{2,1,0:T(8,128)(2,1)S(1)} %get-tuple-element.53), channel_id=1, source_target_pairs={{0,4},{4,0},{8,12},{12,8},{16,20},{20,16},{24,28},{28,24},{1,5},{5... | collective-permute-start | bytes 589832 | tf_op jit(solution)/shard_map/ppermute | solution.py:530
  13.5 6.3 %collective-permute-start.3 = (bf16[384,256]{1,0:T(8,128)(2,1)S(1)}, bf16[384,256]{1,0:T(8,128)(2,1)S(1)}, u32[]{:S(2)}, u32[]{:S(2)}) collective-permute-start(bf16[384,256]{1,0:T(8,128)(2,1)S(1)} %get-tuple-element.56), channel_id=1, source_target_pairs={{0,1},{1,0},{2,3},{3,2},{4,5},{5,4},{6,7},{7,6},{8,9},{9,8},{10,11... | collective-permute-start | bytes 589832 | tf_op jit(solution)/shard_map/ppermute | solution.py:536
  14.8 14.1 %collective-permute-start.8 = (bf16[1040,256]{1,0:T(8,128)(2,1)S(1)}, bf16[1040,256]{1,0:T(8,128)(2,1)S(1)}, u32[]{:S(2)}, u32[]{:S(2)}) collective-permute-start(bf16[1040,256]{1,0:T(8,128)(2,1)S(1)} %get-tuple-element.70), channel_id=1, source_target_pairs={{0,28},{4,20},{8,24},{12,16},{16,12},{20,4},{24,8},{28,0},{1,29},{... | collective-permute-start | bytes 1597448 | tf_op jit(solution)/shard_map/ppermute | solution.py:530
  15.1 4.7 %collective-permute-start.4 = (bf16[384,256]{1,0:T(8,128)(2,1)S(1)}, bf16[384,256]{1,0:T(8,128)(2,1)S(1)}, u32[]{:S(2)}, u32[]{:S(2)}) collective-permute-start(bf16[384,256]{1,0:T(8,128)(2,1)S(1)} %get-tuple-element.60), channel_id=1, source_target_pairs={{0,0},{1,2},{2,1},{3,3},{4,4},{5,6},{6,5},{7,7},{8,8},{9,10},{10,9... | collective-permute-start | bytes 589832 | tf_op jit(solution)/shard_map/ppermute | solution.py:536
  19.9 6.1 %collective-permute-start.6 = (bf16[4,64,256]{2,1,0:T(8,128)(2,1)S(1)}, bf16[4,64,256]{2,1,0:T(8,128)(2,1)S(1)}, u32[]{:S(2)}, u32[]{:S(2)}) collective-permute-start(bf16[4,64,256]{2,1,0:T(8,128)(2,1)S(1)} %get-tuple-element.67), channel_id=1, source_target_pairs={{0,8},{4,12},{8,0},{12,4},{16,24},{20,28},{24,16},{28,20},{1,9},{5... | collective-permute-start | bytes 393224 | tf_op jit(solution)/shard_map/ppermute | solution.py:530
  20.2 13.4 %collective-permute-start.9 = (bf16[768,256]{1,0:T(8,128)(2,1)S(1)}, bf16[768,256]{1,0:T(8,128)(2,1)S(1)}, u32[]{:S(2)}, u32[]{:S(2)}) collective-permute-start(bf16[768,256]{1,0:T(8,128)(2,1)S(1)} %get-tuple-element.72), channel_id=1, source_target_pairs={{0,12},{4,20},{8,24},{12,0},{16,28},{20,4},{24,8},{28,16},{1,13},{... | collective-permute-start | bytes 1179656 | tf_op jit(solution)/shard_map/ppermute | solution.py:530
  21.2 13.8 %collective-permute-start.10 = (bf16[256,256]{1,0:T(8,128)(2,1)S(1)}, bf16[256,256]{1,0:T(8,128)(2,1)S(1)}, u32[]{:S(2)}, u32[]{:S(2)}) collective-permute-start(bf16[256,256]{1,0:T(8,128)(2,1)S(1)} %get-tuple-element.75), channel_id=1, source_target_pairs={{0,12},{4,20},{8,24},{12,0},{16,28},{20,4},{24,8},{28,16},{1,13},{... | collective-permute-start | bytes 393224 | tf_op jit(solution)/shard_map/ppermute | solution.py:530
  26.0 10.1 %collective-permute-start.11 = (bf16[4,32,256]{2,1,0:T(8,128)(2,1)S(1)}, bf16[4,32,256]{2,1,0:T(8,128)(2,1)S(1)}, u32[]{:S(2)}, u32[]{:S(2)}) collective-permute-start(bf16[4,32,256]{2,1,0:T(8,128)(2,1)S(1)} %get-tuple-element.79), channel_id=1, source_target_pairs={{0,16},{4,20},{8,24},{12,28},{16,0},{20,4},{24,8},{28,12},{1,17},{... | collective-permute-start | bytes 196616 | tf_op jit(solution)/shard_map/ppermute | solution.py:530

commit v7 on v6

--- a/solution.py
+++ b/solution.py
@@ -78,7 +78,7 @@
     return index
 
 
-def copy_pairs(roles, half, outs, left, directions, charges, present):
+def copy_pairs(roles, half, outs, left, directions, charges, present, arrived=None):
     count, _, width, _ = left.shape
     sectors = present.shape[1]
     kinds = [directions[p] for p in range(count)]
@@ -103,9 +103,11 @@
     height = meta_rows(sectors)
     row = lax.broadcasted_iota(jnp.int32, (height, width), 0)
     for out, (sent, told, begin, stop) in zip(outs, roles):
-        for i, role in enumerate(sent):
-            index = index_of(role)
-            for s in range(begin, stop):
+        indices = [index_of(role) for role in sent]
+        for s in range(begin, stop):
+            if arrived is not None:
+                arrived(s)
+            for i, index in enumerate(indices):
                 at = (i * (stop - begin) + s - begin) * width
                 out[at : at + width] = left[index, s]
         if not told:
@@ -125,20 +127,17 @@
 
 
 def stage_kernel(roles, half, directions_ref, charges_ref, present_ref, left_ref, *refs):
-    *outs, left, directions, charges, present, few, sem = refs
-    first = left.shape[1]
+    *outs, left, directions, charges, present, few, sems = refs
     bulk = [
-        pltpu.make_async_copy(left_ref.at[p, pl.ds(0, first)], left.at[p], sem)
-        for p in range(left.shape[0])
+        pltpu.make_async_copy(left_ref.at[:, s], left.at[:, s], sems.at[s])
+        for s in range(left.shape[1])
     ]
     for copy in bulk:
         copy.start()
-    fetch_scalars(
-        [(directions_ref, directions), (charges_ref, charges), (present_ref, present)], few
-    )
-    for copy in bulk:
-        copy.wait()
-    copy_pairs(roles, half, outs, left, directions, charges, present)
+    fetch_scalars([(directions_ref, directions)], few)
+    copy_pairs(
+        roles, half, outs, left, directions, charges, present, lambda s: bulk[s].wait()
+    )
 
 
 def restage_kernel(
@@ -176,7 +175,7 @@
     ]
     if token is None:
         scratch.insert(0, pltpu.VMEM((count, roles[0][3], width, width), BF16))
-        scratch.append(pltpu.SemaphoreType.DMA)
+        scratch.append(pltpu.SemaphoreType.DMA((roles[0][3],)))
     else:
         shapes += [x.shape for x in bulk]
         scratch.append(pltpu.SemaphoreType.DMA((3,)))
@@ -408,16 +407,48 @@
     )
 
 
-def renorm_kernel(items, zero, offset, levels, half, turned, rotations, one, two, *refs):
+def frame_kernel(offset, turned, one, two, framed):
+    sectors, width, _ = turned.shape
+    raised = lax.rem(lax.axis_index("sec"), 2) == 1
+    rows = pl.ds(offset, width)
+
+    @pl.when(raised)
+    def _():
+        framed[0] = one[rows]
+        framed[sectors + 1] = two[rows]
+
+    @pl.when(jnp.logical_not(raised))
+    def _():
+        framed[0] = two[rows]
+        framed[sectors + 1] = one[rows]
+
+    for s in range(sectors):
+        framed[s + 1] = turned[s]
+
+
+def frame(token, offset, turned, one, two):
+    sectors, width, _ = turned.shape
+    return kernel_call(
+        functools.partial(frame_kernel, offset),
+        token,
+        (turned, one, two),
+        [VMEM] * 3,
+        [pltpu.VMEM((sectors + 2, width, width), BF16)],
+        [VMEM],
+        mib=4,
+        cost_estimate=estimate(0),
+        name="frame",
+    )
+
+
+def renorm_kernel(items, zero, levels, half, framed, rotations, *refs):
     buffers = refs[: 1 + max(buffer for came, told, *_ in items for buffer in (came[0], told[0]))]
     rest = refs[len(buffers) + (0 if zero else 1) :]
-    out, edge, results, done = rest
+    out, results, done = rest
     sectors, width, _ = rotations.shape
     odd = lax.rem(lax.axis_index("op"), 2)
     end = at_end(half)
     level = lax.axis_index("sec")
-    raised = lax.rem(level, 2) == 1
-    rows = pl.ds(offset, width)
     height = meta_rows(sectors)
     stores = []
     if zero:
@@ -426,10 +457,6 @@
             copy = pltpu.make_async_copy(results.at[len(items)], out.at[place], done)
             copy.start()
             stores.append(copy)
-    if any(begin == 0 for *_, begin, _ in items):
-        edge[0] = jnp.where(raised, one[rows], two[rows])
-    if any(stop == sectors for *_, stop in items):
-        edge[1] = jnp.where(raised, two[rows], one[rows])
     kinds = {"core": 2 - odd, "side": 1 + odd, "half": 3}
     for i, ((buffer, base), (about, top, slot), targets, begin, stop) in enumerate(items):
         values = buffers[about][pl.ds(top, height)].astype(F32)
@@ -449,11 +476,7 @@
             weight = jnp.where(inside, weights[s : s + 1], 0.0)
             block = buffers[buffer][pl.ds(base + (s - begin) * width, width)]
             rotated = jnp.dot(block, rotations[s], preferred_element_type=F32).astype(BF16)
-            target = turned[jnp.clip(at, 0, sectors - 1)]
-            if s == 0:
-                target = jnp.where(at < 0, edge[0], target)
-            if s == sectors - 1:
-                target = jnp.where(at > sectors - 1, edge[1], target)
+            target = framed[jnp.clip(at + 1, 0, sectors + 1)]
             value = jnp.dot(target, rotated, preferred_element_type=F32) * weight
             results[i, s] = value.astype(BF16)
             copy = pltpu.make_async_copy(results.at[i, s], out.at[kind * CAPS + place, s], done)
@@ -464,11 +487,11 @@
 
 
 def renorm(
-    token, name, items, buffers, out, offset, levels, half, turned, rotations, one, two, cost=0
+    token, name, items, buffers, out, levels, half, framed, rotations, cost=0
 ):
     sectors, width, _ = rotations.shape
     zero = out is None
-    operands = [turned, rotations, one, two, *buffers]
+    operands = [framed, rotations, *buffers]
     in_specs = [VMEM] * len(operands)
     if not zero:
         operands.append(out)
@@ -476,7 +499,7 @@
     count = len(items)
     block = (sectors, width, width)
     token, (out,) = kernel_call(
-        functools.partial(renorm_kernel, items, zero, offset, levels, half),
+        functools.partial(renorm_kernel, items, zero, levels, half),
         token,
         operands,
         in_specs,
@@ -484,7 +507,6 @@
         [HBM],
         aliases={} if zero else {len(operands) - 1: 0},
         scratch_shapes=[
-            pltpu.VMEM((2, width, width), BF16),
             pltpu.VMEM((count + (1 if zero else 0), *block), BF16),
             pltpu.SemaphoreType.DMA,
         ],
@@ -592,6 +614,7 @@
         bit = 2
         token, (send, keep) = split(token, bit, chunk, levels, keep, got_edges, got, one, two)
         got = over_op(send, lambda i: i ^ 2)
+        token, (framed,) = frame(token, offset, turned, one, two)
         token, last = choose(token, half, parts, lead, got_front, got_rear, last)
         while 2 * bit < n:
             bit *= 2
@@ -612,10 +635,11 @@
         mid = mid.at[0].add(jnp.where(level > 0, below, 0.0))
         mid = mid.at[sectors - 1].add(jnp.where(level < levels - 1, above, 0.0))
         summed = lax.psum_scatter(mid, "op", scatter_dimension=1, tiled=True)
+        token, (framed,) = frame(token, offset, turned, one, two)
         token, last = choose(token, half, parts, lead, got_front, got_rear, last)
 
     got_last = [over_op(x, lambda i: relay(i) if end(i) else opposite(i)) for x in last]
-    fixed = (offset, levels, half, turned, turn, one, two)
+    fixed = (levels, half, framed, turn)
     tail = (sectors - lead) * width
     told = 2 * tail
     token, out = renorm(

time: 36.9 us -> 36.9 us (level)
    pallas_call x14 -> x15, Pallas kernels: 12.1 us -> 12.2 us  [kernel_call(): pl.pallas_call(run, grid=grid, out_shape=[jax.ShapeDtypeStruct((8, 128),...]
where the time goes in v7:
time: 36.9 us; the launch traced here: 36.7 us
  waiting for transfers between devices  13.3 us (36%)
  Pallas kernels  12.2 us (33%)
  starting transfers between devices  10.6 us (29%)
  between operations  0.73 us (2%)
    pallas_call x15, Pallas kernels, kernel_call(): pl.pallas_call(run, grid=grid, out_shape=[jax.ShapeDtypeStruct((8, 128),...  12.2 us
    ppermute x10, waiting for transfers between devices, over_op(): return lax.ppermute(value, 'op', [(i, target(i)) for i in range(n)])  9.23 us
    ppermute x10, starting transfers between devices, over_op(): return lax.ppermute(value, 'op', [(i, target(i)) for i in range(n)])  8.57 us
    ppermute x2, waiting for transfers between devices, swapped(): return lax.ppermute(value, 'sec', list(enumerate(to)))  4.03 us
    ppermute x2, starting transfers between devices, swapped(): return lax.ppermute(value, 'sec', list(enumerate(to)))  2.02 us
  transfers between devices with their start and end apart: 12, of which 7 were waited for; matrix products, arithmetic and copies ran while one was open for 0% of the time, Pallas kernels for 28%

profile of v7, /device:TPU:1, one launch (start us, length us, event | category | flops | bytes accessed | tf_op | source)
XLA Modules:
  0.0 36.7 jit_solution(7100586396861466839)
XLA Ops:
  0.6 1.2 %stage.1 = (f32[8,128]{1,0:T(8,128)S(1)}, bf16[1024,256]{1,0:T(8,128)(2,1)S(1)}) custom-call(s32[4]{0:T(128)} %bitcast.1, s32[4]{0:T(128)} %refs_1_.3, s32[4,4]{1,0:T(4,128)} %refs_2_.5, bf16[4,4,256,256]{3,2,1,0:T(8,128)(2,1)} %refs_4_.2), custom_call_target="tpu_custom_call" | custom-call | tf_op jit(solution)/shard_map/stage/pallas_call | solution.py:35
  1.9 2.7 %collective-permute-start = (bf16[1024,256]{1,0:T(8,128)(2,1)S(1)}, bf16[1024,256]{1,0:T(8,128)(2,1)S(1)}, u32[]{:S(2)}, u32[]{:S(2)}) collective-permute-start(bf16[1024,256]{1,0:T(8,128)(2,1)S(1)} %get-tuple-element.50), channel_id=1, source_target_pairs={{0,16},{4,8},{8,4},{12,28},{16,0},{20,24},{24,20},{28,12},{1,17},{... | collective-permute-start | bytes 1572872 | tf_op jit(solution)/shard_map/ppermute | solution.py:552
  4.5 1.9 %restage.1 = (f32[8,128]{1,0:T(8,128)S(1)}, bf16[1040,256]{1,0:T(8,128)(2,1)S(1)}, bf16[1040,256]{1,0:T(8,128)(2,1)S(1)}, bf16[1024,256]{1,0:T(8,128)(2,1)S(1)},...) custom-call(f32[8,128]{1,0:T(8,128)S(1)} %get-tuple-element.44.refs_, ...), custom_call_target="tpu_custom_call" | custom-call | tf_op jit(solution)/shard_map/restage/pallas_call | solution.py:35
  6.4 0.5 %collective-permute-start.7 = (bf16[2064,256]{1,0:T(8,128)(2,1)S(1)}, bf16[2064,256]{1,0:T(8,128)(2,1)S(1)}, u32[]{:S(2)}, u32[]{:S(2)}) collective-permute-start(bf16[2064,256]{1,0:T(8,128)(2,1)S(1)} %get-tuple-element.73), channel_id=1, source_target_pairs={{0,4},{4,0},{8,12},{12,8},{16,20},{20,16},{24,28},{28,24},{1,5},{5... | collective-permute-start | bytes 3170312 | tf_op jit(solution)/shard_map/ppermute | solution.py:552
  6.9 0.7 %collective-permute-start.5 = (bf16[1040,256]{1,0:T(8,128)(2,1)S(1)}, bf16[1040,256]{1,0:T(8,128)(2,1)S(1)}, u32[]{:S(2)}, u32[]{:S(2)}) collective-permute-start(bf16[1040,256]{1,0:T(8,128)(2,1)S(1)} %get-tuple-element.66), channel_id=1, source_target_pairs={{0,16},{4,8},{8,4},{12,28},{16,0},{20,24},{24,20},{28,12},{1,17},{... | collective-permute-start | bytes 1597448 | tf_op jit(solution)/shard_map/ppermute | solution.py:552
  7.6 3.4 %sigma_terms.1 = (f32[8,128]{1,0:T(8,128)S(1)}, bf16[3,128,256]{2,1,0:T(8,128)(2,1)S(1)}, bf16[3,128,256]{2,1,0:T(8,128)(2,1)S(1)}, f32[6,128,256]{2,1,0:T(8,128)S(1)}, bf16[4,256,256]{2,1,0:T(8,128)(2,1)S(1)}) custom-call(f32[8,128]{1,0:T(8,128)S(1)} %get-tuple-element.45.refs_0_, s32[4]{0:T(128)} %refs_1_.3, s32[4,4]{1,0:T(4,128)} %refs_2_.5, ...), custom_call_target="tpu_custom_call" | custom-call | tf_op jit(solution)/shard_map/sigma_terms/pallas_call | solution.py:35
  11.0 1.0 %collective-permute-start.1 = (bf16[3,128,256]{2,1,0:T(8,128)(2,1)S(1)}, bf16[3,128,256]{2,1,0:T(8,128)(2,1)S(1)}, u32[]{:S(2)}, u32[]{:S(2)}) collective-permute-start(bf16[3,128,256]{2,1,0:T(8,128)(2,1)S(1)} %get-tuple-element.52), channel_id=1, source_target_pairs={{0,4},{4,0},{8,12},{12,8},{16,20},{20,16},{24,28},{28,24},{1,5},{5... | collective-permute-start | bytes 589832 | tf_op jit(solution)/shard_map/ppermute | solution.py:552
  12.1 1.0 %collective-permute-done.1.refs_1_ = bf16[3,128,256]{2,1,0:T(8,128)(2,1)S(1)} collective-permute-done((bf16[3,128,256]{2,1,0:T(8,128)(2,1)S(1)}, bf16[3,128,256]{2,1,0:T(8,128)(2,1)S(1)}, u32[]{:S(2)}, u32[]{:S(2)}) %collective-permute-start.1) | collective-permute-done | bytes 196640 | tf_op jit(solution)/shard_map/ppermute | solution.py:552
  13.1 0.4 %collective-permute-done.2.refs_2_ = bf16[3,128,256]{2,1,0:T(8,128)(2,1)S(1)} collective-permute-done((bf16[3,128,256]{2,1,0:T(8,128)(2,1)S(1)}, bf16[3,128,256]{2,1,0:T(8,128)(2,1)S(1)}, u32[]{:S(2)}, u32[]{:S(2)}) %collective-permute-start.2) | collective-permute-done | bytes 196640 | tf_op jit(solution)/shard_map/ppermute | solution.py:552
  13.5 1.4 %collective-permute-start.3 = (bf16[384,256]{1,0:T(8,128)(2,1)S(1)}, bf16[384,256]{1,0:T(8,128)(2,1)S(1)}, u32[]{:S(2)}, u32[]{:S(2)}) collective-permute-start(bf16[384,256]{1,0:T(8,128)(2,1)S(1)} %get-tuple-element.58), channel_id=1, source_target_pairs={{0,1},{1,0},{2,3},{3,2},{4,5},{5,4},{6,7},{7,6},{8,9},{9,8},{10,11... | collective-permute-start | bytes 589832 | tf_op jit(solution)/shard_map/ppermute | solution.py:558
  14.8 0.2 collective-permute-start.8
  15.1 0.7 %collective-permute-start.4 = (bf16[384,256]{1,0:T(8,128)(2,1)S(1)}, bf16[384,256]{1,0:T(8,128)(2,1)S(1)}, u32[]{:S(2)}, u32[]{:S(2)}) collective-permute-start(bf16[384,256]{1,0:T(8,128)(2,1)S(1)} %get-tuple-element.62), channel_id=1, source_target_pairs={{0,0},{1,2},{2,1},{3,3},{4,4},{5,6},{6,5},{7,7},{8,8},{9,10},{10,9... | collective-permute-start | bytes 589832 | tf_op jit(solution)/shard_map/ppermute | solution.py:558
  15.7 4.0 %collective-permute-done.3.refs_1_ = bf16[384,256]{1,0:T(8,128)(2,1)S(1)} collective-permute-done((bf16[384,256]{1,0:T(8,128)(2,1)S(1)}, bf16[384,256]{1,0:T(8,128)(2,1)S(1)}, u32[]{:S(2)}, u32[]{:S(2)}) %collective-permute-start.3) | collective-permute-done | bytes 196640 | tf_op jit(solution)/shard_map/ppermute | solution.py:558
  19.8 0.3 collective-permute-start.6
  20.3 1.0 %collective-permute-start.9 = (bf16[768,256]{1,0:T(8,128)(2,1)S(1)}, bf16[768,256]{1,0:T(8,128)(2,1)S(1)}, u32[]{:S(2)}, u32[]{:S(2)}) collective-permute-start(bf16[768,256]{1,0:T(8,128)(2,1)S(1)} %get-tuple-element.76), channel_id=1, source_target_pairs={{0,12},{4,20},{8,24},{12,0},{16,28},{20,4},{24,8},{28,16},{1,13},{... | collective-permute-start | bytes 1179656 | tf_op jit(solution)/shard_map/ppermute | solution.py:552
  21.3 0.6 %collective-permute-start.10 = (bf16[256,256]{1,0:T(8,128)(2,1)S(1)}, bf16[256,256]{1,0:T(8,128)(2,1)S(1)}, u32[]{:S(2)}, u32[]{:S(2)}) collective-permute-start(bf16[256,256]{1,0:T(8,128)(2,1)S(1)} %get-tuple-element.79), channel_id=1, source_target_pairs={{0,12},{4,20},{8,24},{12,0},{16,28},{20,4},{24,8},{28,16},{1,13},{... | collective-permute-start | bytes 393224 | tf_op jit(solution)/shard_map/ppermute | solution.py:552
  21.8 4.1 %collective-permute-done.6.refs_2_ = bf16[4,64,256]{2,1,0:T(8,128)(2,1)S(1)} collective-permute-done((bf16[4,64,256]{2,1,0:T(8,128)(2,1)S(1)}, bf16[4,64,256]{2,1,0:T(8,128)(2,1)S(1)}, u32[]{:S(2)}, u32[]{:S(2)}) %collective-permute-start.6) | collective-permute-done | bytes 131104 | tf_op jit(solution)/shard_map/ppermute | solution.py:552
  25.9 1.6 %collective-permute-start.11 = (bf16[4,32,256]{2,1,0:T(8,128)(2,1)S(1)}, bf16[4,32,256]{2,1,0:T(8,128)(2,1)S(1)}, u32[]{:S(2)}, u32[]{:S(2)}) collective-permute-start(bf16[4,32,256]{2,1,0:T(8,128)(2,1)S(1)} %get-tuple-element.83), channel_id=1, source_target_pairs={{0,16},{4,20},{8,24},{12,28},{16,0},{20,4},{24,8},{28,12},{1,17},{... | collective-permute-start | bytes 196616 | tf_op jit(solution)/shard_map/ppermute | solution.py:552
  27.5 1.4 %collective-permute-done.8.refs_6_.refs_4_ = bf16[1040,256]{1,0:T(8,128)(2,1)S(1)} collective-permute-done((bf16[1040,256]{1,0:T(8,128)(2,1)S(1)}, bf16[1040,256]{1,0:T(8,128)(2,1)S(1)}, u32[]{:S(2)}, u32[]{:S(2)}) %collective-permute-start.8) | collective-permute-done | bytes 532512 | tf_op jit(solution)/shard_map/ppermute | solution.py:552
  29.0 2.4 %renorm_first.1 = (f32[8,128]{1,0:T(8,128)S(1)}, bf16[8,4,256,256]{3,2,1,0:T(8,128)(2,1)}) custom-call(f32[8,128]{1,0:T(8,128)S(1)} %get-tuple-element.71.refs_0_, bf16[6,256,256]{2,1,0:T(8,128)(2,1)S(1)} %get-tuple-element.72.refs_1_, bf16[4,256,256]{2,1,0:T(8,128)(2,1)S(1)} %get-tuple-element.48.refs_6_.refs_2_, ...), custom_call_target="tpu_custom_call" | custom-call | flops 2018625024 | tf_op jit(solution)/shard_map/renorm_first/pallas_call | solution.py:35
  31.4 2.2 %collective-permute-done.9.refs_3_ = bf16[768,256]{1,0:T(8,128)(2,1)S(1)} collective-permute-done((bf16[768,256]{1,0:T(8,128)(2,1)S(1)}, bf16[768,256]{1,0:T(8,128)(2,1)S(1)}, u32[]{:S(2)}, u32[]{:S(2)}) %collective-permute-start.9) | collective-permute-done | bytes 393248 | tf_op jit(solution)/shard_map/ppermute | solution.py:552
  33.6 1.2 %renorm_last.2 = (f32[8,128]{1,0:T(8,128)S(1)}, bf16[8,4,256,256]{3,2,1,0:T(8,128)(2,1)}) custom-call(f32[8,128]{1,0:T(8,128)S(1)} %get-tuple-element.75.refs_0_, bf16[6,256,256]{2,1,0:T(8,128)(2,1)S(1)} %get-tuple-element.72.refs_1_, bf16[4,256,256]{2,1,0:T(8,128)(2,1)S(1)} %get-tuple-element.48.refs_6_.refs_2_, ...), custom_call_target="tpu_custom_call", output_to_operand_aliasing={{1}: (5, {})} | custom-call | tf_op jit(solution)/shard_map/renorm_last/pallas_call | solution.py:35
  35.0 1.1 %renorm_last.3 = (f32[8,128]{1,0:T(8,128)S(1)}, bf16[8,4,256,256]{3,2,1,0:T(8,128)(2,1)}) custom-call(f32[8,128]{1,0:T(8,128)S(1)} %get-tuple-element.78.refs_0_, bf16[6,256,256]{2,1,0:T(8,128)(2,1)S(1)} %get-tuple-element.72.refs_1_, bf16[4,256,256]{2,1,0:T(8,128)(2,1)S(1)} %get-tuple-element.48.refs_6_.refs_2_, ...), custom_call_target="tpu_custom_call", output_to_operand_aliasing={{1}: (5, {})} | custom-call | tf_op jit(solution)/shard_map/renorm_last/pallas_call | solution.py:35
  36.1 0.7 %finish.1 = (f32[8,128]{1,0:T(8,128)}, f32[4,32,256]{2,1,0:T(8,128)}) custom-call(f32[8,128]{1,0:T(8,128)S(1)} %get-tuple-element.81.refs_0_, f32[4,32,256]{2,1,0:T(8,128)S(1)} %get-tuple-element.82.refs_1_, bf16[4,32,256]{2,1,0:T(8,128)(2,1)S(1)} %collective-permute-done.11.refs_2_), custom_call_target="tpu_custom_call" | custom-call | tf_op jit(solution)/shard_map/finish/pallas_call | solution.py:35
  (15 shorter events, 0.5 us)
Async XLA Ops:
  1.9 10.2 %collective-permute-start = (bf16[1024,256]{1,0:T(8,128)(2,1)S(1)}, bf16[1024,256]{1,0:T(8,128)(2,1)S(1)}, u32[]{:S(2)}, u32[]{:S(2)}) collective-permute-start(bf16[1024,256]{1,0:T(8,128)(2,1)S(1)} %get-tuple-element.50), channel_id=1, source_target_pairs={{0,16},{4,8},{8,4},{12,28},{16,0},{20,24},{24,20},{28,12},{1,17},{... | collective-permute-start | bytes 1572872 | tf_op jit(solution)/shard_map/ppermute | solution.py:552
  6.4 22.5 %collective-permute-start.7 = (bf16[2064,256]{1,0:T(8,128)(2,1)S(1)}, bf16[2064,256]{1,0:T(8,128)(2,1)S(1)}, u32[]{:S(2)}, u32[]{:S(2)}) collective-permute-start(bf16[2064,256]{1,0:T(8,128)(2,1)S(1)} %get-tuple-element.73), channel_id=1, source_target_pairs={{0,4},{4,0},{8,12},{12,8},{16,20},{20,16},{24,28},{28,24},{1,5},{5... | collective-permute-start | bytes 3170312 | tf_op jit(solution)/shard_map/ppermute | solution.py:552
  6.9 13.3 %collective-permute-start.5 = (bf16[1040,256]{1,0:T(8,128)(2,1)S(1)}, bf16[1040,256]{1,0:T(8,128)(2,1)S(1)}, u32[]{:S(2)}, u32[]{:S(2)}) collective-permute-start(bf16[1040,256]{1,0:T(8,128)(2,1)S(1)} %get-tuple-element.66), channel_id=1, source_target_pairs={{0,16},{4,8},{8,4},{12,28},{16,0},{20,24},{24,20},{28,12},{1,17},{... | collective-permute-start | bytes 1597448 | tf_op jit(solution)/shard_map/ppermute | solution.py:552
  11.0 2.1 %collective-permute-start.1 = (bf16[3,128,256]{2,1,0:T(8,128)(2,1)S(1)}, bf16[3,128,256]{2,1,0:T(8,128)(2,1)S(1)}, u32[]{:S(2)}, u32[]{:S(2)}) collective-permute-start(bf16[3,128,256]{2,1,0:T(8,128)(2,1)S(1)} %get-tuple-element.52), channel_id=1, source_target_pairs={{0,4},{4,0},{8,12},{12,8},{16,20},{20,16},{24,28},{28,24},{1,5},{5... | collective-permute-start | bytes 589832 | tf_op jit(solution)/shard_map/ppermute | solution.py:552
  12.0 1.4 %collective-permute-start.2 = (bf16[3,128,256]{2,1,0:T(8,128)(2,1)S(1)}, bf16[3,128,256]{2,1,0:T(8,128)(2,1)S(1)}, u32[]{:S(2)}, u32[]{:S(2)}) collective-permute-start(bf16[3,128,256]{2,1,0:T(8,128)(2,1)S(1)} %get-tuple-element.55), channel_id=1, source_target_pairs={{0,4},{4,0},{8,12},{12,8},{16,20},{20,16},{24,28},{28,24},{1,5},{5... | collective-permute-start | bytes 589832 | tf_op jit(solution)/shard_map/ppermute | solution.py:552
  13.5 6.3 %collective-permute-start.3 = (bf16[384,256]{1,0:T(8,128)(2,1)S(1)}, bf16[384,256]{1,0:T(8,128)(2,1)S(1)}, u32[]{:S(2)}, u32[]{:S(2)}) collective-permute-start(bf16[384,256]{1,0:T(8,128)(2,1)S(1)} %get-tuple-element.58), channel_id=1, source_target_pairs={{0,1},{1,0},{2,3},{3,2},{4,5},{5,4},{6,7},{7,6},{8,9},{9,8},{10,11... | collective-permute-start | bytes 589832 | tf_op jit(solution)/shard_map/ppermute | solution.py:558
  14.8 14.1 %collective-permute-start.8 = (bf16[1040,256]{1,0:T(8,128)(2,1)S(1)}, bf16[1040,256]{1,0:T(8,128)(2,1)S(1)}, u32[]{:S(2)}, u32[]{:S(2)}) collective-permute-start(bf16[1040,256]{1,0:T(8,128)(2,1)S(1)} %get-tuple-element.74), channel_id=1, source_target_pairs={{0,28},{4,20},{8,24},{12,16},{16,12},{20,4},{24,8},{28,0},{1,29},{... | collective-permute-start | bytes 1597448 | tf_op jit(solution)/shard_map/ppermute | solution.py:552
  15.1 4.7 %collective-permute-start.4 = (bf16[384,256]{1,0:T(8,128)(2,1)S(1)}, bf16[384,256]{1,0:T(8,128)(2,1)S(1)}, u32[]{:S(2)}, u32[]{:S(2)}) collective-permute-start(bf16[384,256]{1,0:T(8,128)(2,1)S(1)} %get-tuple-element.62), channel_id=1, source_target_pairs={{0,0},{1,2},{2,1},{3,3},{4,4},{5,6},{6,5},{7,7},{8,8},{9,10},{10,9... | collective-permute-start | bytes 589832 | tf_op jit(solution)/shard_map/ppermute | solution.py:558
  19.8 6.1 %collective-permute-start.6 = (bf16[4,64,256]{2,1,0:T(8,128)(2,1)S(1)}, bf16[4,64,256]{2,1,0:T(8,128)(2,1)S(1)}, u32[]{:S(2)}, u32[]{:S(2)}) collective-permute-start(bf16[4,64,256]{2,1,0:T(8,128)(2,1)S(1)} %get-tuple-element.70), channel_id=1, source_target_pairs={{0,8},{4,12},{8,0},{12,4},{16,24},{20,28},{24,16},{28,20},{1,9},{5... | collective-permute-start | bytes 393224 | tf_op jit(solution)/shard_map/ppermute | solution.py:552
  20.3 13.3 %collective-permute-start.9 = (bf16[768,256]{1,0:T(8,128)(2,1)S(1)}, bf16[768,256]{1,0:T(8,128)(2,1)S(1)}, u32[]{:S(2)}, u32[]{:S(2)}) collective-permute-start(bf16[768,256]{1,0:T(8,128)(2,1)S(1)} %get-tuple-element.76), channel_id=1, source_target_pairs={{0,12},{4,20},{8,24},{12,0},{16,28},{20,4},{24,8},{28,16},{1,13},{... | collective-permute-start | bytes 1179656 | tf_op jit(solution)/shard_map/ppermute | solution.py:552
  21.3 13.7 %collective-permute-start.10 = (bf16[256,256]{1,0:T(8,128)(2,1)S(1)}, bf16[256,256]{1,0:T(8,128)(2,1)S(1)}, u32[]{:S(2)}, u32[]{:S(2)}) collective-permute-start(bf16[256,256]{1,0:T(8,128)(2,1)S(1)} %get-tuple-element.79), channel_id=1, source_target_pairs={{0,12},{4,20},{8,24},{12,0},{16,28},{20,4},{24,8},{28,16},{1,13},{... | collective-permute-start | bytes 393224 | tf_op jit(solution)/shard_map/ppermute | solution.py:552
  25.9 10.1 %collective-permute-start.11 = (bf16[4,32,256]{2,1,0:T(8,128)(2,1)S(1)}, bf16[4,32,256]{2,1,0:T(8,128)(2,1)S(1)}, u32[]{:S(2)}, u32[]{:S(2)}) collective-permute-start(bf16[4,32,256]{2,1,0:T(8,128)(2,1)S(1)} %get-tuple-element.83), channel_id=1, source_target_pairs={{0,16},{4,20},{8,24},{12,28},{16,0},{20,4},{24,8},{28,12},{1,17},{... | collective-permute-start | bytes 196616 | tf_op jit(solution)/shard_map/ppermute | solution.py:552

commit v8 on v7

--- a/solution.py
+++ b/solution.py
@@ -141,12 +141,14 @@
 
 
 def restage_kernel(
-    roles, half, directions_ref, charges_ref, present_ref, left_ref, wave_ref, rot_ref, *refs
+    roles, half, directions_ref, charges_ref, present_ref, left_ref, wave_ref, rot_ref, had, *refs
 ):
     outs = refs[: len(roles)]
     left, wave, rot, directions, charges, present, few, sems = refs[len(roles) :]
+    count, lead = had.shape[:2]
+    rest = pl.ds(lead, left.shape[1] - lead)
     bulk = [
-        pltpu.make_async_copy(left_ref, left, sems.at[0]),
+        pltpu.make_async_copy(left_ref.at[:, rest], left.at[:, rest], sems.at[0]),
         pltpu.make_async_copy(wave_ref, wave, sems.at[1]),
         pltpu.make_async_copy(rot_ref, rot, sems.at[2]),
     ]
@@ -155,13 +157,16 @@
     fetch_scalars(
         [(directions_ref, directions), (charges_ref, charges), (present_ref, present)], few
     )
+    for p in range(count):
+        for s in range(lead):
+            left[p, s] = had[p, s]
     bulk[0].wait()
     copy_pairs(roles, half, outs, left, directions, charges, present)
     for copy in bulk[1:]:
         copy.wait()
 
 
-def staged(token, roles, half, directions, charges, present, *bulk):
+def staged(token, roles, half, directions, charges, present, *bulk, had=()):
     count, sectors, width, _ = bulk[0].shape
     shapes = [
         (len(sent) * (stop - begin) * width + (meta_rows(sectors) if told else 0), width)
@@ -174,7 +179,7 @@
         pltpu.SemaphoreType.DMA,
     ]
     if token is None:
-        scratch.insert(0, pltpu.VMEM((count, roles[0][3], width, width), BF16))
+        shapes.append((count, roles[0][3], width, width))
         scratch.append(pltpu.SemaphoreType.DMA((roles[0][3],)))
     else:
         shapes += [x.shape for x in bulk]
@@ -182,8 +187,8 @@
     return kernel_call(
         functools.partial(stage_kernel if token is None else restage_kernel, roles, half),
         token,
-        [in_hbm(x) for x in (directions, charges, present, *bulk)],
-        [HBM] * (3 + len(bulk)),
+        [in_hbm(x) for x in (directions, charges, present, *bulk)] + list(had),
+        [HBM] * (3 + len(bulk)) + [VMEM] * len(had),
         [pltpu.VMEM(shape, BF16) for shape in shapes],
         [VMEM] * len(shapes),
         scratch_shapes=scratch,
@@ -575,7 +580,7 @@
     core_roles = ("extra", "core")
     lead = min(2, sectors)
     whole = (0, sectors)
-    token, (front,) = staged(
+    token, (front, had) = staged(
         None, ((ahead_roles, (), 0, lead),), half, *small, left_operators
     )
     token, (rear, behind, last, first_core, left, wave, turn) = staged(
@@ -591,6 +596,7 @@
         left_operators,
         wavefunction,
         rotations,
+        had=(had,),
     )
     got_front, got_rear = [
         over_op(x, lambda i: opposite(i) if end(i) else side(i)) for x in (front, rear)

time: 36.9 us -> 36.8 us (level)
  waiting for transfers between devices: 13.3 us -> 14.1 us
  starting transfers between devices: 10.6 us -> 10 us
  Pallas kernels: 12.2 us -> 11.8 us
    ppermute x10, waiting for transfers between devices: 9.23 us -> 10 us  [over_op(): return lax.ppermute(value, 'op', [(i, target(i)) for i in range(n)])]
    ppermute x10, starting transfers between devices: 8.57 us -> 7.98 us  [over_op(): return lax.ppermute(value, 'op', [(i, target(i)) for i in range(n)])]
  transfers between devices with their start and end apart: 12 -> 12, of which waited for: 7 -> 7; matrix products, arithmetic and copies ran while one was open for 0% -> 0% of each run, Pallas kernels for 28% -> 27%
where the time goes in v8:
time: 36.8 us; the launch traced here: 36.6 us
  waiting for transfers between devices  14.1 us (38%)
  Pallas kernels  11.8 us (32%)
  starting transfers between devices  10 us (27%)
  between operations  0.73 us (2%)
    pallas_call x15, Pallas kernels, kernel_call(): pl.pallas_call(run, grid=grid, out_shape=[jax.ShapeDtypeStruct((8, 128),...  11.8 us
    ppermute x10, waiting for transfers between devices, over_op(): return lax.ppermute(value, 'op', [(i, target(i)) for i in range(n)])  10 us
    ppermute x10, starting transfers between devices, over_op(): return lax.ppermute(value, 'op', [(i, target(i)) for i in range(n)])  7.98 us
    ppermute x2, waiting for transfers between devices, swapped(): return lax.ppermute(value, 'sec', list(enumerate(to)))  4.03 us
    ppermute x2, starting transfers between devices, swapped(): return lax.ppermute(value, 'sec', list(enumerate(to)))  2.02 us
  transfers between devices with their start and end apart: 12, of which 7 were waited for; matrix products, arithmetic and copies ran while one was open for 0% of the time, Pallas kernels for 27%

profile of v8, /device:TPU:1, one launch (start us, length us, event | category | flops | bytes accessed | tf_op | source)
XLA Modules:
  0.0 36.6 jit_solution(6087451730954946844)
XLA Ops:
  0.6 1.2 %stage.1 = (f32[8,128]{1,0:T(8,128)S(1)}, bf16[1024,256]{1,0:T(8,128)(2,1)S(1)}, bf16[4,2,256,256]{3,2,1,0:T(8,128)(2,1)S(1)}) custom-call(s32[4]{0:T(128)} %bitcast.1, s32[4]{0:T(128)} %refs_1_.3, s32[4,4]{1,0:T(4,128)} %refs_2_.5, bf16[4,4,256,256]{3,2,1,0:T(8,128)(2,1)} %refs_4_.2), custom_call_target="tpu_custom_call" | custom-call | tf_op jit(solution)/shard_map/stage/pallas_call | solution.py:35
  1.9 2.7 %collective-permute-start = (bf16[1024,256]{1,0:T(8,128)(2,1)S(1)}, bf16[1024,256]{1,0:T(8,128)(2,1)S(1)}, u32[]{:S(2)}, u32[]{:S(2)}) collective-permute-start(bf16[1024,256]{1,0:T(8,128)(2,1)S(1)} %get-tuple-element.52), channel_id=1, source_target_pairs={{0,16},{4,8},{8,4},{12,28},{16,0},{20,24},{24,20},{28,12},{1,17},{... | collective-permute-start | bytes 1572872 | tf_op jit(solution)/shard_map/ppermute | solution.py:557
  4.5 1.5 %restage.1 = (f32[8,128]{1,0:T(8,128)S(1)}, bf16[1040,256]{1,0:T(8,128)(2,1)S(1)}, bf16[1040,256]{1,0:T(8,128)(2,1)S(1)}, bf16[1024,256]{1,0:T(8,128)(2,1)S(1)},...) custom-call(f32[8,128]{1,0:T(8,128)S(1)} %get-tuple-element.45.refs_, ...), custom_call_target="tpu_custom_call" | custom-call | tf_op jit(solution)/shard_map/restage/pallas_call | solution.py:35
  6.1 0.5 %collective-permute-start.7 = (bf16[2064,256]{1,0:T(8,128)(2,1)S(1)}, bf16[2064,256]{1,0:T(8,128)(2,1)S(1)}, u32[]{:S(2)}, u32[]{:S(2)}) collective-permute-start(bf16[2064,256]{1,0:T(8,128)(2,1)S(1)} %get-tuple-element.75), channel_id=1, source_target_pairs={{0,4},{4,0},{8,12},{12,8},{16,20},{20,16},{24,28},{28,24},{1,5},{5... | collective-permute-start | bytes 3170312 | tf_op jit(solution)/shard_map/ppermute | solution.py:557
  6.6 0.7 %collective-permute-start.5 = (bf16[1040,256]{1,0:T(8,128)(2,1)S(1)}, bf16[1040,256]{1,0:T(8,128)(2,1)S(1)}, u32[]{:S(2)}, u32[]{:S(2)}) collective-permute-start(bf16[1040,256]{1,0:T(8,128)(2,1)S(1)} %get-tuple-element.68), channel_id=1, source_target_pairs={{0,16},{4,8},{8,4},{12,28},{16,0},{20,24},{24,20},{28,12},{1,17},{... | collective-permute-start | bytes 1597448 | tf_op jit(solution)/shard_map/ppermute | solution.py:557
  7.2 3.4 %sigma_terms.1 = (f32[8,128]{1,0:T(8,128)S(1)}, bf16[3,128,256]{2,1,0:T(8,128)(2,1)S(1)}, bf16[3,128,256]{2,1,0:T(8,128)(2,1)S(1)}, f32[6,128,256]{2,1,0:T(8,128)S(1)}, bf16[4,256,256]{2,1,0:T(8,128)(2,1)S(1)}) custom-call(f32[8,128]{1,0:T(8,128)S(1)} %get-tuple-element.47.refs_0_, s32[4]{0:T(128)} %refs_1_.3, s32[4,4]{1,0:T(4,128)} %refs_2_.5, ...), custom_call_target="tpu_custom_call" | custom-call | tf_op jit(solution)/shard_map/sigma_terms/pallas_call | solution.py:35
  10.6 1.0 %collective-permute-start.1 = (bf16[3,128,256]{2,1,0:T(8,128)(2,1)S(1)}, bf16[3,128,256]{2,1,0:T(8,128)(2,1)S(1)}, u32[]{:S(2)}, u32[]{:S(2)}) collective-permute-start(bf16[3,128,256]{2,1,0:T(8,128)(2,1)S(1)} %get-tuple-element.54), channel_id=1, source_target_pairs={{0,4},{4,0},{8,12},{12,8},{16,20},{20,16},{24,28},{28,24},{1,5},{5... | collective-permute-start | bytes 589832 | tf_op jit(solution)/shard_map/ppermute | solution.py:557
  11.7 1.0 %collective-permute-done.1.refs_1_ = bf16[3,128,256]{2,1,0:T(8,128)(2,1)S(1)} collective-permute-done((bf16[3,128,256]{2,1,0:T(8,128)(2,1)S(1)}, bf16[3,128,256]{2,1,0:T(8,128)(2,1)S(1)}, u32[]{:S(2)}, u32[]{:S(2)}) %collective-permute-start.1) | collective-permute-done | bytes 196640 | tf_op jit(solution)/shard_map/ppermute | solution.py:557
  12.7 0.4 %collective-permute-done.2.refs_2_ = bf16[3,128,256]{2,1,0:T(8,128)(2,1)S(1)} collective-permute-done((bf16[3,128,256]{2,1,0:T(8,128)(2,1)S(1)}, bf16[3,128,256]{2,1,0:T(8,128)(2,1)S(1)}, u32[]{:S(2)}, u32[]{:S(2)}) %collective-permute-start.2) | collective-permute-done | bytes 196640 | tf_op jit(solution)/shard_map/ppermute | solution.py:557
  13.1 1.4 %collective-permute-start.3 = (bf16[384,256]{1,0:T(8,128)(2,1)S(1)}, bf16[384,256]{1,0:T(8,128)(2,1)S(1)}, u32[]{:S(2)}, u32[]{:S(2)}) collective-permute-start(bf16[384,256]{1,0:T(8,128)(2,1)S(1)} %get-tuple-element.60), channel_id=1, source_target_pairs={{0,1},{1,0},{2,3},{3,2},{4,5},{5,4},{6,7},{7,6},{8,9},{9,8},{10,11... | collective-permute-start | bytes 589832 | tf_op jit(solution)/shard_map/ppermute | solution.py:563
  14.5 0.2 collective-permute-start.8
  14.7 0.7 %collective-permute-start.4 = (bf16[384,256]{1,0:T(8,128)(2,1)S(1)}, bf16[384,256]{1,0:T(8,128)(2,1)S(1)}, u32[]{:S(2)}, u32[]{:S(2)}) collective-permute-start(bf16[384,256]{1,0:T(8,128)(2,1)S(1)} %get-tuple-element.64), channel_id=1, source_target_pairs={{0,0},{1,2},{2,1},{3,3},{4,4},{5,6},{6,5},{7,7},{8,8},{9,10},{10,9... | collective-permute-start | bytes 589832 | tf_op jit(solution)/shard_map/ppermute | solution.py:563
  15.4 4.0 %collective-permute-done.3.refs_1_ = bf16[384,256]{1,0:T(8,128)(2,1)S(1)} collective-permute-done((bf16[384,256]{1,0:T(8,128)(2,1)S(1)}, bf16[384,256]{1,0:T(8,128)(2,1)S(1)}, u32[]{:S(2)}, u32[]{:S(2)}) %collective-permute-start.3) | collective-permute-done | bytes 196640 | tf_op jit(solution)/shard_map/ppermute | solution.py:563
  19.5 0.3 collective-permute-start.6
  20.0 1.0 %collective-permute-start.9 = (bf16[768,256]{1,0:T(8,128)(2,1)S(1)}, bf16[768,256]{1,0:T(8,128)(2,1)S(1)}, u32[]{:S(2)}, u32[]{:S(2)}) collective-permute-start(bf16[768,256]{1,0:T(8,128)(2,1)S(1)} %get-tuple-element.78), channel_id=1, source_target_pairs={{0,12},{4,20},{8,24},{12,0},{16,28},{20,4},{24,8},{28,16},{1,13},{... | collective-permute-start | bytes 1179656 | tf_op jit(solution)/shard_map/ppermute | solution.py:557
  20.9 0.6 %collective-permute-start.10 = (bf16[256,256]{1,0:T(8,128)(2,1)S(1)}, bf16[256,256]{1,0:T(8,128)(2,1)S(1)}, u32[]{:S(2)}, u32[]{:S(2)}) collective-permute-start(bf16[256,256]{1,0:T(8,128)(2,1)S(1)} %get-tuple-element.81), channel_id=1, source_target_pairs={{0,12},{4,20},{8,24},{12,0},{16,28},{20,4},{24,8},{28,16},{1,13},{... | collective-permute-start | bytes 393224 | tf_op jit(solution)/shard_map/ppermute | solution.py:557
  21.5 4.7 %collective-permute-done.6.refs_2_ = bf16[4,64,256]{2,1,0:T(8,128)(2,1)S(1)} collective-permute-done((bf16[4,64,256]{2,1,0:T(8,128)(2,1)S(1)}, bf16[4,64,256]{2,1,0:T(8,128)(2,1)S(1)}, u32[]{:S(2)}, u32[]{:S(2)}) %collective-permute-start.6) | collective-permute-done | bytes 131104 | tf_op jit(solution)/shard_map/ppermute | solution.py:557
  26.2 1.0 %collective-permute-start.11 = (bf16[4,32,256]{2,1,0:T(8,128)(2,1)S(1)}, bf16[4,32,256]{2,1,0:T(8,128)(2,1)S(1)}, u32[]{:S(2)}, u32[]{:S(2)}) collective-permute-start(bf16[4,32,256]{2,1,0:T(8,128)(2,1)S(1)} %get-tuple-element.85), channel_id=1, source_target_pairs={{0,16},{4,20},{8,24},{12,28},{16,0},{20,4},{24,8},{28,12},{1,17},{... | collective-permute-start | bytes 196616 | tf_op jit(solution)/shard_map/ppermute | solution.py:557
  27.2 1.6 %collective-permute-done.8.refs_6_.refs_4_ = bf16[1040,256]{1,0:T(8,128)(2,1)S(1)} collective-permute-done((bf16[1040,256]{1,0:T(8,128)(2,1)S(1)}, bf16[1040,256]{1,0:T(8,128)(2,1)S(1)}, u32[]{:S(2)}, u32[]{:S(2)}) %collective-permute-start.8) | collective-permute-done | bytes 532512 | tf_op jit(solution)/shard_map/ppermute | solution.py:557
  28.9 2.4 %renorm_first.1 = (f32[8,128]{1,0:T(8,128)S(1)}, bf16[8,4,256,256]{3,2,1,0:T(8,128)(2,1)}) custom-call(f32[8,128]{1,0:T(8,128)S(1)} %get-tuple-element.73.refs_0_, bf16[6,256,256]{2,1,0:T(8,128)(2,1)S(1)} %get-tuple-element.74.refs_1_, bf16[4,256,256]{2,1,0:T(8,128)(2,1)S(1)} %get-tuple-element.50.refs_6_.refs_2_, ...), custom_call_target="tpu_custom_call" | custom-call | flops 2018625024 | tf_op jit(solution)/shard_map/renorm_first/pallas_call | solution.py:35
  31.3 2.2 %collective-permute-done.9.refs_3_ = bf16[768,256]{1,0:T(8,128)(2,1)S(1)} collective-permute-done((bf16[768,256]{1,0:T(8,128)(2,1)S(1)}, bf16[768,256]{1,0:T(8,128)(2,1)S(1)}, u32[]{:S(2)}, u32[]{:S(2)}) %collective-permute-start.9) | collective-permute-done | bytes 393248 | tf_op jit(solution)/shard_map/ppermute | solution.py:557
  33.5 1.2 %renorm_last.2 = (f32[8,128]{1,0:T(8,128)S(1)}, bf16[8,4,256,256]{3,2,1,0:T(8,128)(2,1)}) custom-call(f32[8,128]{1,0:T(8,128)S(1)} %get-tuple-element.77.refs_0_, bf16[6,256,256]{2,1,0:T(8,128)(2,1)S(1)} %get-tuple-element.74.refs_1_, bf16[4,256,256]{2,1,0:T(8,128)(2,1)S(1)} %get-tuple-element.50.refs_6_.refs_2_, ...), custom_call_target="tpu_custom_call", output_to_operand_aliasing={{1}: (5, {})} | custom-call | tf_op jit(solution)/shard_map/renorm_last/pallas_call | solution.py:35
  34.9 1.1 %renorm_last.3 = (f32[8,128]{1,0:T(8,128)S(1)}, bf16[8,4,256,256]{3,2,1,0:T(8,128)(2,1)}) custom-call(f32[8,128]{1,0:T(8,128)S(1)} %get-tuple-element.80.refs_0_, bf16[6,256,256]{2,1,0:T(8,128)(2,1)S(1)} %get-tuple-element.74.refs_1_, bf16[4,256,256]{2,1,0:T(8,128)(2,1)S(1)} %get-tuple-element.50.refs_6_.refs_2_, ...), custom_call_target="tpu_custom_call", output_to_operand_aliasing={{1}: (5, {})} | custom-call | tf_op jit(solution)/shard_map/renorm_last/pallas_call | solution.py:35
  36.0 0.7 %finish.1 = (f32[8,128]{1,0:T(8,128)}, f32[4,32,256]{2,1,0:T(8,128)}) custom-call(f32[8,128]{1,0:T(8,128)S(1)} %get-tuple-element.83.refs_0_, f32[4,32,256]{2,1,0:T(8,128)S(1)} %get-tuple-element.84.refs_1_, bf16[4,32,256]{2,1,0:T(8,128)(2,1)S(1)} %collective-permute-done.11.refs_2_), custom_call_target="tpu_custom_call" | custom-call | tf_op jit(solution)/shard_map/finish/pallas_call | solution.py:35
  (15 shorter events, 0.5 us)
Async XLA Ops:
  1.9 9.9 %collective-permute-start = (bf16[1024,256]{1,0:T(8,128)(2,1)S(1)}, bf16[1024,256]{1,0:T(8,128)(2,1)S(1)}, u32[]{:S(2)}, u32[]{:S(2)}) collective-permute-start(bf16[1024,256]{1,0:T(8,128)(2,1)S(1)} %get-tuple-element.52), channel_id=1, source_target_pairs={{0,16},{4,8},{8,4},{12,28},{16,0},{20,24},{24,20},{28,12},{1,17},{... | collective-permute-start | bytes 1572872 | tf_op jit(solution)/shard_map/ppermute | solution.py:557
  6.1 22.8 %collective-permute-start.7 = (bf16[2064,256]{1,0:T(8,128)(2,1)S(1)}, bf16[2064,256]{1,0:T(8,128)(2,1)S(1)}, u32[]{:S(2)}, u32[]{:S(2)}) collective-permute-start(bf16[2064,256]{1,0:T(8,128)(2,1)S(1)} %get-tuple-element.75), channel_id=1, source_target_pairs={{0,4},{4,0},{8,12},{12,8},{16,20},{20,16},{24,28},{28,24},{1,5},{5... | collective-permute-start | bytes 3170312 | tf_op jit(solution)/shard_map/ppermute | solution.py:557
  6.6 13.3 %collective-permute-start.5 = (bf16[1040,256]{1,0:T(8,128)(2,1)S(1)}, bf16[1040,256]{1,0:T(8,128)(2,1)S(1)}, u32[]{:S(2)}, u32[]{:S(2)}) collective-permute-start(bf16[1040,256]{1,0:T(8,128)(2,1)S(1)} %get-tuple-element.68), channel_id=1, source_target_pairs={{0,16},{4,8},{8,4},{12,28},{16,0},{20,24},{24,20},{28,12},{1,17},{... | collective-permute-start | bytes 1597448 | tf_op jit(solution)/shard_map/ppermute | solution.py:557
  10.6 2.1 %collective-permute-start.1 = (bf16[3,128,256]{2,1,0:T(8,128)(2,1)S(1)}, bf16[3,128,256]{2,1,0:T(8,128)(2,1)S(1)}, u32[]{:S(2)}, u32[]{:S(2)}) collective-permute-start(bf16[3,128,256]{2,1,0:T(8,128)(2,1)S(1)} %get-tuple-element.54), channel_id=1, source_target_pairs={{0,4},{4,0},{8,12},{12,8},{16,20},{20,16},{24,28},{28,24},{1,5},{5... | collective-permute-start | bytes 589832 | tf_op jit(solution)/shard_map/ppermute | solution.py:557
  11.7 1.4 %collective-permute-start.2 = (bf16[3,128,256]{2,1,0:T(8,128)(2,1)S(1)}, bf16[3,128,256]{2,1,0:T(8,128)(2,1)S(1)}, u32[]{:S(2)}, u32[]{:S(2)}) collective-permute-start(bf16[3,128,256]{2,1,0:T(8,128)(2,1)S(1)} %get-tuple-element.57), channel_id=1, source_target_pairs={{0,4},{4,0},{8,12},{12,8},{16,20},{20,16},{24,28},{28,24},{1,5},{5... | collective-permute-start | bytes 589832 | tf_op jit(solution)/shard_map/ppermute | solution.py:557
  13.1 6.3 %collective-permute-start.3 = (bf16[384,256]{1,0:T(8,128)(2,1)S(1)}, bf16[384,256]{1,0:T(8,128)(2,1)S(1)}, u32[]{:S(2)}, u32[]{:S(2)}) collective-permute-start(bf16[384,256]{1,0:T(8,128)(2,1)S(1)} %get-tuple-element.60), channel_id=1, source_target_pairs={{0,1},{1,0},{2,3},{3,2},{4,5},{5,4},{6,7},{7,6},{8,9},{9,8},{10,11... | collective-permute-start | bytes 589832 | tf_op jit(solution)/shard_map/ppermute | solution.py:563
  14.5 14.3 %collective-permute-start.8 = (bf16[1040,256]{1,0:T(8,128)(2,1)S(1)}, bf16[1040,256]{1,0:T(8,128)(2,1)S(1)}, u32[]{:S(2)}, u32[]{:S(2)}) collective-permute-start(bf16[1040,256]{1,0:T(8,128)(2,1)S(1)} %get-tuple-element.76), channel_id=1, source_target_pairs={{0,28},{4,20},{8,24},{12,16},{16,12},{20,4},{24,8},{28,0},{1,29},{... | collective-permute-start | bytes 1597448 | tf_op jit(solution)/shard_map/ppermute | solution.py:557
  14.7 4.7 %collective-permute-start.4 = (bf16[384,256]{1,0:T(8,128)(2,1)S(1)}, bf16[384,256]{1,0:T(8,128)(2,1)S(1)}, u32[]{:S(2)}, u32[]{:S(2)}) collective-permute-start(bf16[384,256]{1,0:T(8,128)(2,1)S(1)} %get-tuple-element.64), channel_id=1, source_target_pairs={{0,0},{1,2},{2,1},{3,3},{4,4},{5,6},{6,5},{7,7},{8,8},{9,10},{10,9... | collective-permute-start | bytes 589832 | tf_op jit(solution)/shard_map/ppermute | solution.py:563
  19.5 6.7 %collective-permute-start.6 = (bf16[4,64,256]{2,1,0:T(8,128)(2,1)S(1)}, bf16[4,64,256]{2,1,0:T(8,128)(2,1)S(1)}, u32[]{:S(2)}, u32[]{:S(2)}) collective-permute-start(bf16[4,64,256]{2,1,0:T(8,128)(2,1)S(1)} %get-tuple-element.72), channel_id=1, source_target_pairs={{0,8},{4,12},{8,0},{12,4},{16,24},{20,28},{24,16},{28,20},{1,9},{5... | collective-permute-start | bytes 393224 | tf_op jit(solution)/shard_map/ppermute | solution.py:557
  20.0 13.5 %collective-permute-start.9 = (bf16[768,256]{1,0:T(8,128)(2,1)S(1)}, bf16[768,256]{1,0:T(8,128)(2,1)S(1)}, u32[]{:S(2)}, u32[]{:S(2)}) collective-permute-start(bf16[768,256]{1,0:T(8,128)(2,1)S(1)} %get-tuple-element.78), channel_id=1, source_target_pairs={{0,12},{4,20},{8,24},{12,0},{16,28},{20,4},{24,8},{28,16},{1,13},{... | collective-permute-start | bytes 1179656 | tf_op jit(solution)/shard_map/ppermute | solution.py:557
  20.9 13.9 %collective-permute-start.10 = (bf16[256,256]{1,0:T(8,128)(2,1)S(1)}, bf16[256,256]{1,0:T(8,128)(2,1)S(1)}, u32[]{:S(2)}, u32[]{:S(2)}) collective-permute-start(bf16[256,256]{1,0:T(8,128)(2,1)S(1)} %get-tuple-element.81), channel_id=1, source_target_pairs={{0,12},{4,20},{8,24},{12,0},{16,28},{20,4},{24,8},{28,16},{1,13},{... | collective-permute-start | bytes 393224 | tf_op jit(solution)/shard_map/ppermute | solution.py:557
  26.2 9.7 %collective-permute-start.11 = (bf16[4,32,256]{2,1,0:T(8,128)(2,1)S(1)}, bf16[4,32,256]{2,1,0:T(8,128)(2,1)S(1)}, u32[]{:S(2)}, u32[]{:S(2)}) collective-permute-start(bf16[4,32,256]{2,1,0:T(8,128)(2,1)S(1)} %get-tuple-element.85), channel_id=1, source_target_pairs={{0,16},{4,20},{8,24},{12,28},{16,0},{20,4},{24,8},{28,12},{1,17},{... | collective-permute-start | bytes 196616 | tf_op jit(solution)/shard_map/ppermute | solution.py:557

commit v9 on v8

--- a/solution.py
+++ b/solution.py
@@ -446,9 +446,13 @@
     )
 
 
-def renorm_kernel(items, zero, levels, half, framed, rotations, *refs):
+def renorm_kernel(items, zero, levels, half, scale, framed, rotations, *refs):
+    if scale is not None:
+        keep, got, *refs = refs
     buffers = refs[: 1 + max(buffer for came, told, *_ in items for buffer in (came[0], told[0]))]
     rest = refs[len(buffers) + (0 if zero else 1) :]
+    if scale is not None:
+        sigma, *rest, total = [rest[1], rest[0], *rest[2:]]
     out, results, done = rest
     sectors, width, _ = rotations.shape
     odd = lax.rem(lax.axis_index("op"), 2)
@@ -456,6 +460,11 @@
     level = lax.axis_index("sec")
     height = meta_rows(sectors)
     stores = []
+    if scale is not None:
+        total[...] = (keep[...] + got[...].astype(F32)) * scale
+        copy = pltpu.make_async_copy(total, sigma, done)
+        copy.start()
+        stores.append(copy)
     if zero:
         results[len(items)] = jnp.zeros_like(results[len(items)])
         for place in range(CAPS):
@@ -492,51 +501,36 @@
 
 
 def renorm(
-    token, name, items, buffers, out, levels, half, framed, rotations, cost=0
+    token, name, items, buffers, out, levels, half, framed, rotations, cost=0, sums=(), scale=None
 ):
     sectors, width, _ = rotations.shape
     zero = out is None
-    operands = [framed, rotations, *buffers]
+    operands = [framed, rotations, *sums, *buffers]
     in_specs = [VMEM] * len(operands)
     if not zero:
         operands.append(out)
         in_specs.append(HBM)
     count = len(items)
     block = (sectors, width, width)
-    token, (out,) = kernel_call(
-        functools.partial(renorm_kernel, items, zero, levels, half),
+    return kernel_call(
+        functools.partial(renorm_kernel, items, zero, levels, half, scale),
         token,
         operands,
         in_specs,
-        [jax.ShapeDtypeStruct((DIRS * CAPS, *block), BF16)],
-        [HBM],
+        [
+            jax.ShapeDtypeStruct((DIRS * CAPS, *block), BF16),
+            *(jax.ShapeDtypeStruct(x.shape, F32) for x in sums[:1]),
+        ],
+        [HBM] * (1 + len(sums[:1])),
         aliases={} if zero else {len(operands) - 1: 0},
         scratch_shapes=[
             pltpu.VMEM((count + (1 if zero else 0), *block), BF16),
             pltpu.SemaphoreType.DMA,
+            *(pltpu.VMEM(x.shape, F32) for x in sums[:1]),
         ],
         mib=10,
         cost_estimate=estimate(cost),
         name=name,
-    )
-    return token, out
-
-
-def finish_kernel(scale, keep, got, out):
-    out[...] = (keep[...] + got[...].astype(F32)) * scale
-
-
-def finish(token, scale, keep, got):
-    return kernel_call(
-        functools.partial(finish_kernel, scale),
-        token,
-        (keep, got),
-        [VMEM] * 2,
-        [jax.ShapeDtypeStruct(keep.shape, F32)],
-        [VMEM],
-        mib=4,
-        cost_estimate=estimate(0),
-        name="finish",
     )
 
 
@@ -648,7 +642,7 @@
     fixed = (levels, half, framed, turn)
     tail = (sectors - lead) * width
     told = 2 * tail
-    token, out = renorm(
+    token, (out,) = renorm(
         token,
         "renorm_first",
         (
@@ -667,19 +661,19 @@
     )
     scale = 1.0 / math.sqrt(pairs * n)
     for i, (begin, stop) in enumerate(parts):
-        token, out = renorm(
+        token, (out, *sigma_vector) = renorm(
             token,
             "renorm_last",
             (((0, 0), (1, rows, 1), (("side", 1), ("half", 0)), begin, stop),),
             (got_last[i], got_behind),
             out,
             *fixed,
+            sums=(keep, got) if halving and i == len(parts) - 1 else (),
+            scale=scale if halving and i == len(parts) - 1 else None,
         )
-    if halving:
-        token, (sigma_vector,) = finish(token, scale, keep, got)
-    else:
-        sigma_vector = summed * scale
-    return sigma_vector, out
+    if not halving:
+        sigma_vector = [summed * scale]
+    return sigma_vector[0], out
 
 
 def solution(mesh):

time: 36.8 us -> 36.8 us (level)
  waiting for transfers between devices: 14.1 us -> 14.8 us
  Pallas kernels: 11.8 us -> 11.2 us
    ppermute x10, waiting for transfers between devices: 10 us -> 10.7 us  [over_op(): return lax.ppermute(value, 'op', [(i, target(i)) for i in range(n)])]
    pallas_call x15 -> x14, Pallas kernels: 11.8 us -> 11.2 us  [kernel_call(): pl.pallas_call(run, grid=grid, out_shape=[jax.ShapeDtypeStruct((8, 128),...]
  transfers between devices with their start and end apart: 12 -> 12, of which waited for: 7 -> 8; matrix products, arithmetic and copies ran while one was open for 0% -> 0% of each run, Pallas kernels for 27% -> 24%
where the time goes in v9:
time: 36.8 us; the launch traced here: 36.6 us
  waiting for transfers between devices  14.8 us (40%)
  Pallas kernels  11.2 us (30%)
  starting transfers between devices  10 us (27%)
  between operations  0.72 us (2%)
    pallas_call x14, Pallas kernels, kernel_call(): pl.pallas_call(run, grid=grid, out_shape=[jax.ShapeDtypeStruct((8, 128),...  11.2 us
    ppermute x10, waiting for transfers between devices, over_op(): return lax.ppermute(value, 'op', [(i, target(i)) for i in range(n)])  10.7 us
    ppermute x10, starting transfers between devices, over_op(): return lax.ppermute(value, 'op', [(i, target(i)) for i in range(n)])  7.98 us
    ppermute x2, waiting for transfers between devices, swapped(): return lax.ppermute(value, 'sec', list(enumerate(to)))  4.03 us
    ppermute x2, starting transfers between devices, swapped(): return lax.ppermute(value, 'sec', list(enumerate(to)))  2.02 us
  transfers between devices with their start and end apart: 12, of which 8 were waited for; matrix products, arithmetic and copies ran while one was open for 0% of the time, Pallas kernels for 24%

profile of v9, /device:TPU:1, one launch (start us, length us, event | category | flops | bytes accessed | tf_op | source)
XLA Modules:
  0.0 36.6 jit_solution(13179159583150888538)
XLA Ops:
  0.6 1.2 %stage.1 = (f32[8,128]{1,0:T(8,128)S(1)}, bf16[1024,256]{1,0:T(8,128)(2,1)S(1)}, bf16[4,2,256,256]{3,2,1,0:T(8,128)(2,1)S(1)}) custom-call(s32[4]{0:T(128)} %bitcast.1, s32[4]{0:T(128)} %refs_1_.3, s32[4,4]{1,0:T(4,128)} %refs_2_.5, bf16[4,4,256,256]{3,2,1,0:T(8,128)(2,1)} %refs_4_.2), custom_call_target="tpu_custom_call" | custom-call | tf_op jit(solution)/shard_map/stage/pallas_call | solution.py:35
  1.9 2.7 %collective-permute-start = (bf16[1024,256]{1,0:T(8,128)(2,1)S(1)}, bf16[1024,256]{1,0:T(8,128)(2,1)S(1)}, u32[]{:S(2)}, u32[]{:S(2)}) collective-permute-start(bf16[1024,256]{1,0:T(8,128)(2,1)S(1)} %get-tuple-element.51), channel_id=1, source_target_pairs={{0,16},{4,8},{8,4},{12,28},{16,0},{20,24},{24,20},{28,12},{1,17},{... | collective-permute-start | bytes 1572872 | tf_op jit(solution)/shard_map/ppermute | solution.py:551
  4.5 1.5 %restage.1 = (f32[8,128]{1,0:T(8,128)S(1)}, bf16[1040,256]{1,0:T(8,128)(2,1)S(1)}, bf16[1040,256]{1,0:T(8,128)(2,1)S(1)}, bf16[1024,256]{1,0:T(8,128)(2,1)S(1)},...) custom-call(f32[8,128]{1,0:T(8,128)S(1)} %get-tuple-element.44.refs_, ...), custom_call_target="tpu_custom_call" | custom-call | tf_op jit(solution)/shard_map/restage/pallas_call | solution.py:35
  6.1 0.5 %collective-permute-start.7 = (bf16[2064,256]{1,0:T(8,128)(2,1)S(1)}, bf16[2064,256]{1,0:T(8,128)(2,1)S(1)}, u32[]{:S(2)}, u32[]{:S(2)}) collective-permute-start(bf16[2064,256]{1,0:T(8,128)(2,1)S(1)} %get-tuple-element.74), channel_id=1, source_target_pairs={{0,4},{4,0},{8,12},{12,8},{16,20},{20,16},{24,28},{28,24},{1,5},{5... | collective-permute-start | bytes 3170312 | tf_op jit(solution)/shard_map/ppermute | solution.py:551
  6.6 0.7 %collective-permute-start.5 = (bf16[1040,256]{1,0:T(8,128)(2,1)S(1)}, bf16[1040,256]{1,0:T(8,128)(2,1)S(1)}, u32[]{:S(2)}, u32[]{:S(2)}) collective-permute-start(bf16[1040,256]{1,0:T(8,128)(2,1)S(1)} %get-tuple-element.67), channel_id=1, source_target_pairs={{0,16},{4,8},{8,4},{12,28},{16,0},{20,24},{24,20},{28,12},{1,17},{... | collective-permute-start | bytes 1597448 | tf_op jit(solution)/shard_map/ppermute | solution.py:551
  7.2 3.4 %sigma_terms.1 = (f32[8,128]{1,0:T(8,128)S(1)}, bf16[3,128,256]{2,1,0:T(8,128)(2,1)S(1)}, bf16[3,128,256]{2,1,0:T(8,128)(2,1)S(1)}, f32[6,128,256]{2,1,0:T(8,128)S(1)}, bf16[4,256,256]{2,1,0:T(8,128)(2,1)S(1)}) custom-call(f32[8,128]{1,0:T(8,128)S(1)} %get-tuple-element.46.refs_0_, s32[4]{0:T(128)} %refs_1_.3, s32[4,4]{1,0:T(4,128)} %refs_2_.5, ...), custom_call_target="tpu_custom_call" | custom-call | tf_op jit(solution)/shard_map/sigma_terms/pallas_call | solution.py:35
  10.6 1.0 %collective-permute-start.1 = (bf16[3,128,256]{2,1,0:T(8,128)(2,1)S(1)}, bf16[3,128,256]{2,1,0:T(8,128)(2,1)S(1)}, u32[]{:S(2)}, u32[]{:S(2)}) collective-permute-start(bf16[3,128,256]{2,1,0:T(8,128)(2,1)S(1)} %get-tuple-element.53), channel_id=1, source_target_pairs={{0,4},{4,0},{8,12},{12,8},{16,20},{20,16},{24,28},{28,24},{1,5},{5... | collective-permute-start | bytes 589832 | tf_op jit(solution)/shard_map/ppermute | solution.py:551
  11.7 1.0 %collective-permute-done.1.refs_1_ = bf16[3,128,256]{2,1,0:T(8,128)(2,1)S(1)} collective-permute-done((bf16[3,128,256]{2,1,0:T(8,128)(2,1)S(1)}, bf16[3,128,256]{2,1,0:T(8,128)(2,1)S(1)}, u32[]{:S(2)}, u32[]{:S(2)}) %collective-permute-start.1) | collective-permute-done | bytes 196640 | tf_op jit(solution)/shard_map/ppermute | solution.py:551
  12.7 0.4 %collective-permute-done.2.refs_2_ = bf16[3,128,256]{2,1,0:T(8,128)(2,1)S(1)} collective-permute-done((bf16[3,128,256]{2,1,0:T(8,128)(2,1)S(1)}, bf16[3,128,256]{2,1,0:T(8,128)(2,1)S(1)}, u32[]{:S(2)}, u32[]{:S(2)}) %collective-permute-start.2) | collective-permute-done | bytes 196640 | tf_op jit(solution)/shard_map/ppermute | solution.py:551
  13.1 1.4 %collective-permute-start.3 = (bf16[384,256]{1,0:T(8,128)(2,1)S(1)}, bf16[384,256]{1,0:T(8,128)(2,1)S(1)}, u32[]{:S(2)}, u32[]{:S(2)}) collective-permute-start(bf16[384,256]{1,0:T(8,128)(2,1)S(1)} %get-tuple-element.59), channel_id=1, source_target_pairs={{0,1},{1,0},{2,3},{3,2},{4,5},{5,4},{6,7},{7,6},{8,9},{9,8},{10,11... | collective-permute-start | bytes 589832 | tf_op jit(solution)/shard_map/ppermute | solution.py:557
  14.5 0.2 collective-permute-start.8
  14.7 0.7 %collective-permute-start.4 = (bf16[384,256]{1,0:T(8,128)(2,1)S(1)}, bf16[384,256]{1,0:T(8,128)(2,1)S(1)}, u32[]{:S(2)}, u32[]{:S(2)}) collective-permute-start(bf16[384,256]{1,0:T(8,128)(2,1)S(1)} %get-tuple-element.63), channel_id=1, source_target_pairs={{0,0},{1,2},{2,1},{3,3},{4,4},{5,6},{6,5},{7,7},{8,8},{9,10},{10,9... | collective-permute-start | bytes 589832 | tf_op jit(solution)/shard_map/ppermute | solution.py:557
  15.4 4.0 %collective-permute-done.3.refs_1_ = bf16[384,256]{1,0:T(8,128)(2,1)S(1)} collective-permute-done((bf16[384,256]{1,0:T(8,128)(2,1)S(1)}, bf16[384,256]{1,0:T(8,128)(2,1)S(1)}, u32[]{:S(2)}, u32[]{:S(2)}) %collective-permute-start.3) | collective-permute-done | bytes 196640 | tf_op jit(solution)/shard_map/ppermute | solution.py:557
  19.5 0.3 collective-permute-start.6
  20.0 1.0 %collective-permute-start.9 = (bf16[768,256]{1,0:T(8,128)(2,1)S(1)}, bf16[768,256]{1,0:T(8,128)(2,1)S(1)}, u32[]{:S(2)}, u32[]{:S(2)}) collective-permute-start(bf16[768,256]{1,0:T(8,128)(2,1)S(1)} %get-tuple-element.77), channel_id=1, source_target_pairs={{0,12},{4,20},{8,24},{12,0},{16,28},{20,4},{24,8},{28,16},{1,13},{... | collective-permute-start | bytes 1179656 | tf_op jit(solution)/shard_map/ppermute | solution.py:551
  20.9 0.6 %collective-permute-start.11 = (bf16[256,256]{1,0:T(8,128)(2,1)S(1)}, bf16[256,256]{1,0:T(8,128)(2,1)S(1)}, u32[]{:S(2)}, u32[]{:S(2)}) collective-permute-start(bf16[256,256]{1,0:T(8,128)(2,1)S(1)} %get-tuple-element.82), channel_id=1, source_target_pairs={{0,12},{4,20},{8,24},{12,0},{16,28},{20,4},{24,8},{28,16},{1,13},{... | collective-permute-start | bytes 393224 | tf_op jit(solution)/shard_map/ppermute | solution.py:551
  21.5 4.7 %collective-permute-done.6.refs_2_ = bf16[4,64,256]{2,1,0:T(8,128)(2,1)S(1)} collective-permute-done((bf16[4,64,256]{2,1,0:T(8,128)(2,1)S(1)}, bf16[4,64,256]{2,1,0:T(8,128)(2,1)S(1)}, u32[]{:S(2)}, u32[]{:S(2)}) %collective-permute-start.6) | collective-permute-done | bytes 131104 | tf_op jit(solution)/shard_map/ppermute | solution.py:551
  26.2 1.0 %collective-permute-start.10 = (bf16[4,32,256]{2,1,0:T(8,128)(2,1)S(1)}, bf16[4,32,256]{2,1,0:T(8,128)(2,1)S(1)}, u32[]{:S(2)}, u32[]{:S(2)}) collective-permute-start(bf16[4,32,256]{2,1,0:T(8,128)(2,1)S(1)} %get-tuple-element.81), channel_id=1, source_target_pairs={{0,16},{4,20},{8,24},{12,28},{16,0},{20,4},{24,8},{28,12},{1,17},{... | collective-permute-start | bytes 196616 | tf_op jit(solution)/shard_map/ppermute | solution.py:551
  27.2 1.6 %collective-permute-done.8.refs_6_.refs_4_ = bf16[1040,256]{1,0:T(8,128)(2,1)S(1)} collective-permute-done((bf16[1040,256]{1,0:T(8,128)(2,1)S(1)}, bf16[1040,256]{1,0:T(8,128)(2,1)S(1)}, u32[]{:S(2)}, u32[]{:S(2)}) %collective-permute-start.8) | collective-permute-done | bytes 532512 | tf_op jit(solution)/shard_map/ppermute | solution.py:551
  28.9 2.4 %renorm_first.1 = (f32[8,128]{1,0:T(8,128)S(1)}, bf16[8,4,256,256]{3,2,1,0:T(8,128)(2,1)}) custom-call(f32[8,128]{1,0:T(8,128)S(1)} %get-tuple-element.72.refs_0_, bf16[6,256,256]{2,1,0:T(8,128)(2,1)S(1)} %get-tuple-element.73.refs_1_, bf16[4,256,256]{2,1,0:T(8,128)(2,1)S(1)} %get-tuple-element.49.refs_6_.refs_2_, ...), custom_call_target="tpu_custom_call" | custom-call | flops 2018625024 | tf_op jit(solution)/shard_map/renorm_first/pallas_call | solution.py:35
  31.3 2.2 %collective-permute-done.9.refs_3_ = bf16[768,256]{1,0:T(8,128)(2,1)S(1)} collective-permute-done((bf16[768,256]{1,0:T(8,128)(2,1)S(1)}, bf16[768,256]{1,0:T(8,128)(2,1)S(1)}, u32[]{:S(2)}, u32[]{:S(2)}) %collective-permute-start.9) | collective-permute-done | bytes 393248 | tf_op jit(solution)/shard_map/ppermute | solution.py:551
  33.5 1.2 %renorm_last.2 = (f32[8,128]{1,0:T(8,128)S(1)}, bf16[8,4,256,256]{3,2,1,0:T(8,128)(2,1)}) custom-call(f32[8,128]{1,0:T(8,128)S(1)} %get-tuple-element.76.refs_0_, bf16[6,256,256]{2,1,0:T(8,128)(2,1)S(1)} %get-tuple-element.73.refs_1_, bf16[4,256,256]{2,1,0:T(8,128)(2,1)S(1)} %get-tuple-element.49.refs_6_.refs_2_, ...), custom_call_target="tpu_custom_call", output_to_operand_aliasing={{1}: (5, {})} | custom-call | tf_op jit(solution)/shard_map/renorm_last/pallas_call | solution.py:35
  34.9 0.7 %collective-permute-done.10.refs_4_ = bf16[4,32,256]{2,1,0:T(8,128)(2,1)S(1)} collective-permute-done((bf16[4,32,256]{2,1,0:T(8,128)(2,1)S(1)}, bf16[4,32,256]{2,1,0:T(8,128)(2,1)S(1)}, u32[]{:S(2)}, u32[]{:S(2)}) %collective-permute-start.10) | collective-permute-done | bytes 65568 | tf_op jit(solution)/shard_map/ppermute | solution.py:551
  35.6 1.1 %renorm_last.3 = (f32[8,128]{1,0:T(8,128)}, bf16[8,4,256,256]{3,2,1,0:T(8,128)(2,1)}, f32[4,32,256]{2,1,0:T(8,128)}) custom-call(f32[8,128]{1,0:T(8,128)S(1)} %get-tuple-element.79.refs_0_, bf16[6,256,256]{2,1,0:T(8,128)(2,1)S(1)} %get-tuple-element.73.refs_1_, ...), custom_call_target="tpu_custom_call", output_to_operand_aliasing={{1}: (7, {})} | custom-call | tf_op jit(solution)/shard_map/renorm_last/pallas_call | solution.py:35
  (14 shorter events, 0.5 us)
Async XLA Ops:
  1.9 9.9 %collective-permute-start = (bf16[1024,256]{1,0:T(8,128)(2,1)S(1)}, bf16[1024,256]{1,0:T(8,128)(2,1)S(1)}, u32[]{:S(2)}, u32[]{:S(2)}) collective-permute-start(bf16[1024,256]{1,0:T(8,128)(2,1)S(1)} %get-tuple-element.51), channel_id=1, source_target_pairs={{0,16},{4,8},{8,4},{12,28},{16,0},{20,24},{24,20},{28,12},{1,17},{... | collective-permute-start | bytes 1572872 | tf_op jit(solution)/shard_map/ppermute | solution.py:551
  6.1 22.8 %collective-permute-start.7 = (bf16[2064,256]{1,0:T(8,128)(2,1)S(1)}, bf16[2064,256]{1,0:T(8,128)(2,1)S(1)}, u32[]{:S(2)}, u32[]{:S(2)}) collective-permute-start(bf16[2064,256]{1,0:T(8,128)(2,1)S(1)} %get-tuple-element.74), channel_id=1, source_target_pairs={{0,4},{4,0},{8,12},{12,8},{16,20},{20,16},{24,28},{28,24},{1,5},{5... | collective-permute-start | bytes 3170312 | tf_op jit(solution)/shard_map/ppermute | solution.py:551
  6.6 13.3 %collective-permute-start.5 = (bf16[1040,256]{1,0:T(8,128)(2,1)S(1)}, bf16[1040,256]{1,0:T(8,128)(2,1)S(1)}, u32[]{:S(2)}, u32[]{:S(2)}) collective-permute-start(bf16[1040,256]{1,0:T(8,128)(2,1)S(1)} %get-tuple-element.67), channel_id=1, source_target_pairs={{0,16},{4,8},{8,4},{12,28},{16,0},{20,24},{24,20},{28,12},{1,17},{... | collective-permute-start | bytes 1597448 | tf_op jit(solution)/shard_map/ppermute | solution.py:551
  10.6 2.1 %collective-permute-start.1 = (bf16[3,128,256]{2,1,0:T(8,128)(2,1)S(1)}, bf16[3,128,256]{2,1,0:T(8,128)(2,1)S(1)}, u32[]{:S(2)}, u32[]{:S(2)}) collective-permute-start(bf16[3,128,256]{2,1,0:T(8,128)(2,1)S(1)} %get-tuple-element.53), channel_id=1, source_target_pairs={{0,4},{4,0},{8,12},{12,8},{16,20},{20,16},{24,28},{28,24},{1,5},{5... | collective-permute-start | bytes 589832 | tf_op jit(solution)/shard_map/ppermute | solution.py:551
  11.7 1.4 %collective-permute-start.2 = (bf16[3,128,256]{2,1,0:T(8,128)(2,1)S(1)}, bf16[3,128,256]{2,1,0:T(8,128)(2,1)S(1)}, u32[]{:S(2)}, u32[]{:S(2)}) collective-permute-start(bf16[3,128,256]{2,1,0:T(8,128)(2,1)S(1)} %get-tuple-element.56), channel_id=1, source_target_pairs={{0,4},{4,0},{8,12},{12,8},{16,20},{20,16},{24,28},{28,24},{1,5},{5... | collective-permute-start | bytes 589832 | tf_op jit(solution)/shard_map/ppermute | solution.py:551
  13.1 6.3 %collective-permute-start.3 = (bf16[384,256]{1,0:T(8,128)(2,1)S(1)}, bf16[384,256]{1,0:T(8,128)(2,1)S(1)}, u32[]{:S(2)}, u32[]{:S(2)}) collective-permute-start(bf16[384,256]{1,0:T(8,128)(2,1)S(1)} %get-tuple-element.59), channel_id=1, source_target_pairs={{0,1},{1,0},{2,3},{3,2},{4,5},{5,4},{6,7},{7,6},{8,9},{9,8},{10,11... | collective-permute-start | bytes 589832 | tf_op jit(solution)/shard_map/ppermute | solution.py:557
  14.5 14.3 %collective-permute-start.8 = (bf16[1040,256]{1,0:T(8,128)(2,1)S(1)}, bf16[1040,256]{1,0:T(8,128)(2,1)S(1)}, u32[]{:S(2)}, u32[]{:S(2)}) collective-permute-start(bf16[1040,256]{1,0:T(8,128)(2,1)S(1)} %get-tuple-element.75), channel_id=1, source_target_pairs={{0,28},{4,20},{8,24},{12,16},{16,12},{20,4},{24,8},{28,0},{1,29},{... | collective-permute-start | bytes 1597448 | tf_op jit(solution)/shard_map/ppermute | solution.py:551
  14.7 4.7 %collective-permute-start.4 = (bf16[384,256]{1,0:T(8,128)(2,1)S(1)}, bf16[384,256]{1,0:T(8,128)(2,1)S(1)}, u32[]{:S(2)}, u32[]{:S(2)}) collective-permute-start(bf16[384,256]{1,0:T(8,128)(2,1)S(1)} %get-tuple-element.63), channel_id=1, source_target_pairs={{0,0},{1,2},{2,1},{3,3},{4,4},{5,6},{6,5},{7,7},{8,8},{9,10},{10,9... | collective-permute-start | bytes 589832 | tf_op jit(solution)/shard_map/ppermute | solution.py:557
  19.5 6.7 %collective-permute-start.6 = (bf16[4,64,256]{2,1,0:T(8,128)(2,1)S(1)}, bf16[4,64,256]{2,1,0:T(8,128)(2,1)S(1)}, u32[]{:S(2)}, u32[]{:S(2)}) collective-permute-start(bf16[4,64,256]{2,1,0:T(8,128)(2,1)S(1)} %get-tuple-element.71), channel_id=1, source_target_pairs={{0,8},{4,12},{8,0},{12,4},{16,24},{20,28},{24,16},{28,20},{1,9},{5... | collective-permute-start | bytes 393224 | tf_op jit(solution)/shard_map/ppermute | solution.py:551
  20.0 13.5 %collective-permute-start.9 = (bf16[768,256]{1,0:T(8,128)(2,1)S(1)}, bf16[768,256]{1,0:T(8,128)(2,1)S(1)}, u32[]{:S(2)}, u32[]{:S(2)}) collective-permute-start(bf16[768,256]{1,0:T(8,128)(2,1)S(1)} %get-tuple-element.77), channel_id=1, source_target_pairs={{0,12},{4,20},{8,24},{12,0},{16,28},{20,4},{24,8},{28,16},{1,13},{... | collective-permute-start | bytes 1179656 | tf_op jit(solution)/shard_map/ppermute | solution.py:551
  20.9 13.9 %collective-permute-start.11 = (bf16[256,256]{1,0:T(8,128)(2,1)S(1)}, bf16[256,256]{1,0:T(8,128)(2,1)S(1)}, u32[]{:S(2)}, u32[]{:S(2)}) collective-permute-start(bf16[256,256]{1,0:T(8,128)(2,1)S(1)} %get-tuple-element.82), channel_id=1, source_target_pairs={{0,12},{4,20},{8,24},{12,0},{16,28},{20,4},{24,8},{28,16},{1,13},{... | collective-permute-start | bytes 393224 | tf_op jit(solution)/shard_map/ppermute | solution.py:551
  26.2 9.4 %collective-permute-start.10 = (bf16[4,32,256]{2,1,0:T(8,128)(2,1)S(1)}, bf16[4,32,256]{2,1,0:T(8,128)(2,1)S(1)}, u32[]{:S(2)}, u32[]{:S(2)}) collective-permute-start(bf16[4,32,256]{2,1,0:T(8,128)(2,1)S(1)} %get-tuple-element.81), channel_id=1, source_target_pairs={{0,16},{4,20},{8,24},{12,28},{16,0},{20,4},{24,8},{28,12},{1,17},{... | collective-permute-start | bytes 196616 | tf_op jit(solution)/shard_map/ppermute | solution.py:551
